TPU v7x, 32 devices: a whole 2x2x4 slice. The times are simulated.
32 devices in a mesh: dp: 8 (over z, x), expert: 4 (over y, core).
Axes of the slice: x: 2, y: 2, z: 4, core: 2. Of those that a mesh axis runs over, the one named last changes fastest.
Arguments:
- tokens: bfloat16 [16384, 768], P(('dp', 'expert')), may hold values from -6 to 6
- qkv_weight: bfloat16 [3, 768, 768], P(None, 'dp'), may hold values from -0.21875 to 0.21875
- out_weight: bfloat16 [768, 768], P('dp'), may hold values from -1.75 to 1.75
- position_bias_table: float32 [12, 32], replicated, may hold values from -3 to 3
- gain_attn: float32 [768], replicated, may hold values from 0.5 to 1.5
- gain_moe: float32 [768], replicated, may hold values from 0.5 to 1.5
- router: bfloat16 [768, 8], replicated, may hold values from -0.15625 to 0.15625
- w_in: bfloat16 [8, 768, 3072], P('expert'), may hold values from -0.21875 to 0.21875
- w_out: bfloat16 [8, 3072, 768], P('expert'), may hold values from -0.109375 to 0.109375
- routes: int32 [16384, 2], P(('dp', 'expert')), may hold values from 0 to 7, all different within a row; in each aligned block of 512 rows (0 to 511, 512 to 1023, ...) at most 160 rows name the same one
- prefix: int32 [32], P(('dp', 'expert')), may hold values from 51 to 256
- valid_mask: int32 [16384], P(('dp', 'expert')), may hold values from 0 to 1, as said below
- teacher: bfloat16 [16384, 768], P(('dp', 'expert')), may hold values from -6 to 6
- cotangent: bfloat16 [16384, 768], P(('dp', 'expert')), may hold values from -6 to 6
Outputs:
- output: bfloat16 [16384, 768], P(('dp', 'expert'))
- distill_loss: float32 [], replicated
- grad_input: float32 [16384, 768], P(('dp', 'expert'))
- grad_qkv: float32 [3, 768, 768], P(None, 'dp')
- grad_out_weight: float32 [768, 768], P('dp')
- grad_w_in: float32 [8, 768, 3072], P('expert', 'dp')
- grad_w_out: float32 [8, 3072, 768], P('expert', 'dp')
- grad_router: float32 [768, 8], replicated
- grad_table: float32 [12, 32], replicated
- grad_gain_attn: float32 [768], replicated
- grad_gain_moe: float32 [768], replicated
Inputs may be any that keep to these rules, and one draw needn't show every extreme that they name: `routes`: each row names 2 different experts. Among the 512 rows of one device no expert is named more than 160 times, a bound that some block reaches. `valid_mask`: the first token of every sequence is valid.
All inputs are finite; a program needn't handle non-finite values.
Results may differ from a plain program's by a relative error of at most 0.015.
Values may be sent and summed in bfloat16 or wider, within the bound.
No kernel may reach another device: no remote copies, remote signals or barrier semaphores. Data moves between devices by JAX's collectives and lax.ppermute only.
A program may use at most 192 MiB of HBM per device.

v0:
```python
import math

import jax
import jax.numpy as jnp
from jax import lax
from jax.sharding import PartitionSpec as P

HEAD_DIM = 64


EPS = 1e-06
BOUNDS = (12, 16, 23, 32, 46, 64, 91)
TOP_PRECISION = lax.Precision.HIGHEST


def bucket_index(offset):
    distance = jnp.abs(offset)
    far_bucket = 8 + sum([(distance >= cutoff_level).astype(jnp.int32) for cutoff_level in BOUNDS])
    near_bucket = jnp.where(distance < 8, distance, far_bucket)
    return jnp.where(offset > 0, 16, 0) + near_bucket


def norm_apply(inputs, gain_vec):
    return inputs * lax.rsqrt(jnp.mean(inputs * inputs, axis=-1, keepdims=True) + EPS) * gain_vec


def gate_values(logits, routes):
    soft_probs = jax.nn.softmax(logits, axis=-1)
    picked_hot = (
        routes[:, :, None] == jnp.arange(logits.shape[1], dtype=jnp.int32)[None, None, :]
    ).astype(jnp.float32)
    chosen = jnp.sum(soft_probs[:, None, :] * picked_hot, axis=-1)
    return chosen / jnp.sum(chosen, axis=1, keepdims=True)


def score_block(q_rows, key_rows, position_bias_table, row_start, prefix_len):
    block_rows = q_rows.shape[0]
    length = key_rows.shape[0]
    bucket_count = position_bias_table.shape[1]
    row_ids = row_start + lax.broadcasted_iota(jnp.int32, (block_rows, length), 0)
    col_ids = lax.broadcasted_iota(jnp.int32, (block_rows, length), 1)
    bucket_ids = bucket_index(col_ids - row_ids)
    bucket_onehot_matrix = (
        bucket_ids[None] == lax.broadcasted_iota(jnp.int32, (bucket_count, 1, 1), 0)
    ).astype(jnp.bfloat16)
    pos_bias = jnp.einsum(
        "cg,gxz->cxz",
        position_bias_table,
        bucket_onehot_matrix.astype(jnp.float32),
        precision=TOP_PRECISION,
    )
    raw_scores = (
        jnp.einsum("qhd,khd->hqk", q_rows, key_rows, preferred_element_type=jnp.float32)
        / math.sqrt(HEAD_DIM)
        + pos_bias
    )
    visible = ((col_ids <= row_ids) | (col_ids < prefix_len))[None]
    return (raw_scores, visible, bucket_onehot_matrix)


def row_stats(raw_scores, visible):
    masked = jnp.where(visible, raw_scores, -1e30)
    row_peak = jnp.max(masked, axis=-1, keepdims=True)
    row_total = jnp.sum(jnp.where(visible, jnp.exp(masked - row_peak), 0.0), axis=-1, keepdims=True)
    return (row_peak, row_total)


def soft_weights(raw_scores, visible, row_peak, row_total):
    masked = jnp.where(visible, raw_scores, -1e30)
    return jnp.where(visible, jnp.exp(masked - row_peak), 0.0) / row_total


def attend_forward(queries, key_rows, values, position_bias_table, prefix_len):
    raw_scores, visible, bucket_onehot_matrix = score_block(
        queries, key_rows, position_bias_table, 0, prefix_len
    )
    row_peak, row_total = row_stats(raw_scores, visible)
    weights = soft_weights(raw_scores, visible, row_peak, row_total).astype(jnp.bfloat16)
    outputs = jnp.einsum("hqk,khd->qhd", weights, values, preferred_element_type=jnp.float32)
    stats = [(row_peak, row_total)]
    return (outputs.astype(jnp.bfloat16), stats)


def attend_backward(
    queries, key_rows, values, position_bias_table, prefix_len, block_rows, stats, grad_attended
):
    length = queries.shape[0]
    grad_keys = jnp.zeros(key_rows.shape, jnp.float32)
    grad_values = jnp.zeros(values.shape, jnp.float32)
    grad_table = jnp.zeros(position_bias_table.shape, jnp.float32)
    grad_queries = []
    for block_id, row_start in enumerate(range(0, length, block_rows)):
        raw_scores, visible, bucket_onehot_matrix = score_block(
            queries, key_rows, position_bias_table, row_start, prefix_len
        )
        row_peak, row_total = stats[block_id]
        soft = soft_weights(raw_scores, visible, row_peak, row_total)
        grad_probs = jnp.einsum(
            "qhd,khd->hqk", grad_attended, values, preferred_element_type=jnp.float32
        )
        grad_values = jnp.einsum(
            "hqk,qhd->khd",
            soft.astype(jnp.bfloat16),
            grad_attended,
            preferred_element_type=jnp.float32,
        )
        inner_sum = jnp.sum(soft * grad_probs, axis=-1, keepdims=True)
        score_gradient = (soft * (grad_probs - inner_sum)).astype(jnp.bfloat16)
        grad_queries.append(
            jnp.einsum("hqk,khd->qhd", score_gradient, key_rows, preferred_element_type=jnp.float32)
            / math.sqrt(HEAD_DIM)
        )
        grad_keys = jnp.einsum(
            "hqk,qhd->khd", score_gradient, queries, preferred_element_type=jnp.float32
        ) / math.sqrt(HEAD_DIM)
        grad_table = jnp.einsum(
            "mti,dti->md", score_gradient, bucket_onehot_matrix, preferred_element_type=jnp.float32
        )
    return (grad_queries[0], grad_keys, grad_values, grad_table)


def expert_back(grad_rows, rows_seen, w_in, w_out):
    pre_act = jnp.einsum("secd,edf->secf", rows_seen, w_in, preferred_element_type=jnp.float32)
    hidden, gelu_derivative_back = jax.vjp(
        lambda pre_vals: jax.nn.gelu(pre_vals, approximate=True), pre_act
    )
    grad_hidden = jnp.einsum("secd,efd->secf", grad_rows, w_out, preferred_element_type=jnp.float32)
    grad_pre = gelu_derivative_back(grad_hidden)[0].astype(jnp.bfloat16)
    grad_in_rows = jnp.einsum(
        "secf,edf->secd", grad_pre, w_in, preferred_element_type=jnp.float32
    ).astype(jnp.bfloat16)
    return (grad_in_rows, hidden.astype(jnp.bfloat16), grad_pre)


def on_device(
    tokens,
    qkv_weight,
    out_weight,
    position_bias_table,
    gain_attn,
    gain_moe,
    router,
    w_in,
    w_out,
    routes,
    prefix,
    valid_mask,
    teacher,
    cotangent,
):
    length, width = tokens.shape
    head_count = position_bias_table.shape[0]
    block_rows = min(512, length)
    expert_count = router.shape[1]
    top_count = routes.shape[1]
    group_count = lax.axis_size("expert")
    local_experts = w_in.shape[0]
    capacity = 5 * length * top_count // (4 * expert_count)
    total_tokens = length * lax.axis_size("dp") * group_count
    qkv_full, out_full = (
        lax.all_gather(qkv_weight, "dp", axis=1, tiled=True),
        lax.all_gather(out_weight, "dp", axis=0, tiled=True),
    )
    valid_rows = valid_mask.astype(jnp.float32)[:, None]
    valid_count = lax.psum(jnp.sum(valid_rows), ("dp", "expert"))
    resid = tokens.astype(jnp.float32)
    normed1 = norm_apply(resid, gain_attn).astype(jnp.bfloat16)
    qkv_rows = jnp.einsum(
        "td,cde->cte", normed1, qkv_full, preferred_element_type=jnp.float32
    ).astype(jnp.bfloat16)
    queries = qkv_rows[0].reshape(length, head_count, -1)
    key_rows = qkv_rows[1].reshape(length, head_count, -1)
    values = qkv_rows[2].reshape(length, head_count, -1)
    prefix_len = prefix[0]
    attended, stats = attend_forward(queries, key_rows, values, position_bias_table, prefix_len)
    attended_flat = attended.reshape(length, width)
    middle = resid + jnp.dot(attended_flat, out_full, preferred_element_type=jnp.float32)
    normed2 = norm_apply(middle, gain_moe).astype(jnp.bfloat16)
    logits = jnp.dot(normed2, router, preferred_element_type=jnp.float32)
    gate_vals = gate_values(logits, routes)
    pair_count = length * top_count
    slot_count = expert_count * capacity
    flat_routes = routes.reshape(-1)
    route_hits = (
        flat_routes[:, None] == jnp.arange(expert_count, dtype=jnp.int32)[None, :]
    ).astype(jnp.bfloat16)
    lower_ones = (
        lax.broadcasted_iota(jnp.int32, (pair_count, pair_count), 0)
        >= lax.broadcasted_iota(jnp.int32, (pair_count, pair_count), 1)
    ).astype(jnp.bfloat16)
    running = jnp.dot(lower_ones, route_hits, preferred_element_type=jnp.float32)
    pair_rank = jnp.sum((running - 1.0) * route_hits.astype(jnp.float32), axis=1).astype(jnp.int32)
    slot_of_pair = (flat_routes * capacity + pair_rank).reshape(length, top_count)
    slot_hot = (
        slot_of_pair[:, :, None] == lax.broadcasted_iota(jnp.int32, (1, 1, slot_count), 2)
    ).astype(jnp.bfloat16)
    send_rows = jnp.einsum(
        "tks,td->sd", slot_hot, normed2, preferred_element_type=jnp.float32
    ).astype(jnp.bfloat16)
    send_rows = send_rows.reshape(group_count, local_experts, capacity, width)
    hidden = jax.nn.gelu(
        jnp.einsum(
            "secd,edf->secf",
            lax.all_to_all(send_rows, "expert", split_axis=0, concat_axis=0, tiled=True),
            w_in,
            preferred_element_type=jnp.float32,
        ),
        approximate=True,
    ).astype(jnp.bfloat16)
    produced = jnp.einsum(
        "secf,efd->secd", hidden, w_out, preferred_element_type=jnp.float32
    ).astype(jnp.bfloat16)
    returned = lax.all_to_all(produced, "expert", split_axis=0, concat_axis=0, tiled=True)
    picked = jnp.einsum(
        "tks,sd->tkd",
        slot_hot,
        returned.reshape(slot_count, width),
        preferred_element_type=jnp.float32,
    )
    output = middle + jnp.sum(gate_vals[:, :, None] * picked, axis=1)
    misfit = output - teacher.astype(jnp.float32)
    square_sum = jnp.sum(valid_rows * misfit * misfit)
    grad_y = cotangent.astype(jnp.float32) + valid_rows * misfit * (total_tokens / valid_count)
    grad_gates = jnp.sum(grad_y[:, None, :] * picked, axis=-1)
    grad_pairs = (gate_vals[:, :, None] * grad_y[:, None, :]).astype(jnp.bfloat16)
    send_grads = jnp.einsum(
        "tks,tkd->sd", slot_hot, grad_pairs, preferred_element_type=jnp.float32
    ).astype(jnp.bfloat16)
    send_grads = send_grads.reshape(group_count, local_experts, capacity, width)
    grad_rows = lax.all_to_all(send_grads, "expert", split_axis=0, concat_axis=0, tiled=True)
    rows_in = lax.all_to_all(send_rows, "expert", split_axis=0, concat_axis=0, tiled=True)
    grad_in_rows, hidden_in, grad_pre_in = expert_back(grad_rows, rows_in, w_in, w_out)
    sent_back = lax.all_to_all(grad_in_rows, "expert", split_axis=0, concat_axis=0, tiled=True)
    grad_w_out_local = jnp.einsum(
        "secf,secd->efd", hidden_in, grad_rows, preferred_element_type=jnp.float32
    )
    grad_w_in_local = jnp.einsum(
        "secd,secf->edf", rows_in, grad_pre_in, preferred_element_type=jnp.float32
    )
    grad_w_in, grad_w_out = (
        lax.psum_scatter(
            grad_w_in_local.astype(jnp.bfloat16), "dp", scatter_dimension=1, tiled=True
        ).astype(jnp.float32),
        lax.psum_scatter(
            grad_w_out_local.astype(jnp.bfloat16), "dp", scatter_dimension=1, tiled=True
        ).astype(jnp.float32),
    )
    grad_normed2 = jnp.einsum(
        "tks,sd->td",
        slot_hot,
        sent_back.reshape(slot_count, width),
        preferred_element_type=jnp.float32,
    )
    gate_out, gate_back = jax.vjp(lambda logit_vals: gate_values(logit_vals, routes), logits)
    grad_logits = gate_back(grad_gates)[0].astype(jnp.bfloat16)
    grad_router = jnp.einsum("td,te->de", normed2, grad_logits, preferred_element_type=jnp.float32)
    grad_normed2 = grad_normed2 + jnp.einsum(
        "te,de->td", grad_logits, router, preferred_element_type=jnp.float32
    )
    norm_out, norm_back = jax.vjp(norm_apply, middle, gain_moe)
    grad_mid_norm, grad_gain_moe = norm_back(grad_normed2)
    grad_middle = grad_y + grad_mid_norm
    grad_attn_proj = grad_middle.astype(jnp.bfloat16)
    grad_out_local = jnp.einsum(
        "td,te->de", attended_flat, grad_attn_proj, preferred_element_type=jnp.float32
    )
    grad_attended = jnp.einsum(
        "te,de->td", grad_attn_proj, out_full, preferred_element_type=jnp.float32
    ).astype(jnp.bfloat16)
    grad_attended = grad_attended.reshape(length, head_count, -1)
    grad_queries, grad_keys, grad_values, grad_table = attend_backward(
        queries, key_rows, values, position_bias_table, prefix_len, block_rows, stats, grad_attended
    )
    grad_qkv_rows = jnp.stack(
        [
            grad_queries.reshape(length, width),
            grad_keys.reshape(length, width),
            grad_values.reshape(length, width),
        ]
    ).astype(jnp.bfloat16)
    grad_qkv_local = jnp.einsum(
        "td,cte->cde", normed1, grad_qkv_rows, preferred_element_type=jnp.float32
    )
    grad_normed1 = jnp.einsum(
        "cte,cde->td", grad_qkv_rows, qkv_full, preferred_element_type=jnp.float32
    )
    first_out, first_back = jax.vjp(norm_apply, resid, gain_attn)
    grad_resid_norm, grad_gain_attn = first_back(grad_normed1)
    grad_input = grad_middle + grad_resid_norm
    grad_qkv_part, grad_out_part = (
        lax.psum_scatter(
            grad_qkv_local.astype(jnp.bfloat16), "dp", scatter_dimension=1, tiled=True
        ).astype(jnp.float32),
        lax.psum_scatter(
            grad_out_local.astype(jnp.bfloat16), "dp", scatter_dimension=0, tiled=True
        ).astype(jnp.float32),
    )
    grad_qkv, grad_out_weight = (
        lax.psum(grad_qkv_part.astype(jnp.bfloat16), "expert").astype(jnp.float32),
        lax.psum(grad_out_part.astype(jnp.bfloat16), "expert").astype(jnp.float32),
    )
    grad_gain_attn, grad_gain_moe, grad_table, grad_router, square_total = lax.psum(
        (grad_gain_attn, grad_gain_moe, grad_table, grad_router, square_sum), ("dp", "expert")
    )
    distill_loss = square_total / (width * valid_count)
    return (
        output.astype(jnp.bfloat16),
        distill_loss,
        grad_input,
        grad_qkv,
        grad_out_weight,
        grad_w_in,
        grad_w_out,
        grad_router,
        grad_table,
        grad_gain_attn,
        grad_gain_moe,
    )


def solution(mesh):
    return jax.shard_map(
        on_device,
        mesh=mesh,
        in_specs=(
            P(("dp", "expert"), None),
            P(None, "dp", None),
            P("dp", None),
            P(),
            P(),
            P(),
            P(),
            P("expert", None, None),
            P("expert", None, None),
            P(("dp", "expert"), None),
            P(("dp", "expert")),
            P(("dp", "expert")),
            P(("dp", "expert"), None),
            P(("dp", "expert"), None),
        ),
        out_specs=(
            P(("dp", "expert"), None),
            P(),
            P(("dp", "expert"), None),
            P(None, "dp", None),
            P("dp", None),
            P("expert", "dp", None),
            P("expert", "dp", None),
            P(),
            P(),
            P(),
            P(),
        ),
        check_vma=False,
    )
```

profile of v0, /device:TPU:0, one launch (start us, length us, event | category | flops | bytes accessed | tf_op | source)
XLA Modules:
  0.0 931.1 jit_solution(1385574733964653199)
XLA Ops:
  16.0 13.6 %fusion.2 = f32[512,512,12]{0,2,1:T(8,128)} fusion(s32[512,512]{0,1:T(8,128)S(1)} %fusion.70, f32[12,32]{1,0:T(8,128)S(1)} %copy-done.32), kind=kOutput, calls=%fused_computation.3 | convolution fusion | flops 1216348160 | bytes 13633024 | tf_op jit(solution)/shard_map/cg,gxz->cxz/dot_general | solution.py:46
  29.6 48.5 %all-gather.3.cloned.1.call-done = bf16[3,768,768]{2,1,0:T(8,128)(2,1)} async-done(((bf16[3,96,768]{2,1,0:T(8,128)(2,1)}), bf16[3,768,768]{2,1,0:T(8,128)(2,1)}) %all-gather.3.cloned.1.call-update) | async-done | bytes 3538960 | tf_op jit(solution)/shard_map/all_gather | solution.py:161
  78.2 4.1 convert_bitcast_fusion.1
  83.0 20.9 %fusion.99 = (f32[12,512]{1,0:T(8,128)S(1)}, f32[12,512,512]{1,2,0:T(8,128)}) fusion(pred[512,512]{0,1:T(8,128)(4,1)S(1)} %fusion.80, f32[512,512,12]{0,2,1:T(8,128)} %fusion.2, bf16[512,12,64]{0,2,1:T(8,128)(2,1)S(1)} %bitcast.150, bf16[512,12,64]{0,2,1:T(8,128)(2,1)S(1)} %bitcast.147), kind=kOutput, calls=%fused_computation.153 | convolution fusion | flops 421528064 | bytes 27025408 | tf_op jit(solution)/shard_map/sub | solution.py:70
  104.2 6.2 fusion.58
  110.4 9.5 %all-gather.5.cloned.1.call-done = bf16[768,768]{1,0:T(8,128)(2,1)} async-done(((bf16[96,768]{1,0:T(8,128)(2,1)}), bf16[768,768]{1,0:T(8,128)(2,1)}) %all-gather.5.cloned.1.call-update) | async-done | bytes 1179664 | tf_op jit(solution)/shard_map/all_gather | solution.py:162
  123.7 27.6 %all_to_all.21 = bf16[4,2,160,768]{3,2,1,0:T(8,128)(2,1)S(1)} all-to-all(bf16[4,2,160,768]{3,2,1,0:T(8,128)(2,1)S(1)} %bitcast.155), channel_id=1, replica_groups=mesh['dp'=8,'expert'=4] {'expert'}, dimensions={0} | all-to-all | bytes 3932160 | tf_op jit(solution)/shard_map/all_to_all | solution.py:204
  152.5 13.5 %fusion.19 = f32[2,4,160,3072]{3,2,1,0:T(8,128)} fusion(bf16[2,768,3072]{2,1,0:T(8,128)(2,1)} %param.21, bf16[4,2,160,768]{3,2,1,0:T(8,128)(2,1)S(1)} %all_to_all.21), kind=kOutput, calls=%fused_computation.31 | convolution fusion | flops 6039797760 | bytes 27131904 | tf_op jit(solution)/shard_map/secd,edf->secf/dot_general | solution.py:202
  166.0 12.6 %convert_bitcast_fusion.3 = bf16[4,2,160,768]{3,2,0,1:T(8,128)(2,1)S(1)} fusion(bf16[2,3072,768]{2,1,0:T(8,128)(2,1)S(1)} %bitcast.164, f32[2,4,160,3072]{3,2,1,0:T(8,128)} %fusion.19), kind=kOutput, calls=%fused_computation.73 | convolution fusion | flops 6076170240 | bytes 27131904 | tf_op jit(solution)/shard_map/secf,efd->secd/dot_general | solution.py:210
  180.0 4.4 all-to-all-start.1
  185.0 55.7 %psum.57 = f32[]{:T(128)} all-reduce(f32[]{:T(128)} %convert_reduce_fusion.1), channel_id=1, replica_groups=mesh['dp'=8,'expert'=4] {'dp','expert'}, use_global_device_ids=true, to_apply=%region_14.15 | all-reduce | flops 1 | bytes 8 | tf_op jit(solution)/shard_map/psum | solution.py:165
  241.9 5.9 multiply_reduce_fusion.2
  252.0 28.1 %all_to_all.22 = bf16[4,2,160,768]{3,2,1,0:T(8,128)(2,1)} all-to-all(bf16[4,2,160,768]{3,2,1,0:T(8,128)(2,1)S(1)} %bitcast.154), channel_id=1, replica_groups=mesh['dp'=8,'expert'=4] {'expert'}, dimensions={0} | all-to-all | bytes 3932160 | tf_op jit(solution)/shard_map/all_to_all | solution.py:230
  280.1 21.2 %fusion.11 = bf16[4,2,160,3072]{3,2,0,1:T(8,128)(2,1)} fusion(f32[2,4,160,3072]{3,2,1,0:T(8,128)} %fusion.19, bf16[2,3072,768]{2,1,0:T(8,128)(2,1)} %param.22, bf16[4,2,160,768]{3,2,1,0:T(8,128)(2,1)} %all_to_all.22), kind=kOutput, calls=%fused_computation.16 | convolution fusion | flops 6118440960 | bytes 34996224 | tf_op jit(solution)/shard_map/secd,efd->secf/dot_general | solution.py:127
  301.3 11.4 %convert_bitcast_fusion.2 = bf16[4,2,160,768]{3,2,0,1:T(8,128)(2,1)S(1)} fusion(bf16[4,2,160,3072]{3,2,0,1:T(8,128)(2,1)} %fusion.11, bf16[2,768,3072]{2,1,0:T(8,128)(2,1)} %param.21), kind=kOutput, calls=%fused_computation.72 | convolution fusion | flops 6040780800 | bytes 19267584 | tf_op jit(solution)/shard_map/secf,edf->secd/dot_general | solution.py:129
  314.1 4.4 all-to-all-start.3
  321.2 21.7 %all-to-all-done.3 = bf16[4,2,160,768]{3,2,1,0:T(8,128)(2,1)} async-done(((bf16[4,2,160,768]{3,2,1,0:T(8,128)(2,1)}), bf16[4,2,160,768]{3,2,1,0:T(8,128)(2,1)}, u32[]{:S(2)}, u32[]{:S(2)}) %all-to-all-start.3) | async-done | bytes 1966112 | tf_op jit(solution)/shard_map/all_to_all | solution.py:233
  342.9 3.2 fusion.101
  353.1 10.5 %multiply_reduce_fusion = (f32[12,512]{1,0:T(8,128)S(1)}, f32[12,512,512]{1,2,0:T(8,128)}) fusion(f32[12,512,512]{1,2,0:T(8,128)} %get-tuple-element.85, f32[12,512]{1,0:T(8,128)S(1)} %get-tuple-element.84, bf16[512,12,64]{0,2,1:T(8,128)(2,1)S(1)} %bitcast.160, bf16[512,12,64]{0,2,1:T(8,128)(2,1)S(1)} %bitcast.159), kind=kOutput, calls=%fused_computation.27 | convolution fusion | flops 412084224 | bytes 26787840 | tf_op jit(solution)/shard_map/qhd,khd->hqk/dot_general | solution.py:98
  365.7 6.0 multiply_convert_fusion
  386.1 5.3 convert_bitcast_fusion
  391.5 8.2 copy.167
  399.7 4.9 copy.169
  407.5 75.2 %reduce-scatter.13.cloned.1.call-done = bf16[96,2304]{1,0:T(8,128)(2,1)} async-done(((bf16[768,2304]{1,0:T(8,128)(2,1)}), bf16[96,2304]{1,0:T(8,128)(2,1)}) %reduce-scatter.13.cloned.1.call-update) | async-done | bytes 442384
  485.6 64.6 %reduce-scatter.7.cloned.1.call-done = bf16[96,768]{1,0:T(8,128)(2,1)} async-done(((bf16[768,768]{1,0:T(8,128)(2,1)}), bf16[96,768]{1,0:T(8,128)(2,1)}) %reduce-scatter.7.cloned.1.call-update) | async-done | bytes 147472 | tf_op jit(solution)/shard_map/reduce_scatter | solution.py:294
  550.3 16.1 %bitcast_convert_fusion = bf16[2,3072,768]{2,1,0:T(8,128)(2,1)} fusion(bf16[4,2,160,768]{3,2,1,0:T(8,128)(2,1)} %all_to_all.22, f32[2,4,160,3072]{3,2,1,0:T(8,128)} %fusion.19), kind=kOutput, calls=%fused_computation.6 | convolution fusion | flops 6079905792 | bytes 27131904 | tf_op jit(solution)/shard_map/secf,secd->efd/dot_general | solution.py:234
  566.4 13.1 %bitcast_convert_fusion.1 = bf16[2,768,3072]{2,1,0:T(8,128)(2,1)} fusion(bf16[4,2,160,768]{3,2,1,0:T(8,128)(2,1)} %copy-done.21, bf16[4,2,160,3072]{3,2,0,1:T(8,128)(2,1)} %fusion.11), kind=kOutput, calls=%fused_computation.7 | convolution fusion | flops 6044516352 | bytes 19267584 | tf_op jit(solution)/shard_map/secd,secf->edf/dot_general | solution.py:237
  580.9 6.2 fusion.49
  587.1 10.1 %fusion.67 = f32[12,32]{1,0:T(8,128)S(1)} fusion(s32[512,512]{0,1:T(8,128)S(1)} %copy-done.13, bf16[12,512,512]{1,2,0:T(8,128)(2,1)} %copy-done.2), kind=kOutput, calls=%fused_computation.104 | convolution fusion | flops 209715200 | bytes 7341568 | tf_op jit(solution)/shard_map/mti,dti->md/dot_general | solution.py:116
  597.2 44.5 %all-reduce = (f32[]{:T(128)}, f32[768,8]{0,1:T(8,128)}, f32[12,32]{1,0:T(8,128)}, f32[768]{0:T(1024)}, f32[768]{0:T(1024)}) all-reduce(f32[]{:T(128)} %get-tuple-element.70, f32[768,8]{0,1:T(8,128)S(1)} %fusion.102, f32[12,32]{1,0:T(8,128)S(1)} %fusion.67, ...), channel_id=1, replica_groups=mesh['dp'=8,'expert'=4] {'dp','expert'}, use_global_device_ids=true, to_apply=%region_12.13 | all-reduce | flops 8065 | bytes 64520 | tf_op jit(solution)/shard_map/psum | solution.py:302
  649.2 104.6 %reduce-scatter.11.cloned.1.call-done = bf16[2,384,768]{2,1,0:T(8,128)(2,1)} async-done(((bf16[2,3072,768]{2,1,0:T(8,128)(2,1)}), bf16[2,384,768]{2,1,0:T(8,128)(2,1)}) %reduce-scatter.11.cloned.1.call-update) | async-done | bytes 1179664 | tf_op jit(solution)/shard_map/reduce_scatter | solution.py:244
  756.7 163.3 %reduce-scatter.9.cloned.1.call-done = bf16[2,96,3072]{2,1,0:T(8,128)(2,1)} async-done(((bf16[2,768,3072]{2,1,0:T(8,128)(2,1)}), bf16[2,96,3072]{2,1,0:T(8,128)(2,1)}) %reduce-scatter.9.cloned.1.call-update) | async-done | bytes 1179664 | tf_op jit(solution)/shard_map/reduce_scatter | solution.py:241
  (171 shorter events, 67.1 us)
Async XLA Ops:
  7.2 234.3 %copy-start = (bf16[768,8]{0,1:T(8,128)(2,1)S(1)}, bf16[768,8]{0,1:T(8,128)(2,1)}, u32[]{:S(2)}) copy-start(bf16[768,8]{0,1:T(8,128)(2,1)} %param.20) | copy-start | bytes 36868
  7.2 8.8 copy-start.32
  7.2 70.9 %all-gather.3.cloned.1.call-start = ((), (), s32[]{:S(2)}) async-start(), calls=%async_computation.8 | async-start | bytes 3981312 | tf_op jit(solution)/shard_map/all_gather | solution.py:161
  8.0 112.0 %all-gather.5.cloned.1.call-start = ((), (), s32[]{:S(2)}) async-start(), calls=%async_computation.9 | async-start | bytes 1327104 | tf_op jit(solution)/shard_map/all_gather | solution.py:162
  9.1 20.5 %copy-start.12 = (s32[512,512]{0,1:T(8,128)}, s32[512,512]{0,1:T(8,128)S(1)}, u32[]{:S(2)}) copy-start(s32[512,512]{0,1:T(8,128)S(1)} %fusion.70) | copy-start | bytes 3145732
  10.9 67.3 %copy-start.33 = (f32[512]{0:T(512)}, f32[512]{0:T(512)S(1)}, u32[]{:S(2)}) copy-start(f32[512]{0:T(512)S(1)} %fusion.92) | copy-start | bytes 6148
  16.0 62.2 %copy-start.16 = (bf16[512,768]{1,0:T(8,128)(2,1)S(1)}, bf16[512,768]{1,0:T(8,128)(2,1)}, u32[]{:S(2)}) copy-start(bf16[512,768]{1,0:T(8,128)(2,1)} %param.14) | copy-start | bytes 2359300
  16.0 62.2 %copy-start.36 = (f32[768]{0:T(1024)S(1)}, f32[768]{0:T(1024)}, u32[]{:S(2)}) copy-start(f32[768]{0:T(1024)} %param.18) | copy-start | bytes 9220
  82.7 21.2 %copy-start.19 = (bf16[1,512,768]{1,2,0:T(8,128)(2,1)}, bf16[1,512,768]{1,2,0:T(8,128)(2,1)S(1)}, u32[]{:S(2)}) copy-start(bf16[1,512,768]{1,2,0:T(8,128)(2,1)S(1)} %copy.135) | copy-start | bytes 2359300
  83.0 20.9 %copy-start.7 = (bf16[1,512,768]{1,2,0:T(8,128)(2,1)}, bf16[1,512,768]{1,2,0:T(8,128)(2,1)S(1)}, u32[]{:S(2)}) copy-start(bf16[1,512,768]{1,2,0:T(8,128)(2,1)S(1)} %copy.136) | copy-start | bytes 2359300
  104.2 15.8 %copy-start.17 = (bf16[512,768]{1,0:T(8,128)(2,1)S(1)}, bf16[512,768]{1,0:T(8,128)(2,1)}, u32[]{:S(2)}) copy-start(bf16[512,768]{1,0:T(8,128)(2,1)} %param.14) | copy-start | bytes 2359300
  110.4 12.1 %copy-start.23 = (bf16[12,64,512]{2,1,0:T(8,128)(2,1)}, bf16[12,64,512]{2,1,0:T(8,128)(2,1)S(1)}, u32[]{:S(2)}) copy-start(bf16[12,64,512]{2,1,0:T(8,128)(2,1)S(1)} %fusion.58) | copy-start | bytes 2359300
  110.4 11.9 %copy-start.29 = (f32[768]{0:T(1024)S(1)}, f32[768]{0:T(1024)}, u32[]{:S(2)}) copy-start(f32[768]{0:T(1024)} %param.19) | copy-start | bytes 9220
  122.5 119.0 %copy-start.5 = (bf16[512,768]{1,0:T(8,128)(2,1)}, bf16[512,768]{1,0:T(8,128)(2,1)S(1)}, u32[]{:S(2)}) copy-start(bf16[512,768]{1,0:T(8,128)(2,1)S(1)} %multiply_convert_fusion.5) | copy-start | bytes 2359300
  123.7 42.3 %slice-start.3 = ((s8[9437184]{0:T(1024)(128)(4,1)}), s8[4194304]{0:T(1024)(128)(4,1)S(1)}, s32[]{:S(2)}) async-start(s8[9437184]{0:T(1024)(128)(4,1)} %bitcast.163), calls=%async_computation.18 | async-start | bytes 8388608
  152.5 13.5 %slice-start.4 = ((s8[9437184]{0:T(1024)(128)(4,1)}), s8[4194304]{0:T(1024)(128)(4,1)S(1)}, s32[]{:S(2)}) async-start(s8[9437184]{0:T(1024)(128)(4,1)} %bitcast.163), calls=%async_computation.19 | async-start | bytes 8388608
  152.5 13.5 %slice-start.5 = ((s8[9437184]{0:T(1024)(128)(4,1)}), s8[1048576]{0:T(1024)(128)(4,1)S(1)}, s32[]{:S(2)}) async-start(s8[9437184]{0:T(1024)(128)(4,1)} %bitcast.163), calls=%async_computation.20 | async-start | bytes 2097152
  180.0 61.9 %all-to-all-start.1 = ((bf16[4,2,160,768]{3,2,1,0:T(8,128)(2,1)}), bf16[4,2,160,768]{3,2,1,0:T(8,128)(2,1)}, u32[]{:S(2)}, u32[]{:S(2)}) async-start(bf16[4,2,160,768]{3,2,1,0:T(8,128)(2,1)} %copy.142), calls=%async_computation.1 | async-start | bytes 3932160 | tf_op jit(solution)/shard_map/all_to_all | solution.py:213
  241.9 7.1 copy-start.14
  249.4 69.2 %copy-start.3 = (f32[512,768]{1,0:T(8,128)}, f32[512,768]{1,0:T(8,128)S(1)}, u32[]{:S(2)}) copy-start(f32[512,768]{1,0:T(8,128)S(1)} %fusion.51) | copy-start | bytes 4718596
  314.1 28.8 %all-to-all-start.3 = ((bf16[4,2,160,768]{3,2,1,0:T(8,128)(2,1)}), bf16[4,2,160,768]{3,2,1,0:T(8,128)(2,1)}, u32[]{:S(2)}, u32[]{:S(2)}) async-start(bf16[4,2,160,768]{3,2,1,0:T(8,128)(2,1)} %copy.145), calls=%async_computation.3 | async-start | bytes 3932160 | tf_op jit(solution)/shard_map/all_to_all | solution.py:233
  318.5 164.2 %reduce-scatter.13.cloned.1.call-start = ((), (), s32[]{:S(2)}) async-start(), calls=%async_computation.13 | async-start | bytes 3981312
  321.0 25.1 %copy-start.10 = (f32[512,768]{1,0:T(8,128)S(1)}, f32[512,768]{1,0:T(8,128)}, u32[]{:S(2)}) copy-start(f32[512,768]{1,0:T(8,128)} %copy-done.9) | copy-start | bytes 4718596
  353.1 10.5 %slice-start = ((s8[12582912]{0:T(1024)(128)(4,1)}), s8[4194304]{0:T(1024)(128)(4,1)S(1)}, s32[]{:S(2)}) async-start(s8[12582912]{0:T(1024)(128)(4,1)} %bitcast.145), calls=%async_computation.15 | async-start | bytes 8388608
  353.1 11.2 %slice-start.1 = ((s8[12582912]{0:T(1024)(128)(4,1)}), s8[4194304]{0:T(1024)(128)(4,1)S(1)}, s32[]{:S(2)}) async-start(s8[12582912]{0:T(1024)(128)(4,1)} %bitcast.145), calls=%async_computation.16 | async-start | bytes 8388608
  353.1 12.6 %slice-start.2 = ((s8[12582912]{0:T(1024)(128)(4,1)}), s8[4194304]{0:T(1024)(128)(4,1)S(1)}, s32[]{:S(2)}) async-start(s8[12582912]{0:T(1024)(128)(4,1)} %bitcast.145), calls=%async_computation.17 | async-start | bytes 8388608
  404.6 145.6 %reduce-scatter.7.cloned.1.call-start = ((), (), s32[]{:S(2)}) async-start(), calls=%async_computation.10 | async-start | bytes 1327104 | tf_op jit(solution)/shard_map/reduce_scatter | solution.py:294
  407.5 237.9 %all-reduce.4.cloned.1.call-start = ((), (), s32[]{:S(2)}) async-start(), calls=%async_computation.14 | async-start | bytes 1474560 | tf_op jit(solution)/shard_map/psum | solution.py:299
  550.2 203.6 %reduce-scatter.11.cloned.1.call-start = ((), (), s32[]{:S(2)}) async-start(), calls=%async_computation.12 | async-start | bytes 10616832 | tf_op jit(solution)/shard_map/reduce_scatter | solution.py:244
  566.4 353.6 %reduce-scatter.9.cloned.1.call-start = ((), (), s32[]{:S(2)}) async-start(), calls=%async_computation.11 | async-start | bytes 10616832 | tf_op jit(solution)/shard_map/reduce_scatter | solution.py:241
  587.1 55.3 %copy-start.31 = (f32[512]{0:T(512)S(1)}, f32[512]{0:T(512)}, u32[]{:S(2)}) copy-start(f32[512]{0:T(512)} %copy-done.30) | copy-start | bytes 6148
  647.6 275.4 %copy-start.1 = (bf16[768,8]{0,1:T(8,128)(2,1)S(1)}, bf16[768,8]{0,1:T(8,128)(2,1)}, u32[]{:S(2)}) copy-start(bf16[768,8]{0,1:T(8,128)(2,1)} %param.20) | copy-start | bytes 36868
  (22 other events, 83.4 us)
Sparse Core Ops, SparseCore 0:
  10.2 67.8 all-gather.2
  80.3 39.5 all-gather.4
  404.7 77.9 reduce-scatter.12
  486.6 63.5 reduce-scatter.6
  552.5 33.3 all-reduce.3
  589.3 164.5 reduce-scatter.10
  757.4 162.5 reduce-scatter.8
where the time goes:
time: 939 us; the launch traced here: 931 us
  waiting for transfers between devices  489 us (52%)
  matrix products  194 us (21%)
  blocking collectives  156 us (17%)
  local copies, waits for them, and re-layouts  39 us (4%)
  other arithmetic  25.5 us (3%)
  between operations  18.9 us (2%)
    reduce_scatter x1, waiting for transfers between devices, on_device(): lax.psum_scatter(grad_w_in_local.astype(jnp.bfloat16), 'dp', scatter_dime...  163 us
    reduce_scatter x1, waiting for transfers between devices, on_device(): lax.psum_scatter(grad_w_out_local.astype(jnp.bfloat16), 'dp', scatter_dim...  105 us
    unnamed x8, waiting for transfers between devices  76.6 us
    reduce_scatter x1, waiting for transfers between devices, on_device(): lax.psum_scatter(grad_out_local.astype(jnp.bfloat16), 'dp', scatter_dimen...  64.6 us
    psum x1, blocking collectives, on_device(): valid_count = lax.psum(jnp.sum(valid_rows), ('dp', 'expert'))  55.7 us
    all_gather x1, waiting for transfers between devices, on_device(): lax.all_gather(qkv_weight, 'dp', axis=1, tiled=True)  48.5 us
    psum x1, blocking collectives, on_device(): lax.psum((grad_gain_attn, grad_gain_moe, grad_table, grad_router, square_...  44.5 us
    all_to_all x1, blocking collectives, on_device(): lax.all_to_all(send_grads, 'expert', split_axis=0, concat_axis=0, tiled=T...  28.1 us
  transfers between devices with their start and end apart: 9, of which 7 were waited for; matrix products, arithmetic and copies ran while one was open for 12% of the time, Pallas kernels for 0%

commit v1 on v0

v1 whole, which is shorter than its diff:
```python
import math
import jax
import jax.numpy as jnp
from jax import lax
from jax.experimental import pallas as pl
from jax.experimental.pallas import tpu as pltpu
from jax.sharding import PartitionSpec as P

BLOCK = 128
GELU_A = math.sqrt(2.0 / math.pi)
GELU_B = 0.044715
NT = (((1,), (1,)), ((), ()))
TN = (((0,), (0,)), ((), ()))
VMEM_BYTES = 56 * 1024 * 1024


def dot_f32(left, right, dims=(((1,), (0,)), ((), ()))):
    return lax.dot_general(left, right, dims, preferred_element_type=jnp.float32)


def expert_forward_kernel(pick, rows, w_in, w_out, hidden, slope, produced, total, *, chunk):
    step = pl.program_id(0)

    @pl.when(step == 0)
    def _():
        total[...] = jnp.zeros_like(total)

    for start in range(0, rows.shape[0], chunk):
        part = pl.ds(start, chunk)
        pre = dot_f32(rows[part, :], w_in[0])
        square = pre * pre
        bend = jnp.tanh(pre * (GELU_A + (GELU_A * GELU_B) * square))
        half = 0.5 + 0.5 * bend
        act = (pre * half).astype(jnp.bfloat16)
        lift = pre * (0.5 * GELU_A + (1.5 * GELU_A * GELU_B) * square)
        slope[part, :] = (half + lift * (1.0 - bend * bend)).astype(jnp.bfloat16)
        hidden[part, :] = act
        total[part, :] += dot_f32(act, w_out[0])

    @pl.when(step == pl.num_programs(0) - 1)
    def _():
        produced[...] = total[...].astype(jnp.bfloat16)


def expert_forward(pick, rows, w_in, w_out, tile=512, chunk=256):
    count, width = rows.shape
    inner = w_in.shape[2]
    if count % chunk: chunk = count
    return pl.pallas_call(
        lambda *refs: expert_forward_kernel(*refs, chunk=chunk),
        grid_spec=pltpu.PrefetchScalarGridSpec(
            num_scalar_prefetch=1,
            grid=(inner // tile,),
            in_specs=[
                pl.BlockSpec((count, width), lambda f, pick: (0, 0)),
                pl.BlockSpec((1, width, tile), lambda f, pick: (pick[0], 0, f)),
                pl.BlockSpec((1, tile, width), lambda f, pick: (pick[0], f, 0)),
            ],
            out_specs=[
                pl.BlockSpec((count, tile), lambda f, pick: (0, f)),
                pl.BlockSpec((count, tile), lambda f, pick: (0, f)),
                pl.BlockSpec((count, width), lambda f, pick: (0, 0)),
            ],
            scratch_shapes=[pltpu.VMEM((count, width), jnp.float32)],
        ),
        out_shape=[
            jax.ShapeDtypeStruct((count, inner), jnp.bfloat16),
            jax.ShapeDtypeStruct((count, inner), jnp.bfloat16),
            jax.ShapeDtypeStruct((count, width), jnp.bfloat16),
        ],
        compiler_params=pltpu.CompilerParams(vmem_limit_bytes=VMEM_BYTES),
        cost_estimate=pl.CostEstimate(flops=4 * count * width * inner, bytes_accessed=4 * (width + count) * inner + 4 * count * width, transcendentals=count * inner),
        name="expert_forward",
    )(pick, rows, w_in, w_out)


def expert_backward_kernel(pick, grads, w_in, w_out, slope, grad_pre, grad_rows, total, *, chunk):
    step = pl.program_id(0)

    @pl.when(step == 0)
    def _():
        total[...] = jnp.zeros_like(total)

    for start in range(0, grads.shape[0], chunk):
        part = pl.ds(start, chunk)
        back = dot_f32(grads[part, :], w_out[0], NT) * slope[part, :].astype(jnp.float32)
        back = back.astype(jnp.bfloat16)
        grad_pre[part, :] = back
        total[part, :] += dot_f32(back, w_in[0], NT)

    @pl.when(step == pl.num_programs(0) - 1)
    def _():
        grad_rows[...] = total[...].astype(jnp.bfloat16)


def expert_backward(pick, grads, w_in, w_out, slope, tile=512, chunk=256):
    count, width = grads.shape
    inner = w_in.shape[2]
    if count % chunk: chunk = count
    return pl.pallas_call(
        lambda *refs: expert_backward_kernel(*refs, chunk=chunk),
        grid_spec=pltpu.PrefetchScalarGridSpec(
            num_scalar_prefetch=1,
            grid=(inner // tile,),
            in_specs=[
                pl.BlockSpec((count, width), lambda f, pick: (0, 0)),
                pl.BlockSpec((1, width, tile), lambda f, pick: (pick[0], 0, f)),
                pl.BlockSpec((1, tile, width), lambda f, pick: (pick[0], f, 0)),
                pl.BlockSpec((count, tile), lambda f, pick: (0, f)),
            ],
            out_specs=[
                pl.BlockSpec((count, tile), lambda f, pick: (0, f)),
                pl.BlockSpec((count, width), lambda f, pick: (0, 0)),
            ],
            scratch_shapes=[pltpu.VMEM((count, width), jnp.float32)],
        ),
        out_shape=[
            jax.ShapeDtypeStruct((count, inner), jnp.bfloat16),
            jax.ShapeDtypeStruct((count, width), jnp.bfloat16),
        ],
        compiler_params=pltpu.CompilerParams(vmem_limit_bytes=VMEM_BYTES),
        cost_estimate=pl.CostEstimate(flops=4 * count * width * inner, bytes_accessed=4 * (width + count) * inner + 4 * count * width, transcendentals=0),
        name="expert_backward",
    )(pick, grads, w_in, w_out, slope)


def seen_blocks(row_block, blocks):
    return max(row_block + 1, blocks // 2)


def attention_forward_kernel(far, queries, keys, values, near, attended, probs, *, heads, blocks):
    pair = pl.program_id(0)
    lane = lax.broadcasted_iota(jnp.int32, (BLOCK, 2 * heads), 1)
    for row_block in range(blocks):
        rows = pl.ds(row_block * BLOCK, BLOCK)
        span = seen_blocks(row_block, blocks)
        seen = pl.ds(0, span * BLOCK)
        outs = []
        for head in range(2):
            mine = (lane < heads) if head == 0 else (lane >= heads)
            query = jnp.where(mine, queries[rows, :] * 0.125, 0.0).astype(jnp.bfloat16)
            score = dot_f32(query, keys[seen, :], NT)
            far_bias = far[pair * 2 + head]
            pieces = []
            for key_block in range(span):
                piece = score[:, key_block * BLOCK : (key_block + 1) * BLOCK]
                slot = near_slot(row_block, key_block, blocks)
                pieces.append(piece + (far_bias if slot is None else near[head, slot]))
            peak = pieces[0]
            for piece in pieces[1:]:
                peak = jnp.maximum(peak, piece)
            peak = jnp.max(peak, axis=1, keepdims=True)
            pieces = [jnp.exp(piece - peak) for piece in pieces]
            mass = pieces[0]
            for piece in pieces[1:]:
                mass = mass + piece
            scale = 1.0 / jnp.sum(mass, axis=1, keepdims=True)
            weights = jnp.concatenate([(piece * scale).astype(jnp.bfloat16) for piece in pieces], axis=1)
            probs[head, rows, seen] = weights
            outs.append(dot_f32(weights, values[seen, :]))
        attended[rows, :] = jnp.where(lane < heads, outs[0], outs[1]).astype(jnp.bfloat16)


def near_slot(row_block, key_block, blocks):
    half = blocks // 2
    if key_block < row_block - 1:
        return None
    if key_block == row_block - 1:
        return 0
    if key_block == row_block:
        return 1 + min(row_block, half)
    count = 2 + half
    for row in range(half):
        for key in range(row + 1, half):
            if (row, key) == (row_block, key_block):
                return count
            count += 1
    raise ValueError


def near_pairs(blocks):
    half = blocks // 2
    pairs = [(1, 0)] + [(row, row) for row in range(half + 1)]
    return pairs + [(row, key) for row in range(half) for key in range(row + 1, half)]


def attention_forward(far, qkv_rows, near):
    length, width = qkv_rows.shape[1:]
    pairs = width // 128
    blocks = length // BLOCK
    slots = near.shape[1]
    return pl.pallas_call(
        lambda *refs: attention_forward_kernel(*refs, heads=64, blocks=blocks),
        grid_spec=pltpu.PrefetchScalarGridSpec(
            num_scalar_prefetch=1,
            grid=(pairs,),
            in_specs=[
                pl.BlockSpec((None, length, 128), lambda h, far: (0, 0, h)),
                pl.BlockSpec((None, length, 128), lambda h, far: (1, 0, h)),
                pl.BlockSpec((None, length, 128), lambda h, far: (2, 0, h)),
                pl.BlockSpec((2, slots, BLOCK, BLOCK), lambda h, far: (h, 0, 0, 0)),
            ],
            out_specs=[
                pl.BlockSpec((length, 128), lambda h, far: (0, h)),
                pl.BlockSpec((2, length, length), lambda h, far: (h, 0, 0)),
            ],
        ),
        out_shape=[
            jax.ShapeDtypeStruct((length, width), jnp.bfloat16),
            jax.ShapeDtypeStruct((2 * pairs, length, length), jnp.bfloat16),
        ],
        compiler_params=pltpu.CompilerParams(vmem_limit_bytes=VMEM_BYTES),
        cost_estimate=pl.CostEstimate(flops=8 * pairs * 128 * length * length, bytes_accessed=4 * pairs * length * length, transcendentals=2 * pairs * length * length),
        name="attention_forward",
    )(far, qkv_rows, qkv_rows, qkv_rows, near)


def attention_backward_kernel(queries, keys, values, grads, probs, grad_q, grad_k, grad_v, bands, flow, *, heads, blocks):
    lane = lax.broadcasted_iota(jnp.int32, (BLOCK, 2 * heads), 1)
    query_t = (queries[...] * 0.125).astype(jnp.bfloat16).T
    grad_t = grads[...].T
    half = blocks // 2
    dk, dv = [], []
    dq = [[], []]
    for head in range(2):
        mine = (lane < heads) if head == 0 else (lane >= heads)
        sums = [None] * 4
        for row_block in range(blocks):
            rows = pl.ds(row_block * BLOCK, BLOCK)
            span = seen_blocks(row_block, blocks)
            seen = pl.ds(0, span * BLOCK)
            grad = jnp.where(mine, grads[rows, :], 0.0).astype(jnp.bfloat16)
            soft = probs[head, rows, seen].astype(jnp.float32)
            back = dot_f32(grad, values[seen, :], NT)
            inner = jnp.sum(soft * back, axis=1, keepdims=True)
            score_grad = (soft * (back - inner)).astype(jnp.bfloat16)
            flow[rows, seen] = score_grad
            dq[head].append(dot_f32(score_grad, keys[seen, :]) * 0.125)
            for key_block in range(span):
                band = max(key_block - row_block, -2)
                if band > 1:
                    continue
                tile = score_grad[:, key_block * BLOCK : (key_block + 1) * BLOCK].astype(jnp.float32)
                sums[band + 2] = tile if sums[band + 2] is None else sums[band + 2] + tile
        for band in range(4):
            bands[head, band] = sums[band]
        part = slice(head * heads, (head + 1) * heads)
        key_pieces, value_pieces = [], []
        for key_block in range(blocks):
            first = 0 if key_block < half else key_block
            rows = pl.ds(first * BLOCK, (blocks - first) * BLOCK)
            cols = pl.ds(key_block * BLOCK, BLOCK)
            key_pieces.append(dot_f32(query_t[part, first * BLOCK :], flow[rows, cols]))
            value_pieces.append(dot_f32(grad_t[part, first * BLOCK :], probs[head, rows, cols]))
        dk.append(jnp.concatenate(key_pieces, axis=1))
        dv.append(jnp.concatenate(value_pieces, axis=1))
    for row_block in range(blocks):
        rows = pl.ds(row_block * BLOCK, BLOCK)
        grad_q[rows, :] = jnp.where(lane < heads, dq[0][row_block], dq[1][row_block]).astype(jnp.bfloat16)
    grad_k[...] = jnp.concatenate(dk, axis=0).T.astype(jnp.bfloat16)
    grad_v[...] = jnp.concatenate(dv, axis=0).T.astype(jnp.bfloat16)


def attention_backward(qkv_rows, grads, probs):
    length, width = grads.shape
    pairs = width // 128
    blocks = length // BLOCK
    block = pl.BlockSpec((length, 128), lambda h: (0, h))
    of_three = [pl.BlockSpec((None, length, 128), lambda h, c=c: (c, 0, h)) for c in range(3)]
    return pl.pallas_call(
        lambda *refs: attention_backward_kernel(*refs, heads=64, blocks=blocks),
        grid=(pairs,),
        in_specs=[*of_three, block, pl.BlockSpec((2, length, length), lambda h: (h, 0, 0))],
        out_specs=[block, block, block, pl.BlockSpec((2, 4, BLOCK, BLOCK), lambda h: (h, 0, 0, 0))],
        out_shape=[jax.ShapeDtypeStruct((length, width), jnp.bfloat16)] * 3
        + [jax.ShapeDtypeStruct((2 * pairs, 4, BLOCK, BLOCK), jnp.float32)],
        scratch_shapes=[pltpu.VMEM((length, length), jnp.bfloat16)],
        compiler_params=pltpu.CompilerParams(vmem_limit_bytes=VMEM_BYTES),
        cost_estimate=pl.CostEstimate(flops=20 * pairs * 128 * length * length, bytes_accessed=4 * pairs * length * length, transcendentals=0),
        name="attention_backward",
    )(qkv_rows, qkv_rows, qkv_rows, grads, probs)


EPS = 1e-06
BOUNDS = (12, 16, 23, 32, 46, 64, 91)
TOP_PRECISION = lax.Precision.HIGHEST
AXES = ("dp", "expert")
PAIR = 2


def outer_kernel(picks, left, right, *parts):
    whole = dot_f32(left[...], right[...], TN).astype(jnp.bfloat16)
    rows = whole.shape[0] // len(parts)
    for place, part in enumerate(parts):
        part[0] = whole[place * rows : (place + 1) * rows]


def outer_slices(picks, left, right, rows, pieces):
    depth, width = right.shape
    count = picks.shape[0]
    return pl.pallas_call(
        outer_kernel,
        grid_spec=pltpu.PrefetchScalarGridSpec(
            num_scalar_prefetch=1,
            grid=(count,),
            in_specs=[
                pl.BlockSpec((depth, rows), lambda i, picks: (0, picks[i])),
                pl.BlockSpec((depth, width), lambda i, picks: (0, 0)),
            ],
            out_specs=[pl.BlockSpec((1, rows // pieces, width), lambda i, picks: (i, 0, 0))] * pieces,
        ),
        out_shape=[jax.ShapeDtypeStruct((count, rows // pieces, width), jnp.bfloat16)] * pieces,
        compiler_params=pltpu.CompilerParams(vmem_limit_bytes=VMEM_BYTES),
        cost_estimate=pl.CostEstimate(flops=2 * count * depth * rows * width, bytes_accessed=2 * depth * (count * rows + width) + 2 * count * rows * width, transcendentals=0),
        name="outer_slices",
    )(picks, left, right)


def bucket_index(offset):
    distance = jnp.abs(offset)
    far_bucket = 8 + sum([(distance >= level).astype(jnp.int32) for level in BOUNDS])
    near_bucket = jnp.where(distance < 8, distance, far_bucket)
    return jnp.where(offset > 0, 16, 0) + near_bucket


def norm_apply(inputs, gain_vec):
    return inputs * lax.rsqrt(jnp.mean(inputs * inputs, axis=-1, keepdims=True) + EPS) * gain_vec


def gate_values(logits, routes):
    soft_probs = jax.nn.softmax(logits, axis=-1)
    picked_hot = (
        routes[:, :, None] == jnp.arange(logits.shape[1], dtype=jnp.int32)[None, None, :]
    ).astype(jnp.float32)
    chosen = jnp.sum(soft_probs[:, None, :] * picked_hot, axis=-1)
    return chosen / jnp.sum(chosen, axis=1, keepdims=True)


def tile_offsets(query_block, key_block):
    rows = query_block * BLOCK + lax.broadcasted_iota(jnp.int32, (BLOCK, BLOCK), 0)
    cols = key_block * BLOCK + lax.broadcasted_iota(jnp.int32, (BLOCK, BLOCK), 1)
    return rows, cols


def near_bias(table, prefix_len, blocks):
    buckets = table.shape[1]
    tiles = []
    for query_block, key_block in near_pairs(blocks):
        rows, cols = tile_offsets(query_block, key_block)
        hot = (bucket_index(cols - rows)[None] == jnp.arange(buckets, dtype=jnp.int32)[:, None, None]).astype(jnp.float32)
        tile = jnp.einsum("hb,bxy->hxy", table, hot, precision=TOP_PRECISION)
        if key_block >= query_block:
            tile = jnp.where(((cols <= rows) | (cols < prefix_len))[None], tile, -1e30)
        tiles.append(tile)
    return jnp.stack(tiles, axis=1)


def table_gradient(bands, buckets):
    rows, cols = tile_offsets(0, 0)
    ids = [jnp.full((BLOCK, BLOCK), bucket_far(), jnp.int32)]
    ids += [bucket_index(shift * BLOCK + cols - rows) for shift in (-1, 0, 1)]
    hot = (jnp.stack(ids)[..., None] == jnp.arange(buckets, dtype=jnp.int32)).astype(jnp.float32)
    return jnp.einsum("hdxy,dxyb->hb", bands, hot, precision=TOP_PRECISION)


def bucket_far():
    return 8 + len(BOUNDS)


def on_device(
    tokens,
    qkv_weight,
    out_weight,
    position_bias_table,
    gain_attn,
    gain_moe,
    router,
    w_in,
    w_out,
    routes,
    prefix,
    valid_mask,
    teacher,
    cotangent,
):
    length, width = tokens.shape
    bf16, f32 = jnp.bfloat16, jnp.float32
    expert_count = router.shape[1]
    top_count = routes.shape[1]
    groups = lax.axis_size("expert")
    copies = lax.axis_size("dp")
    inner = w_in.shape[2]
    capacity = 5 * length * top_count // (4 * expert_count)
    total_tokens = length * copies * groups
    sources = 2 * groups
    blocks = length // BLOCK
    here_dp, here_group = lax.axis_index("dp"), lax.axis_index("expert")
    half = (here_dp // PAIR) % 2
    core = here_group % 2
    rest = copies // 4

    def swap(value, dp_mask, group_mask):
        pairs = [
            (i, ((i // groups) ^ dp_mask) * groups + ((i % groups) ^ group_mask))
            for i in range(copies * groups)
        ]
        return lax.ppermute(value, AXES, pairs)

    def bits(count):
        return [1 << place for place in range(count.bit_length() - 1)]

    def all_sum(value):
        for mask in bits(groups):
            value = value + swap(value, 0, mask)
        for mask in bits(copies):
            value = value + swap(value, mask, 0)
        return value

    def exchange(rows):
        parts = rows.reshape(sources, capacity, width)
        got = [parts[0]]
        for away in range(1, sources):
            got.append(swap(parts[away], PAIR * (away // groups), away % groups))
        return jnp.concatenate(got, axis=0)

    def gather_weight(piece, axis):
        columns = piece.shape[-1] // 2
        mine = lax.dynamic_slice_in_dim(piece, core * columns, columns, piece.ndim - 1)
        mine = lax.all_gather(mine, "dp", axis=axis, tiled=True)
        other = swap(mine, 0, 1)
        first, second = jnp.where(core == 0, mine, other), jnp.where(core == 0, other, mine)
        return jnp.concatenate([first, second], axis=-1)

    qkv_full = gather_weight(qkv_weight, 1)
    out_full = gather_weight(out_weight, 0)
    valid_rows = valid_mask.astype(f32)[:, None]
    valid_count = all_sum(jnp.broadcast_to(jnp.sum(valid_rows), (8, 128)))[0, 0]
    prefix_len = prefix[0]
    near = near_bias(position_bias_table, prefix_len, blocks)

    flat_routes = routes.reshape(-1)
    pair_count = length * top_count
    slot_count = sources * capacity
    route_hits = (flat_routes[:, None] == jnp.arange(expert_count, dtype=jnp.int32)[None, :]).astype(bf16)
    lower_ones = (
        lax.broadcasted_iota(jnp.int32, (pair_count, pair_count), 0)
        >= lax.broadcasted_iota(jnp.int32, (pair_count, pair_count), 1)
    ).astype(bf16)
    running = jnp.dot(lower_ones, route_hits, preferred_element_type=f32)
    pair_rank = jnp.sum((running - 1.0) * route_hits.astype(f32), axis=1).astype(jnp.int32)
    away = ((flat_routes % 2) ^ half) * groups + ((flat_routes // 2) ^ here_group)
    slot_of_pair = (away * capacity + pair_rank).reshape(length, top_count)
    slot_hot = (
        slot_of_pair[:, :, None] == lax.broadcasted_iota(jnp.int32, (1, 1, slot_count), 2)
    ).astype(bf16)

    resid = tokens.astype(f32)
    normed1 = norm_apply(resid, gain_attn).astype(bf16)
    qkv_rows = jnp.einsum("td,cde->cte", normed1, qkv_full, preferred_element_type=f32).astype(bf16)
    attended, probs = attention_forward(position_bias_table[:, bucket_far()], qkv_rows, near)
    middle = resid + jnp.dot(attended, out_full, preferred_element_type=f32)
    normed2 = norm_apply(middle, gain_moe).astype(bf16)
    logits = jnp.dot(normed2, router, preferred_element_type=f32)
    gate_vals = gate_values(logits, routes)

    send_rows = jnp.einsum("tks,td->sd", slot_hot, normed2, preferred_element_type=f32).astype(bf16)
    rows_in = exchange(send_rows)
    pick = half.reshape(1).astype(jnp.int32)
    hidden, slope, produced = expert_forward(pick, rows_in, w_in, w_out)
    returned = exchange(produced)
    picked = jnp.einsum("tks,sd->tkd", slot_hot, returned, preferred_element_type=f32)
    output = middle + jnp.sum(gate_vals[:, :, None] * picked, axis=1)
    misfit = output - teacher.astype(f32)
    square_sum = jnp.sum(valid_rows * misfit * misfit)
    grad_y = cotangent.astype(f32) + valid_rows * misfit * (total_tokens / valid_count)
    grad_pairs = (gate_vals[:, :, None] * grad_y[:, None, :]).astype(bf16)
    send_grads = jnp.einsum("tks,tkd->sd", slot_hot, grad_pairs, preferred_element_type=f32).astype(bf16)
    grad_rows = exchange(send_grads)

    out_rows = inner // copies
    in_rows = width // copies
    far_bit = here_dp % 2
    slices = jnp.arange(rest, dtype=jnp.int32) * 4

    def owner_slices(other_half, bit0):
        return (slices + ((half ^ other_half) * 2 + bit0)).astype(jnp.int32)

    def out_units(bit0):
        units = []
        for other_half in (1, 0):
            picks = owner_slices(other_half, bit0)
            if out_rows % 128 == 0:
                units += outer_slices(picks, hidden, grad_rows, out_rows, 2)
            else:
                part = jnp.take(hidden.reshape(-1, copies, out_rows), picks, axis=1)
                part = jnp.einsum("rsf,rd->sfd", part, grad_rows, preferred_element_type=f32).astype(bf16)
                units += [part[:, : out_rows // 2], part[:, out_rows // 2 :]]
        return units

    def in_units(bit0):
        rows_t = rows_in.T.reshape(rest, 2, 2, in_rows, slot_count)
        rows_t = lax.dynamic_index_in_dim(rows_t, bit0, 2, keepdims=False)
        units = []
        for other_half in (1, 0):
            part = lax.dynamic_index_in_dim(rows_t, half ^ other_half, 1, keepdims=False)
            for piece in range(2):
                cols = grad_pre[:, piece * (inner // 2) : (piece + 1) * (inner // 2)]
                units.append(jnp.einsum("sir,rf->sif", part, cols, preferred_element_type=f32).astype(bf16))
        return units

    send_units = out_units(1 - far_bit)
    got_units = [swap(unit, 1, 0) for unit in send_units]
    grad_pre, grad_in_rows = expert_backward(pick, grad_rows, w_in, w_out, slope)
    sent_back = exchange(grad_in_rows)
    send_units = in_units(1 - far_bit)
    got_units += [swap(unit, 1, 0) for unit in send_units]
    keep_units = out_units(far_bit) + in_units(far_bit)

    reduced = []
    token = None
    for got, keep in zip(got_units, keep_units):
        if token is not None:
            got, _ = lax.optimization_barrier((got, token))
        unit = (got.astype(f32) + keep.astype(f32)).astype(bf16)
        for mask in reversed(bits(copies)[2:]):
            bit = (here_dp // mask) % 2
            unit = unit.reshape((2, unit.shape[0] // 2) + unit.shape[1:])
            away_part = lax.dynamic_index_in_dim(unit, 1 - bit, 0, keepdims=False)
            stay_part = lax.dynamic_index_in_dim(unit, bit, 0, keepdims=False)
            token = stay_part
            unit = (swap(away_part, mask, 0).astype(f32) + stay_part.astype(f32)).astype(bf16)
        reduced.append(unit[0])
    final = []
    for first in (0, 4):
        theirs = [swap(unit, PAIR, 0) for unit in reduced[first : first + 2]]
        axis = 0 if first == 0 else 1
        mine = jnp.concatenate(reduced[first + 2 : first + 4], axis=axis).astype(f32)
        theirs = jnp.concatenate(theirs, axis=axis).astype(f32)
        final.append(jnp.stack([jnp.where(half == 0, mine, theirs), jnp.where(half == 0, theirs, mine)]))
    grad_w_out, grad_w_in = final

    grad_gates = jnp.sum(grad_y[:, None, :] * picked, axis=-1)
    grad_normed2 = jnp.einsum("tks,sd->td", slot_hot, sent_back, preferred_element_type=f32)
    gate_out, gate_back = jax.vjp(lambda logit_vals: gate_values(logit_vals, routes), logits)
    grad_logits = gate_back(grad_gates)[0].astype(bf16)
    grad_router = jnp.einsum("td,te->de", normed2, grad_logits, preferred_element_type=f32)
    grad_normed2 = grad_normed2 + jnp.einsum("te,de->td", grad_logits, router, preferred_element_type=f32)
    norm_out, norm_back = jax.vjp(norm_apply, middle, gain_moe)
    grad_mid_norm, grad_gain_moe = norm_back(grad_normed2)
    grad_middle = grad_y + grad_mid_norm
    grad_attn_proj = grad_middle.astype(bf16)
    grad_attended = jnp.einsum("te,de->td", grad_attn_proj, out_full, preferred_element_type=f32).astype(bf16)
    grad_q, grad_k, grad_v, bands = attention_backward(qkv_rows, grad_attended, probs)

    def weight_gradient(left, right):
        return jnp.einsum("td,te->de", left, right, preferred_element_type=f32).astype(bf16)

    mats = [weight_gradient(normed1, part) for part in (grad_q, grad_k, grad_v)]
    mats.append(weight_gradient(attended, grad_attn_proj))
    group_bits = bits(groups)
    share = 4 * in_rows // groups
    if share == in_rows:
        total = jnp.stack([mats[0], mats[2], mats[1], mats[3]]).reshape((2,) * len(group_bits) + (copies, share, width))
    else:
        total = jnp.stack(mats).reshape(4, copies, in_rows, width).transpose(1, 0, 2, 3)
        total = total.reshape((copies,) + (2,) * len(group_bits) + (share, width))
        order = list(range(len(group_bits), 0, -1)) + [0, len(group_bits) + 1, len(group_bits) + 2]
        total = total.transpose(order)
    for mask in group_bits:
        bit = (here_group // mask) % 2
        away_part = lax.dynamic_index_in_dim(total, 1 - bit, 0, keepdims=False)
        stay_part = lax.dynamic_index_in_dim(total, bit, 0, keepdims=False)
        total = (swap(away_part, 0, mask).astype(f32) + stay_part.astype(f32)).astype(bf16)
    for mask in reversed(bits(copies)):
        bit = (here_dp // mask) % 2
        total = total.reshape((2, total.shape[0] // 2) + total.shape[1:])
        away_part = lax.dynamic_index_in_dim(total, 1 - bit, 0, keepdims=False)
        stay_part = lax.dynamic_index_in_dim(total, bit, 0, keepdims=False)
        total = (swap(away_part, mask, 0).astype(f32) + stay_part.astype(f32)).astype(bf16)
    total = total[0]
    for mask in reversed(group_bits):
        bit = (here_group // mask) % 2
        other = swap(total, 0, mask)
        total = jnp.stack([jnp.where(bit == 0, total, other), jnp.where(bit == 0, other, total)])
    order = list(range(len(group_bits) - 1, -1, -1)) + [len(group_bits), len(group_bits) + 1]
    total = total.transpose(order).reshape(4, in_rows, width).astype(f32)
    grad_qkv, grad_out_weight = total[:3], total[3]

    grad_normed1 = sum(
        jnp.einsum("te,de->td", part, qkv_full[c], preferred_element_type=f32)
        for c, part in enumerate((grad_q, grad_k, grad_v))
    )
    first_out, first_back = jax.vjp(norm_apply, resid, gain_attn)
    grad_resid_norm, grad_gain_attn = first_back(grad_normed1)
    grad_input = grad_middle + grad_resid_norm
    grad_table = table_gradient(bands, position_bias_table.shape[1])

    def sum_many(values):
        flat = jnp.concatenate([value.reshape(-1) for value in values])
        size = flat.shape[0]
        flat = jnp.pad(flat, (0, -size % 1024)).reshape(-1, 128)
        flat = all_sum(flat).reshape(-1)
        done, place = [], 0
        for value in values:
            done.append(flat[place : place + value.size].reshape(value.shape))
            place += value.size
        return done

    grad_gain_moe, grad_router, square_total = sum_many((grad_gain_moe, grad_router, square_sum))
    grad_gain_attn, grad_table = sum_many((grad_gain_attn, grad_table))
    distill_loss = square_total / (width * valid_count)
    return (
        output.astype(bf16),
        distill_loss,
        grad_input,
        grad_qkv,
        grad_out_weight,
        grad_w_in,
        grad_w_out,
        grad_router,
        grad_table,
        grad_gain_attn,
        grad_gain_moe,
    )


def solution(mesh):
    rows = P(AXES, None)
    return jax.shard_map(
        on_device,
        mesh=mesh,
        in_specs=(
            rows,
            P(None, "dp", None),
            P("dp", None),
            P(),
            P(),
            P(),
            P(),
            P("expert", None, None),
            P("expert", None, None),
            rows,
            P(AXES),
            P(AXES),
            rows,
            rows,
        ),
        out_specs=(
            rows,
            P(),
            rows,
            P(None, "dp", None),
            P("dp", None),
            P("expert", "dp", None),
            P("expert", "dp", None),
            P(),
            P(),
            P(),
            P(),
        ),
        check_vma=False,
    )
```

time: 939 us -> 594 us (0.63)
  waiting for transfers between devices: 489 us -> 202 us
  matrix products: 194 us -> 69.8 us
  blocking collectives: 156 us -> 33.5 us
  Pallas kernels: 0 us -> 99.2 us
  starting transfers between devices: 9.12 us -> 75 us
  other arithmetic: 25.5 us -> 40.4 us
    reduce_scatter x3 -> x0, waiting for transfers between devices: 333 us -> none  [the longest x1 163 us: on_device(): lax.psum_scatter(grad_w_in_local.astype(jnp.bfloat16), 'dp', scatter_dime...]
    ppermute x0 -> x72, waiting for transfers between devices: none -> 202 us  [swap(): return lax.ppermute(value, AXES, pairs)]
    dot_general x26 -> x31, matrix products: 171 us -> 68.1 us  [the longest x8 20.3 us: in_units(): jnp.einsum('sir,rf->sif', part, cols, preferred_element_type=f32)]
    psum x2 -> x0, blocking collectives: 100 us -> none  [the longest x1 55.7 us: on_device(): valid_count = lax.psum(jnp.sum(valid_rows), ('dp', 'expert'))]
    pallas_call x0 -> x8, Pallas kernels: none -> 99.2 us  [the longest x1 22.8 us: expert_forward(): pl.pallas_call(lambda *refs: expert_forward_kernel(*refs, chunk=chunk), g...]
    unnamed x8 -> x1, waiting for transfers between devices: 76.6 us -> 0.02 us
    ppermute x0 -> x72, starting transfers between devices: none -> 75 us  [swap(): return lax.ppermute(value, AXES, pairs)]
    all_gather x2 -> x1, waiting for transfers between devices: 58.1 us -> 0.14 us  [gather_weight(): mine = lax.all_gather(mine, 'dp', axis=axis, tiled=True)]
  transfers between devices with their start and end apart: 9 -> 73, of which waited for: 7 -> 31; matrix products, arithmetic and copies ran while one was open for 12% -> 19% of each run, Pallas kernels for 0% -> 5%
where the time goes in v1:
time: 594 us; the launch traced here: 586 us
  waiting for transfers between devices  202 us (34%)
  Pallas kernels  99.2 us (17%)
  starting transfers between devices  75 us (13%)
  matrix products  69.8 us (12%)
  local copies, waits for them, and re-layouts  46 us (8%)
  other arithmetic  40.4 us (7%)
  blocking collectives  33.5 us (6%)
  between operations  20.2 us (3%)
    ppermute x72, waiting for transfers between devices, swap(): return lax.ppermute(value, AXES, pairs)  202 us
    ppermute x72, starting transfers between devices, swap(): return lax.ppermute(value, AXES, pairs)  75 us
    all_gather x1, blocking collectives, gather_weight(): mine = lax.all_gather(mine, 'dp', axis=axis, tiled=True)  33.5 us
    pallas_call x1, Pallas kernels, expert_forward(): pl.pallas_call(lambda *refs: expert_forward_kernel(*refs, chunk=chunk), g...  22.8 us
    unnamed x213, local copies, waits for them, and re-layouts  22.5 us
    pallas_call x4, Pallas kernels, outer_slices(): pl.pallas_call(outer_kernel, grid_spec=pltpu.PrefetchScalarGridSpec(num_s...  21.5 us
    pallas_call x1, Pallas kernels, expert_backward(): pl.pallas_call(lambda *refs: expert_backward_kernel(*refs, chunk=chunk),...  20.9 us
    dot_general x8, matrix products, in_units(): jnp.einsum('sir,rf->sif', part, cols, preferred_element_type=f32)  20.3 us
  transfers between devices with their start and end apart: 73, of which 31 were waited for; matrix products, arithmetic and copies ran while one was open for 19% of the time, Pallas kernels for 5%

profile of v1, /device:TPU:0, one launch (start us, length us, event | category | flops | bytes accessed | tf_op | source)
XLA Modules:
  0.0 586.1 jit_solution(9277526107191364563)
XLA Ops:
  11.4 33.5 %all_gather.7 = bf16[768,384]{1,0:T(8,128)(2,1)S(1)} all-gather(bf16[96,384]{1,0:T(8,128)(2,1)S(1)} %constant_dynamic-slice_fusion.16), channel_id=1, replica_groups=mesh['dp'=8,'expert'=4] {'dp'}, dimensions={0}, use_global_device_ids=true | all-gather | bytes 663552 | tf_op jit(solution)/shard_map/all_gather | solution.py:429
  96.3 16.7 %attention_forward.1 = (bf16[512,768]{1,0:T(8,128)(2,1)}, bf16[12,512,512]{2,1,0:T(8,128)(2,1)}) custom-call(f32[12]{0:T(128)} %slice_reduce_fusion.refs_0_, bf16[3,512,768]{2,1,0:T(8,128)(2,1)} %convert_bitcast_fusion.refs_1_.refs_2_.refs_3_.refs_0_, bf16[3,512,768]{2,1,0:T(8,128)(2,1)} %convert_bitcast_fusion.refs_1_.refs_2_.refs_3_.refs_0_, ...), custom_call_target="tpu_custom_call" | custom-call | flops 1610612736 | bytes 6291456 | tf_op jit(solution)/shard_map/attention_forward/pallas_call | solution.py:192
  125.3 18.2 %collective-permute-done.3 = bf16[160,768]{1,0:T(8,128)(2,1)S(1)} collective-permute-done((bf16[160,768]{1,0:T(8,128)(2,1)S(1)}, bf16[160,768]{1,0:T(8,128)(2,1)S(1)}, u32[]{:S(2)}, u32[]{:S(2)}) %collective-permute-start.3) | collective-permute-done | bytes 245792 | tf_op jit(solution)/shard_map/ppermute | solution.py:407
  145.0 6.5 %collective-permute-done.6 = bf16[160,768]{1,0:T(8,128)(2,1)S(1)} collective-permute-done((bf16[160,768]{1,0:T(8,128)(2,1)S(1)}, bf16[160,768]{1,0:T(8,128)(2,1)S(1)}, u32[]{:S(2)}, u32[]{:S(2)}) %collective-permute-start.6) | collective-permute-done | bytes 245792 | tf_op jit(solution)/shard_map/ppermute | solution.py:407
  152.9 22.8 %expert_forward.1 = (bf16[1280,3072]{1,0:T(8,128)(2,1)}, bf16[1280,3072]{1,0:T(8,128)(2,1)}, bf16[1280,768]{1,0:T(8,128)(2,1)}) custom-call(s32[1]{0:T(128)} %bitcast.17.refs_0_, bf16[1280,768]{1,0:T(8,128)(2,1)} %copy-done.28, bf16[2,768,3072]{2,1,0:T(8,128)(2,1)} %refs_2_.3, bf16[2,3072,768]{2,1,0:T(8,128)(2,1)} %refs_3_.3), custom_call_target="tpu_custom_call" | custom-call | flops 12079595520 | bytes 29097984 | tf_op jit(solution)/shard_map/expert_forward/pallas_call | solution.py:49
  190.6 13.2 %collective-permute-done.10 = bf16[160,768]{1,0:T(8,128)(2,1)} collective-permute-done((bf16[160,768]{1,0:T(8,128)(2,1)}, bf16[160,768]{1,0:T(8,128)(2,1)}, u32[]{:S(2)}, u32[]{:S(2)}) %collective-permute-start.10) | collective-permute-done | bytes 245792 | tf_op jit(solution)/shard_map/ppermute | solution.py:407
  214.2 4.3 multiply_reduce_fusion.1
  236.5 14.2 %collective-permute-done.22 = bf16[160,768]{1,0:T(8,128)(2,1)} collective-permute-done((bf16[160,768]{1,0:T(8,128)(2,1)}, bf16[160,768]{1,0:T(8,128)(2,1)}, u32[]{:S(2)}, u32[]{:S(2)}) %collective-permute-start.22) | collective-permute-done | bytes 245792 | tf_op jit(solution)/shard_map/ppermute | solution.py:407
  254.1 4.9 collective-permute-done.25
  260.4 20.9 %expert_backward.1 = (bf16[1280,3072]{1,0:T(8,128)(2,1)}, bf16[1280,768]{1,0:T(8,128)(2,1)}) custom-call(s32[1]{0:T(128)} %bitcast.17.refs_0_, bf16[1280,768]{1,0:T(8,128)(2,1)} %copy-done.2, bf16[2,768,3072]{2,1,0:T(8,128)(2,1)} %refs_2_.3, bf16[2,3072,768]{2,1,0:T(8,128)(2,1)} %refs_3_.3, bf16[1280,3072]{1,0:T(8,128)(2,1)} %get-tuple-element.39.refs_4_), custom_call_target="tpu_custom_call" | custom-call | flops 12079595520 | bytes 29097984 | tf_op jit(solution)/shard_map/expert_backward/pallas_call | solution.py:100
  281.3 4.0 fusion.38
  291.4 5.3 outer_slices.7
  296.7 5.4 outer_slices.6
  304.5 5.3 outer_slices.5
  309.8 5.5 outer_slices.4
  321.1 5.1 collective-permute-done.31
  326.2 4.3 collective-permute-done.32
  331.6 6.3 %collective-permute-done.33 = bf16[160,768]{1,0:T(8,128)(2,1)S(1)} collective-permute-done((bf16[160,768]{1,0:T(8,128)(2,1)S(1)}, bf16[160,768]{1,0:T(8,128)(2,1)S(1)}, u32[]{:S(2)}, u32[]{:S(2)}) %collective-permute-start.33) | collective-permute-done | bytes 245792 | tf_op jit(solution)/shard_map/ppermute | solution.py:407
  349.0 17.3 %attention_backward.1 = (bf16[512,768]{1,0:T(8,128)(2,1)}, bf16[512,768]{1,0:T(8,128)(2,1)}, bf16[512,768]{1,0:T(8,128)(2,1)}, f32[12,4,128,128]{3,2,1,0:T(8,128)}) custom-call(bf16[3,512,768]{2,1,0:T(8,128)(2,1)} %convert_bitcast_fusion.refs_1_.refs_2_.refs_3_.refs_0_, bf16[3,512,768]{2,1,0:T(8,128)(2,1)} %convert_bitcast_fusion.refs_1_.refs_2_.refs_3_.refs_0_, ...), custom_call_target="tpu_custom_call" | custom-call | flops 4026531840 | bytes 6291456 | tf_op jit(solution)/shard_map/attention_backward/pallas_call | solution.py:270
  377.1 5.3 fusion.109
  396.2 12.4 %collective-permute-done.63 = bf16[1,192,768]{2,1,0:T(8,128)(2,1)S(1)} collective-permute-done((bf16[1,192,768]{2,1,0:T(8,128)(2,1)S(1)}, bf16[1,192,768]{2,1,0:T(8,128)(2,1)S(1)}, u32[]{:S(2)}, u32[]{:S(2)}) %collective-permute-start.63) | collective-permute-done | bytes 294944 | tf_op jit(solution)/shard_map/ppermute | solution.py:407
  415.4 13.2 %collective-permute-done.65 = bf16[1,192,768]{2,1,0:T(8,128)(2,1)S(1)} collective-permute-done((bf16[1,192,768]{2,1,0:T(8,128)(2,1)S(1)}, bf16[1,192,768]{2,1,0:T(8,128)(2,1)S(1)}, u32[]{:S(2)}, u32[]{:S(2)}) %collective-permute-start.65) | collective-permute-done | bytes 294944 | tf_op jit(solution)/shard_map/ppermute | solution.py:407
  434.1 10.5 %collective-permute-done.61 = bf16[1,192,768]{2,1,0:T(8,128)(2,1)S(1)} collective-permute-done((bf16[1,192,768]{2,1,0:T(8,128)(2,1)S(1)}, bf16[1,192,768]{2,1,0:T(8,128)(2,1)S(1)}, u32[]{:S(2)}, u32[]{:S(2)}) %collective-permute-start.61) | collective-permute-done | bytes 294944 | tf_op jit(solution)/shard_map/ppermute | solution.py:407
  453.6 9.5 %collective-permute-done.71 = f32[16,128]{1,0:T(8,128)S(1)} collective-permute-done((f32[16,128]{1,0:T(8,128)S(1)}, f32[16,128]{1,0:T(8,128)S(1)}, u32[]{:S(2)}, u32[]{:S(2)}) %collective-permute-start.71) | collective-permute-done | bytes 8224 | tf_op jit(solution)/shard_map/ppermute | solution.py:407
  477.1 8.8 %collective-permute-done.57 = bf16[1,96,1536]{2,1,0:T(8,128)(2,1)} collective-permute-done((bf16[1,96,1536]{2,1,0:T(8,128)(2,1)}, bf16[1,96,1536]{2,1,0:T(8,128)(2,1)}, u32[]{:S(2)}, u32[]{:S(2)}) %collective-permute-start.57) | collective-permute-done | bytes 294944 | tf_op jit(solution)/shard_map/ppermute | solution.py:407
  493.9 6.9 %collective-permute-done.64 = bf16[192,768]{1,0:T(8,128)(2,1)S(1)} collective-permute-done((bf16[192,768]{1,0:T(8,128)(2,1)}, bf16[192,768]{1,0:T(8,128)(2,1)S(1)}, u32[]{:S(2)}, u32[]{:S(2)}) %collective-permute-start.64) | collective-permute-done | bytes 294944 | tf_op jit(solution)/shard_map/ppermute | solution.py:407
  502.2 4.2 collective-permute-done.66
  510.9 10.5 %collective-permute-done.41 = bf16[8,96,768]{2,1,0:T(8,128)(2,1)S(1)} collective-permute-done((bf16[8,96,768]{2,1,0:T(8,128)(2,1)S(1)}, bf16[8,96,768]{2,1,0:T(8,128)(2,1)S(1)}, u32[]{:S(2)}, u32[]{:S(2)}) %collective-permute-start.41) | collective-permute-done | bytes 1179680 | tf_op jit(solution)/shard_map/ppermute | solution.py:407
  527.4 7.9 %collective-permute-done.54 = bf16[1,96,1536]{2,1,0:T(8,128)(2,1)S(1)} collective-permute-done((bf16[1,96,1536]{2,1,0:T(8,128)(2,1)S(1)}, bf16[1,96,1536]{2,1,0:T(8,128)(2,1)S(1)}, u32[]{:S(2)}, u32[]{:S(2)}) %collective-permute-start.54) | collective-permute-done | bytes 294944 | tf_op jit(solution)/shard_map/ppermute | solution.py:407
  535.4 14.7 %collective-permute-done.42 = bf16[4,96,768]{2,1,0:T(8,128)(2,1)S(1)} collective-permute-done((bf16[4,96,768]{2,1,0:T(8,128)(2,1)S(1)}, bf16[4,96,768]{2,1,0:T(8,128)(2,1)S(1)}, u32[]{:S(2)}, u32[]{:S(2)}) %collective-permute-start.42) | collective-permute-done | bytes 589856 | tf_op jit(solution)/shard_map/ppermute | solution.py:407
  555.4 7.7 %collective-permute-done.43 = bf16[2,96,768]{2,1,0:T(8,128)(2,1)S(1)} collective-permute-done((bf16[2,96,768]{2,1,0:T(8,128)(2,1)S(1)}, bf16[2,96,768]{2,1,0:T(8,128)(2,1)S(1)}, u32[]{:S(2)}, u32[]{:S(2)}) %collective-permute-start.43) | collective-permute-done | bytes 294944 | tf_op jit(solution)/shard_map/ppermute | solution.py:407
  564.5 4.2 collective-permute-done.56
  (509 shorter events, 236.4 us)
Async XLA Ops:
  7.2 53.5 %all-gather.2.cloned.1.call-start = ((), (), s32[]{:S(2)}) async-start(), calls=%async_computation | async-start | bytes 1990656 | tf_op jit(solution)/shard_map/all_gather | solution.py:429
  9.3 59.7 %collective-permute-start.16 = (f32[8,128]{1,0:T(8,128)S(1)}, f32[8,128]{1,0:T(8,128)S(1)}, u32[]{:S(2)}, u32[]{:S(2)}) collective-permute-start(f32[8,128]{1,0:T(8,128)S(1)} %broadcast_in_dim.118), channel_id=1, source_target_pairs={{0,1},{1,0},{2,3},{3,2},{4,5},{5,4},{6,7},{7,6},{8,9},{9,8},{10,11... | collective-permute-start | bytes 12296 | tf_op jit(solution)/shard_map/ppermute | solution.py:407
  44.9 42.7 %collective-permute-start.1 = (bf16[768,384]{1,0:T(8,128)(2,1)S(1)}, bf16[768,384]{1,0:T(8,128)(2,1)}, u32[]{:S(2)}, u32[]{:S(2)}) collective-permute-start(bf16[768,384]{1,0:T(8,128)(2,1)S(1)} %all_gather.7), channel_id=1, source_target_pairs={{0,1},{1,0},{2,3},{3,2},{4,5},{5,4},{6,7},{7,6},{8,9},{9,8},{10,11... | collective-permute-start | bytes 1769480 | tf_op jit(solution)/shard_map/ppermute | solution.py:407
  63.5 25.3 %collective-permute-start = (bf16[3,768,384]{1,2,0:T(8,128)(2,1)S(1)}, bf16[3,768,384]{1,2,0:T(8,128)(2,1)}, u32[]{:S(2)}, u32[]{:S(2)}) collective-permute-start(bf16[3,768,384]{1,2,0:T(8,128)(2,1)S(1)} %copy.131), channel_id=1, source_target_pairs={{0,1},{1,0},{2,3},{3,2},{4,5},{5,4},{6,7},{7,6},{8,9},{9,8},{10,11... | collective-permute-start | bytes 5308424 | tf_op jit(solution)/shard_map/ppermute | solution.py:407
  118.5 33.1 %collective-permute-start.8 = (bf16[160,768]{1,0:T(8,128)(2,1)S(1)}, bf16[160,768]{1,0:T(8,128)(2,1)S(1)}, u32[]{:S(2)}, u32[]{:S(2)}) collective-permute-start(bf16[160,768]{1,0:T(8,128)(2,1)S(1)} %get-tuple-element.155), channel_id=1, source_target_pairs={{0,11},{1,10},{2,9},{3,8},{4,15},{5,14},{6,13},{7,12},{8,3},{9,2},... | collective-permute-start | bytes 737288 | tf_op jit(solution)/shard_map/ppermute | solution.py:407
  120.8 30.7 %collective-permute-start.7 = (bf16[160,768]{1,0:T(8,128)(2,1)S(1)}, bf16[160,768]{1,0:T(8,128)(2,1)S(1)}, u32[]{:S(2)}, u32[]{:S(2)}) collective-permute-start(bf16[160,768]{1,0:T(8,128)(2,1)S(1)} %get-tuple-element.156), channel_id=1, source_target_pairs={{0,10},{1,11},{2,8},{3,9},{4,14},{5,15},{6,12},{7,13},{8,2},{9,3},... | collective-permute-start | bytes 737288 | tf_op jit(solution)/shard_map/ppermute | solution.py:407
  121.3 23.7 %collective-permute-start.4 = (bf16[160,768]{1,0:T(8,128)(2,1)S(1)}, bf16[160,768]{1,0:T(8,128)(2,1)S(1)}, u32[]{:S(2)}, u32[]{:S(2)}) collective-permute-start(bf16[160,768]{1,0:T(8,128)(2,1)S(1)} %get-tuple-element.159), channel_id=1, source_target_pairs={{0,3},{1,2},{2,1},{3,0},{4,7},{5,6},{6,5},{7,4},{8,11},{9,10},{10,... | collective-permute-start | bytes 737288 | tf_op jit(solution)/shard_map/ppermute | solution.py:407
  122.6 21.0 %collective-permute-start.3 = (bf16[160,768]{1,0:T(8,128)(2,1)S(1)}, bf16[160,768]{1,0:T(8,128)(2,1)S(1)}, u32[]{:S(2)}, u32[]{:S(2)}) collective-permute-start(bf16[160,768]{1,0:T(8,128)(2,1)S(1)} %get-tuple-element.160), channel_id=1, source_target_pairs={{0,2},{1,3},{2,0},{3,1},{4,6},{5,7},{6,4},{7,5},{8,10},{9,11},{10,... | collective-permute-start | bytes 737288 | tf_op jit(solution)/shard_map/ppermute | solution.py:407
  123.6 21.4 %collective-permute-start.5 = (bf16[160,768]{1,0:T(8,128)(2,1)S(1)}, bf16[160,768]{1,0:T(8,128)(2,1)S(1)}, u32[]{:S(2)}, u32[]{:S(2)}) collective-permute-start(bf16[160,768]{1,0:T(8,128)(2,1)S(1)} %get-tuple-element.158), channel_id=1, source_target_pairs={{0,8},{1,9},{2,10},{3,11},{4,12},{5,13},{6,14},{7,15},{8,0},{9,1},... | collective-permute-start | bytes 737288 | tf_op jit(solution)/shard_map/ppermute | solution.py:407
  179.4 26.9 %collective-permute-start.11 = (bf16[160,768]{1,0:T(8,128)(2,1)}, bf16[160,768]{1,0:T(8,128)(2,1)}, u32[]{:S(2)}, u32[]{:S(2)}) collective-permute-start(bf16[160,768]{1,0:T(8,128)(2,1)} %get-tuple-element.151), channel_id=1, source_target_pairs={{0,3},{1,2},{2,1},{3,0},{4,7},{5,6},{6,5},{7,4},{8,11},{9,10},{10,... | collective-permute-start | bytes 737288 | tf_op jit(solution)/shard_map/ppermute | solution.py:407
  181.1 22.7 %collective-permute-start.10 = (bf16[160,768]{1,0:T(8,128)(2,1)}, bf16[160,768]{1,0:T(8,128)(2,1)}, u32[]{:S(2)}, u32[]{:S(2)}) collective-permute-start(bf16[160,768]{1,0:T(8,128)(2,1)} %get-tuple-element.152), channel_id=1, source_target_pairs={{0,2},{1,3},{2,0},{3,1},{4,6},{5,7},{6,4},{7,5},{8,10},{9,11},{10,... | collective-permute-start | bytes 737288 | tf_op jit(solution)/shard_map/ppermute | solution.py:407
  184.8 28.7 %collective-permute-start.15 = (bf16[160,768]{1,0:T(8,128)(2,1)}, bf16[160,768]{1,0:T(8,128)(2,1)S(1)}, u32[]{:S(2)}, u32[]{:S(2)}) collective-permute-start(bf16[160,768]{1,0:T(8,128)(2,1)} %get-tuple-element.147), channel_id=1, source_target_pairs={{0,11},{1,10},{2,9},{3,8},{4,15},{5,14},{6,13},{7,12},{8,3},{9,2},... | collective-permute-start | bytes 737288 | tf_op jit(solution)/shard_map/ppermute | solution.py:407
  186.9 25.9 %collective-permute-start.14 = (bf16[160,768]{1,0:T(8,128)(2,1)}, bf16[160,768]{1,0:T(8,128)(2,1)S(1)}, u32[]{:S(2)}, u32[]{:S(2)}) collective-permute-start(bf16[160,768]{1,0:T(8,128)(2,1)} %get-tuple-element.148), channel_id=1, source_target_pairs={{0,10},{1,11},{2,8},{3,9},{4,14},{5,15},{6,12},{7,13},{8,2},{9,3},... | collective-permute-start | bytes 737288 | tf_op jit(solution)/shard_map/ppermute | solution.py:407
  187.6 20.4 %collective-permute-start.12 = (bf16[160,768]{1,0:T(8,128)(2,1)}, bf16[160,768]{1,0:T(8,128)(2,1)S(1)}, u32[]{:S(2)}, u32[]{:S(2)}) collective-permute-start(bf16[160,768]{1,0:T(8,128)(2,1)} %get-tuple-element.150), channel_id=1, source_target_pairs={{0,8},{1,9},{2,10},{3,11},{4,12},{5,13},{6,14},{7,15},{8,0},{9,1},... | collective-permute-start | bytes 737288 | tf_op jit(solution)/shard_map/ppermute | solution.py:407
  226.4 26.7 %collective-permute-start.23 = (bf16[160,768]{1,0:T(8,128)(2,1)}, bf16[160,768]{1,0:T(8,128)(2,1)}, u32[]{:S(2)}, u32[]{:S(2)}) collective-permute-start(bf16[160,768]{1,0:T(8,128)(2,1)} %get-tuple-element.143), channel_id=1, source_target_pairs={{0,3},{1,2},{2,1},{3,0},{4,7},{5,6},{6,5},{7,4},{8,11},{9,10},{10,... | collective-permute-start | bytes 737288 | tf_op jit(solution)/shard_map/ppermute | solution.py:407
  227.9 22.9 %collective-permute-start.22 = (bf16[160,768]{1,0:T(8,128)(2,1)}, bf16[160,768]{1,0:T(8,128)(2,1)}, u32[]{:S(2)}, u32[]{:S(2)}) collective-permute-start(bf16[160,768]{1,0:T(8,128)(2,1)} %get-tuple-element.144), channel_id=1, source_target_pairs={{0,2},{1,3},{2,0},{3,1},{4,6},{5,7},{6,4},{7,5},{8,10},{9,11},{10,... | collective-permute-start | bytes 737288 | tf_op jit(solution)/shard_map/ppermute | solution.py:407
  231.2 27.8 %collective-permute-start.27 = (bf16[160,768]{1,0:T(8,128)(2,1)}, bf16[160,768]{1,0:T(8,128)(2,1)S(1)}, u32[]{:S(2)}, u32[]{:S(2)}) collective-permute-start(bf16[160,768]{1,0:T(8,128)(2,1)} %get-tuple-element.139), channel_id=1, source_target_pairs={{0,11},{1,10},{2,9},{3,8},{4,15},{5,14},{6,13},{7,12},{8,3},{9,2},... | collective-permute-start | bytes 737288 | tf_op jit(solution)/shard_map/ppermute | solution.py:407
  233.5 25.5 %collective-permute-start.26 = (bf16[160,768]{1,0:T(8,128)(2,1)}, bf16[160,768]{1,0:T(8,128)(2,1)S(1)}, u32[]{:S(2)}, u32[]{:S(2)}) collective-permute-start(bf16[160,768]{1,0:T(8,128)(2,1)} %get-tuple-element.140), channel_id=1, source_target_pairs={{0,10},{1,11},{2,8},{3,9},{4,14},{5,15},{6,12},{7,13},{8,2},{9,3},... | collective-permute-start | bytes 737288 | tf_op jit(solution)/shard_map/ppermute | solution.py:407
  315.3 193.0 %collective-permute-start.47 = (bf16[2,96,1536]{2,1,0:T(8,128)(2,1)}, bf16[2,96,1536]{2,1,0:T(8,128)(2,1)}, u32[]{:S(2)}, u32[]{:S(2)}) collective-permute-start(bf16[2,96,1536]{2,1,0:T(8,128)(2,1)} %fusion.35), channel_id=1, source_target_pairs={{0,4},{1,5},{2,6},{3,7},{4,0},{5,1},{6,2},{7,3},{8,12},{9,13},{10,... | collective-permute-start | bytes 1769480 | tf_op jit(solution)/shard_map/ppermute | solution.py:407
  317.0 92.5 %collective-permute-start.52 = (bf16[2,192,768]{2,1,0:T(8,128)(2,1)}, bf16[2,192,768]{2,1,0:T(8,128)(2,1)}, u32[]{:S(2)}, u32[]{:S(2)}) collective-permute-start(bf16[2,192,768]{2,1,0:T(8,128)(2,1)} %get-tuple-element.49), channel_id=1, source_target_pairs={{0,4},{1,5},{2,6},{3,7},{4,0},{5,1},{6,2},{7,3},{8,12},{9,13},{10,... | collective-permute-start | bytes 1769480 | tf_op jit(solution)/shard_map/ppermute | solution.py:407
  330.5 58.7 %collective-permute-start.53 = (bf16[2,192,768]{2,1,0:T(8,128)(2,1)}, bf16[2,192,768]{2,1,0:T(8,128)(2,1)}, u32[]{:S(2)}, u32[]{:S(2)}) collective-permute-start(bf16[2,192,768]{2,1,0:T(8,128)(2,1)} %get-tuple-element.50), channel_id=1, source_target_pairs={{0,4},{1,5},{2,6},{3,7},{4,0},{5,1},{6,2},{7,3},{8,12},{9,13},{10,... | collective-permute-start | bytes 1769480 | tf_op jit(solution)/shard_map/ppermute | solution.py:407
  338.0 108.2 %collective-permute-start.50 = (bf16[2,192,768]{2,1,0:T(8,128)(2,1)}, bf16[2,192,768]{2,1,0:T(8,128)(2,1)}, u32[]{:S(2)}, u32[]{:S(2)}) collective-permute-start(bf16[2,192,768]{2,1,0:T(8,128)(2,1)} %get-tuple-element.47), channel_id=1, source_target_pairs={{0,4},{1,5},{2,6},{3,7},{4,0},{5,1},{6,2},{7,3},{8,12},{9,13},{10,... | collective-permute-start | bytes 1769480 | tf_op jit(solution)/shard_map/ppermute | solution.py:407
  394.8 35.2 %collective-permute-start.51 = (bf16[2,192,768]{2,1,0:T(8,128)(2,1)S(1)}, bf16[2,192,768]{2,1,0:T(8,128)(2,1)S(1)}, u32[]{:S(2)}, u32[]{:S(2)}) collective-permute-start(bf16[2,192,768]{2,1,0:T(8,128)(2,1)S(1)} %copy-done.87), channel_id=1, source_target_pairs={{0,4},{1,5},{2,6},{3,7},{4,0},{5,1},{6,2},{7,3},{8,12},{9,13},{10,... | collective-permute-start | bytes 1769480 | tf_op jit(solution)/shard_map/ppermute | solution.py:407
  430.3 33.9 %collective-permute-start.49 = (bf16[2,96,1536]{2,1,0:T(8,128)(2,1)S(1)}, bf16[2,96,1536]{2,1,0:T(8,128)(2,1)S(1)}, u32[]{:S(2)}, u32[]{:S(2)}) collective-permute-start(bf16[2,96,1536]{2,1,0:T(8,128)(2,1)S(1)} %copy-done.86), channel_id=1, source_target_pairs={{0,4},{1,5},{2,6},{3,7},{4,0},{5,1},{6,2},{7,3},{8,12},{9,13},{10,... | collective-permute-start | bytes 1769480 | tf_op jit(solution)/shard_map/ppermute | solution.py:407
  463.1 24.1 %collective-permute-start.48 = (bf16[2,96,1536]{2,1,0:T(8,128)(2,1)}, bf16[2,96,1536]{2,1,0:T(8,128)(2,1)}, u32[]{:S(2)}, u32[]{:S(2)}) collective-permute-start(bf16[2,96,1536]{2,1,0:T(8,128)(2,1)} %fusion.53), channel_id=1, source_target_pairs={{0,4},{1,5},{2,6},{3,7},{4,0},{5,1},{6,2},{7,3},{8,12},{9,13},{10,... | collective-permute-start | bytes 1769480 | tf_op jit(solution)/shard_map/ppermute | solution.py:407
  464.0 28.9 %collective-permute-start.40 = (bf16[2,8,96,768]{3,2,1,0:T(8,128)(2,1)}, bf16[2,8,96,768]{3,2,1,0:T(8,128)(2,1)S(1)}, u32[]{:S(2)}, u32[]{:S(2)}) collective-permute-start(bf16[2,8,96,768]{3,2,1,0:T(8,128)(2,1)} %dynamic-slice_bitcast_fusion), channel_id=1, source_target_pairs={{0,1},{1,0},{2,3},{3,2},{4,5},{5,4},{6,7},{7,6},{8,9},{9,8},{10,11... | collective-permute-start | bytes 7077896 | tf_op jit(solution)/shard_map/ppermute | solution.py:407
  473.1 62.3 %collective-permute-start.55 = (bf16[2,96,1536]{2,1,0:T(8,128)(2,1)}, bf16[2,96,1536]{2,1,0:T(8,128)(2,1)}, u32[]{:S(2)}, u32[]{:S(2)}) collective-permute-start(bf16[2,96,1536]{2,1,0:T(8,128)(2,1)} %fusion.62), channel_id=1, source_target_pairs={{0,4},{1,5},{2,6},{3,7},{4,0},{5,1},{6,2},{7,3},{8,12},{9,13},{10,... | collective-permute-start | bytes 1769480 | tf_op jit(solution)/shard_map/ppermute | solution.py:407
  500.7 20.7 %collective-permute-start.41 = (bf16[8,96,768]{2,1,0:T(8,128)(2,1)S(1)}, bf16[8,96,768]{2,1,0:T(8,128)(2,1)S(1)}, u32[]{:S(2)}, u32[]{:S(2)}) collective-permute-start(bf16[8,96,768]{2,1,0:T(8,128)(2,1)S(1)} %dynamic-slice_bitcast_fusion.1), channel_id=1, source_target_pairs={{0,2},{1,3},{2,0},{3,1},{4,6},{5,7},{6,4},{7,5},{8,10},{9,11},{10,... | collective-permute-start | bytes 3538952 | tf_op jit(solution)/shard_map/ppermute | solution.py:407
  510.4 24.9 %collective-permute-start.54 = (bf16[1,96,1536]{2,1,0:T(8,128)(2,1)S(1)}, bf16[1,96,1536]{2,1,0:T(8,128)(2,1)S(1)}, u32[]{:S(2)}, u32[]{:S(2)}) collective-permute-start(bf16[1,96,1536]{2,1,0:T(8,128)(2,1)S(1)} %constant_dynamic-slice_fusion.8), channel_id=1, source_target_pairs={{0,16},{1,17},{2,18},{3,19},{4,20},{5,21},{6,22},{7,23},{8,24},{9,... | collective-permute-start | bytes 884744 | tf_op jit(solution)/shard_map/ppermute | solution.py:407
  521.8 28.4 %collective-permute-start.42 = (bf16[4,96,768]{2,1,0:T(8,128)(2,1)S(1)}, bf16[4,96,768]{2,1,0:T(8,128)(2,1)S(1)}, u32[]{:S(2)}, u32[]{:S(2)}) collective-permute-start(bf16[4,96,768]{2,1,0:T(8,128)(2,1)S(1)} %dynamic-slice_bitcast_fusion.2), channel_id=1, source_target_pairs={{0,16},{1,17},{2,18},{3,19},{4,20},{5,21},{6,22},{7,23},{8,24},{9,... | collective-permute-start | bytes 1769480 | tf_op jit(solution)/shard_map/ppermute | solution.py:407
  525.4 45.0 %collective-permute-start.58 = (bf16[96,1536]{1,0:T(8,128)(2,1)S(1)}, bf16[96,1536]{1,0:T(8,128)(2,1)S(1)}, u32[]{:S(2)}, u32[]{:S(2)}) collective-permute-start(bf16[96,1536]{1,0:T(8,128)(2,1)S(1)} %fusion.153), channel_id=1, source_target_pairs={{0,8},{1,9},{2,10},{3,11},{4,12},{5,13},{6,14},{7,15},{8,0},{9,1},... | collective-permute-start | bytes 884744 | tf_op jit(solution)/shard_map/ppermute | solution.py:407
  525.8 44.6 %collective-permute-start.60 = (bf16[96,1536]{1,0:T(8,128)(2,1)S(1)}, bf16[96,1536]{1,0:T(8,128)(2,1)S(1)}, u32[]{:S(2)}, u32[]{:S(2)}) collective-permute-start(bf16[96,1536]{1,0:T(8,128)(2,1)S(1)} %fusion.154), channel_id=1, source_target_pairs={{0,8},{1,9},{2,10},{3,11},{4,12},{5,13},{6,14},{7,15},{8,0},{9,1},... | collective-permute-start | bytes 884744 | tf_op jit(solution)/shard_map/ppermute | solution.py:407
  (134 other events, 1509.8 us)
Sparse Core Ops, SparseCore 0:
  10.8 49.8 all-gather.1

commit v2 on v1

--- a/solution.py
+++ b/solution.py
@@ -7,6 +7,7 @@
 from jax.sharding import PartitionSpec as P
 
 BLOCK = 128
+THIRDS = 3
 GELU_A = math.sqrt(2.0 / math.pi)
 GELU_B = 0.044715
 NT = (((1,), (1,)), ((), ()))
@@ -14,16 +15,21 @@
 VMEM_BYTES = 56 * 1024 * 1024
 
 
+def cost(micros):
+    return pl.CostEstimate(flops=int(micros * 1.1e9), bytes_accessed=0, transcendentals=0)
+
+
 def dot_f32(left, right, dims=(((1,), (0,)), ((), ()))):
     return lax.dot_general(left, right, dims, preferred_element_type=jnp.float32)
 
 
-def expert_forward_kernel(pick, rows, w_in, w_out, hidden, slope, produced, total, *, chunk):
+def expert_forward_kernel(pick, rows, w_in, w_out, hidden_t, slope, produced, rows_t, total, *, chunk):
     step = pl.program_id(0)
 
     @pl.when(step == 0)
     def _():
         total[...] = jnp.zeros_like(total)
+        rows_t[...] = rows[...].T
 
     for start in range(0, rows.shape[0], chunk):
         part = pl.ds(start, chunk)
@@ -34,7 +40,7 @@
         act = (pre * half).astype(jnp.bfloat16)
         lift = pre * (0.5 * GELU_A + (1.5 * GELU_A * GELU_B) * square)
         slope[part, :] = (half + lift * (1.0 - bend * bend)).astype(jnp.bfloat16)
-        hidden[part, :] = act
+        hidden_t[:, part] = act.T
         total[part, :] += dot_f32(act, w_out[0])
 
     @pl.when(step == pl.num_programs(0) - 1)
@@ -45,7 +51,6 @@
 def expert_forward(pick, rows, w_in, w_out, tile=512, chunk=256):
     count, width = rows.shape
     inner = w_in.shape[2]
-    if count % chunk: chunk = count
     return pl.pallas_call(
         lambda *refs: expert_forward_kernel(*refs, chunk=chunk),
         grid_spec=pltpu.PrefetchScalarGridSpec(
@@ -57,19 +62,21 @@
                 pl.BlockSpec((1, tile, width), lambda f, pick: (pick[0], f, 0)),
             ],
             out_specs=[
-                pl.BlockSpec((count, tile), lambda f, pick: (0, f)),
+                pl.BlockSpec((tile, count), lambda f, pick: (f, 0)),
                 pl.BlockSpec((count, tile), lambda f, pick: (0, f)),
                 pl.BlockSpec((count, width), lambda f, pick: (0, 0)),
+                pl.BlockSpec((width, count), lambda f, pick: (0, 0)),
             ],
             scratch_shapes=[pltpu.VMEM((count, width), jnp.float32)],
         ),
         out_shape=[
-            jax.ShapeDtypeStruct((count, inner), jnp.bfloat16),
+            jax.ShapeDtypeStruct((inner, count), jnp.bfloat16),
             jax.ShapeDtypeStruct((count, inner), jnp.bfloat16),
             jax.ShapeDtypeStruct((count, width), jnp.bfloat16),
+            jax.ShapeDtypeStruct((width, count), jnp.bfloat16),
         ],
         compiler_params=pltpu.CompilerParams(vmem_limit_bytes=VMEM_BYTES),
-        cost_estimate=pl.CostEstimate(flops=4 * count * width * inner, bytes_accessed=4 * (width + count) * inner + 4 * count * width, transcendentals=count * inner),
+        cost_estimate=cost(22),
         name="expert_forward",
     )(pick, rows, w_in, w_out)
 
@@ -96,7 +103,6 @@
 def expert_backward(pick, grads, w_in, w_out, slope, tile=512, chunk=256):
     count, width = grads.shape
     inner = w_in.shape[2]
-    if count % chunk: chunk = count
     return pl.pallas_call(
         lambda *refs: expert_backward_kernel(*refs, chunk=chunk),
         grid_spec=pltpu.PrefetchScalarGridSpec(
@@ -119,7 +125,7 @@
             jax.ShapeDtypeStruct((count, width), jnp.bfloat16),
         ],
         compiler_params=pltpu.CompilerParams(vmem_limit_bytes=VMEM_BYTES),
-        cost_estimate=pl.CostEstimate(flops=4 * count * width * inner, bytes_accessed=4 * (width + count) * inner + 4 * count * width, transcendentals=0),
+        cost_estimate=cost(20),
         name="expert_backward",
     )(pick, grads, w_in, w_out, slope)
 
@@ -210,7 +216,7 @@
             jax.ShapeDtypeStruct((2 * pairs, length, length), jnp.bfloat16),
         ],
         compiler_params=pltpu.CompilerParams(vmem_limit_bytes=VMEM_BYTES),
-        cost_estimate=pl.CostEstimate(flops=8 * pairs * 128 * length * length, bytes_accessed=4 * pairs * length * length, transcendentals=2 * pairs * length * length),
+        cost_estimate=cost(17),
         name="attention_forward",
     )(far, qkv_rows, qkv_rows, qkv_rows, near)
 
@@ -276,9 +282,51 @@
         + [jax.ShapeDtypeStruct((2 * pairs, 4, BLOCK, BLOCK), jnp.float32)],
         scratch_shapes=[pltpu.VMEM((length, length), jnp.bfloat16)],
         compiler_params=pltpu.CompilerParams(vmem_limit_bytes=VMEM_BYTES),
-        cost_estimate=pl.CostEstimate(flops=20 * pairs * 128 * length * length, bytes_accessed=4 * pairs * length * length, transcendentals=0),
+        cost_estimate=cost(17),
         name="attention_backward",
     )(qkv_rows, qkv_rows, qkv_rows, grads, probs)
+
+
+def weight_part_kernel(picks, *refs, count, layout):
+    lefts, right, outs = refs[:count], refs[count], refs[count + 1 :]
+    left = jnp.concatenate([ref[...] for ref in lefts], axis=0)
+    whole = dot_f32(left, right[...]).astype(jnp.bfloat16)
+    rows = whole.shape[0] // count
+    part, many = rows // THIRDS, count // 2
+    place = 0
+    for out, pieces in zip(outs, layout):
+        for piece in range(pieces):
+            half, third = divmod(place, THIRDS)
+            for k in range(many):
+                start = (half * many + k) * rows + third * part
+                out[k, piece] = whole[start : start + part]
+            place += 1
+
+
+def weight_part(picks, left, right, rows, layout, tile):
+    depth, width = right.shape
+    count = picks.shape[0]
+    many, part = count // 2, rows // THIRDS
+    if part % 16:
+        whole = jnp.take(left.reshape(-1, rows, depth), picks, axis=0)
+        whole = jnp.einsum("srd,dw->srw", whole, right, preferred_element_type=jnp.float32).astype(jnp.bfloat16)
+        whole = whole.reshape(2, many, THIRDS, part, width).transpose(1, 0, 2, 3, 4).reshape(many, 2 * THIRDS, part, width)
+        starts = [sum(layout[:place]) for place in range(len(layout))]
+        return [whole[:, start : start + pieces] for start, pieces in zip(starts, layout)]
+    return pl.pallas_call(
+        lambda *refs: weight_part_kernel(*refs, count=count, layout=layout),
+        grid_spec=pltpu.PrefetchScalarGridSpec(
+            num_scalar_prefetch=1,
+            grid=(width // tile,),
+            in_specs=[pl.BlockSpec((rows, depth), lambda i, picks, k=k: (picks[k], 0)) for k in range(count)]
+            + [pl.BlockSpec((depth, tile), lambda i, picks: (0, i))],
+            out_specs=[pl.BlockSpec((many, pieces, part, tile), lambda i, picks: (0, 0, 0, i)) for pieces in layout],
+        ),
+        out_shape=[jax.ShapeDtypeStruct((many, pieces, part, width), jnp.bfloat16) for pieces in layout],
+        compiler_params=pltpu.CompilerParams(vmem_limit_bytes=VMEM_BYTES),
+        cost_estimate=cost(5),
+        name="weight_part",
+    )(picks, *([left] * count), right)
 
 
 EPS = 1e-06
@@ -288,32 +336,8 @@
 PAIR = 2
 
 
-def outer_kernel(picks, left, right, *parts):
-    whole = dot_f32(left[...], right[...], TN).astype(jnp.bfloat16)
-    rows = whole.shape[0] // len(parts)
-    for place, part in enumerate(parts):
-        part[0] = whole[place * rows : (place + 1) * rows]
-
-
-def outer_slices(picks, left, right, rows, pieces):
-    depth, width = right.shape
-    count = picks.shape[0]
-    return pl.pallas_call(
-        outer_kernel,
-        grid_spec=pltpu.PrefetchScalarGridSpec(
-            num_scalar_prefetch=1,
-            grid=(count,),
-            in_specs=[
-                pl.BlockSpec((depth, rows), lambda i, picks: (0, picks[i])),
-                pl.BlockSpec((depth, width), lambda i, picks: (0, 0)),
-            ],
-            out_specs=[pl.BlockSpec((1, rows // pieces, width), lambda i, picks: (i, 0, 0))] * pieces,
-        ),
-        out_shape=[jax.ShapeDtypeStruct((count, rows // pieces, width), jnp.bfloat16)] * pieces,
-        compiler_params=pltpu.CompilerParams(vmem_limit_bytes=VMEM_BYTES),
-        cost_estimate=pl.CostEstimate(flops=2 * count * depth * rows * width, bytes_accessed=2 * depth * (count * rows + width) + 2 * count * rows * width, transcendentals=0),
-        name="outer_slices",
-    )(picks, left, right)
+def after(value, *others):
+    return lax.optimization_barrier((value, *others))[0]
 
 
 def bucket_index(offset):
@@ -416,23 +440,37 @@
             value = value + swap(value, mask, 0)
         return value
 
-    def exchange(rows):
-        parts = rows.reshape(sources, capacity, width)
-        got = [parts[0]]
-        for away in range(1, sources):
-            got.append(swap(parts[away], PAIR * (away // groups), away % groups))
-        return jnp.concatenate(got, axis=0)
-
-    def gather_weight(piece, axis):
-        columns = piece.shape[-1] // 2
-        mine = lax.dynamic_slice_in_dim(piece, core * columns, columns, piece.ndim - 1)
-        mine = lax.all_gather(mine, "dp", axis=axis, tiled=True)
-        other = swap(mine, 0, 1)
-        first, second = jnp.where(core == 0, mine, other), jnp.where(core == 0, other, mine)
-        return jnp.concatenate([first, second], axis=-1)
-
-    qkv_full = gather_weight(qkv_weight, 1)
-    out_full = gather_weight(out_weight, 0)
+    near_count = groups
+
+    def across(value, place):
+        return swap(value, PAIR * (place // (groups // 2)), 2 * (place % (groups // 2)))
+
+    def send_out(rows):
+        parts = rows.reshape(2, near_count, capacity, width)
+        got = [across(parts[:, place], place) for place in range(1, near_count)]
+        relay = jnp.stack([parts[1, 0]] + [pair[1] for pair in got])
+        relay = swap(relay, 0, 1)
+        direct = jnp.stack([parts[0, 0]] + [pair[0] for pair in got])
+        return jnp.concatenate([direct, relay]).reshape(slot_count, width)
+
+    def send_back(rows):
+        parts = rows.reshape(2, near_count, capacity, width)
+        relay = swap(parts[1], 0, 1)
+        got = [across(jnp.stack([parts[0, place], relay[place]]), place) for place in range(1, near_count)]
+        return parts[0, 0], relay, got
+
+    def collect(own, relay, got):
+        direct = jnp.stack([own] + [pair[0] for pair in got])
+        relay = jnp.stack([relay[0]] + [pair[1] for pair in got])
+        return jnp.concatenate([direct, relay]).reshape(slot_count, width)
+
+    columns = width // 2
+    mine = lax.dynamic_slice_in_dim(qkv_weight, core * columns, columns, 2)
+    mine = lax.all_gather(mine, "dp", axis=1, tiled=True)
+    out_full = lax.all_gather(after(out_weight, mine), "dp", axis=0, tiled=True)
+    other = swap(mine, 0, 1)
+    first, second = jnp.where(core == 0, mine, other), jnp.where(core == 0, other, mine)
+    qkv_full = jnp.concatenate([first, second], axis=-1)
     valid_rows = valid_mask.astype(f32)[:, None]
     valid_count = all_sum(jnp.broadcast_to(jnp.sum(valid_rows), (8, 128)))[0, 0]
     prefix_len = prefix[0]
@@ -448,7 +486,8 @@
     ).astype(bf16)
     running = jnp.dot(lower_ones, route_hits, preferred_element_type=f32)
     pair_rank = jnp.sum((running - 1.0) * route_hits.astype(f32), axis=1).astype(jnp.int32)
-    away = ((flat_routes % 2) ^ half) * groups + ((flat_routes // 2) ^ here_group)
+    away = (flat_routes // 2) ^ here_group
+    away = ((away % 2) * 2 + ((flat_routes % 2) ^ half)) * (groups // 2) + away // 2
     slot_of_pair = (away * capacity + pair_rank).reshape(length, top_count)
     slot_hot = (
         slot_of_pair[:, :, None] == lax.broadcasted_iota(jnp.int32, (1, 1, slot_count), 2)
@@ -464,10 +503,10 @@
     gate_vals = gate_values(logits, routes)
 
     send_rows = jnp.einsum("tks,td->sd", slot_hot, normed2, preferred_element_type=f32).astype(bf16)
-    rows_in = exchange(send_rows)
+    rows_in = send_out(send_rows)
     pick = half.reshape(1).astype(jnp.int32)
-    hidden, slope, produced = expert_forward(pick, rows_in, w_in, w_out)
-    returned = exchange(produced)
+    hidden_t, slope, produced, rows_t = expert_forward(pick, rows_in, w_in, w_out)
+    returned = collect(*send_back(produced))
     picked = jnp.einsum("tks,sd->tkd", slot_hot, returned, preferred_element_type=f32)
     output = middle + jnp.sum(gate_vals[:, :, None] * picked, axis=1)
     misfit = output - teacher.astype(f32)
@@ -475,69 +514,59 @@
     grad_y = cotangent.astype(f32) + valid_rows * misfit * (total_tokens / valid_count)
     grad_pairs = (gate_vals[:, :, None] * grad_y[:, None, :]).astype(bf16)
     send_grads = jnp.einsum("tks,tkd->sd", slot_hot, grad_pairs, preferred_element_type=f32).astype(bf16)
-    grad_rows = exchange(send_grads)
+    grad_rows = send_out(send_grads)
 
     out_rows = inner // copies
     in_rows = width // copies
     far_bit = here_dp % 2
     slices = jnp.arange(rest, dtype=jnp.int32) * 4
 
-    def owner_slices(other_half, bit0):
-        return (slices + ((half ^ other_half) * 2 + bit0)).astype(jnp.int32)
-
-    def out_units(bit0):
-        units = []
-        for other_half in (1, 0):
-            picks = owner_slices(other_half, bit0)
-            if out_rows % 128 == 0:
-                units += outer_slices(picks, hidden, grad_rows, out_rows, 2)
-            else:
-                part = jnp.take(hidden.reshape(-1, copies, out_rows), picks, axis=1)
-                part = jnp.einsum("rsf,rd->sfd", part, grad_rows, preferred_element_type=f32).astype(bf16)
-                units += [part[:, : out_rows // 2], part[:, out_rows // 2 :]]
-        return units
-
-    def in_units(bit0):
-        rows_t = rows_in.T.reshape(rest, 2, 2, in_rows, slot_count)
-        rows_t = lax.dynamic_index_in_dim(rows_t, bit0, 2, keepdims=False)
-        units = []
-        for other_half in (1, 0):
-            part = lax.dynamic_index_in_dim(rows_t, half ^ other_half, 1, keepdims=False)
-            for piece in range(2):
-                cols = grad_pre[:, piece * (inner // 2) : (piece + 1) * (inner // 2)]
-                units.append(jnp.einsum("sir,rf->sif", part, cols, preferred_element_type=f32).astype(bf16))
-        return units
-
-    send_units = out_units(1 - far_bit)
-    got_units = [swap(unit, 1, 0) for unit in send_units]
-    grad_pre, grad_in_rows = expert_backward(pick, grad_rows, w_in, w_out, slope)
-    sent_back = exchange(grad_in_rows)
-    send_units = in_units(1 - far_bit)
-    got_units += [swap(unit, 1, 0) for unit in send_units]
-    keep_units = out_units(far_bit) + in_units(far_bit)
-
-    reduced = []
-    token = None
-    for got, keep in zip(got_units, keep_units):
-        if token is not None:
-            got, _ = lax.optimization_barrier((got, token))
-        unit = (got.astype(f32) + keep.astype(f32)).astype(bf16)
-        for mask in reversed(bits(copies)[2:]):
-            bit = (here_dp // mask) % 2
-            unit = unit.reshape((2, unit.shape[0] // 2) + unit.shape[1:])
-            away_part = lax.dynamic_index_in_dim(unit, 1 - bit, 0, keepdims=False)
-            stay_part = lax.dynamic_index_in_dim(unit, bit, 0, keepdims=False)
-            token = stay_part
-            unit = (swap(away_part, mask, 0).astype(f32) + stay_part.astype(f32)).astype(bf16)
-        reduced.append(unit[0])
-    final = []
-    for first in (0, 4):
-        theirs = [swap(unit, PAIR, 0) for unit in reduced[first : first + 2]]
-        axis = 0 if first == 0 else 1
-        mine = jnp.concatenate(reduced[first + 2 : first + 4], axis=axis).astype(f32)
-        theirs = jnp.concatenate(theirs, axis=axis).astype(f32)
-        final.append(jnp.stack([jnp.where(half == 0, mine, theirs), jnp.where(half == 0, theirs, mine)]))
-    grad_w_out, grad_w_in = final
+    def pieces_of(left, right, rows, bit0, layout, tile):
+        picks = jnp.concatenate([slices + ((half ^ other_half) * 2 + bit0) for other_half in (1, 0)])
+        return weight_part(picks.astype(jnp.int32), left, right, rows, layout, tile)
+
+    def add(left, right):
+        return (left.astype(f32) + right.astype(f32)).astype(bf16)
+
+    def fold(unit, bit):
+        unit = unit.reshape((2, unit.shape[0] // 2) + unit.shape[1:])
+        away_part = lax.dynamic_index_in_dim(unit, 1 - bit, 0, keepdims=False)
+        return away_part, lax.dynamic_index_in_dim(unit, bit, 0, keepdims=False)
+
+    far_masks = list(reversed(bits(copies)[2:]))
+
+    def near_add(got, keep):
+        away_part, stay_part = fold(add(got, keep), (here_dp // far_masks[0]) % 2)
+        return away_part, stay_part
+
+    def far_trade(away_part):
+        return swap(away_part, far_masks[0], 0)
+
+    def finish(got, stay):
+        unit = add(got, stay)
+        for mask in far_masks[1:]:
+            away_part, stay_part = fold(unit, (here_dp // mask) % 2)
+            unit = add(swap(away_part, mask, 0), stay_part)
+        return unit[0]
+
+    out_layout, in_layout = (2, 3, 1), (2, 1, 1, 2)
+    send_a, send_b, send_c = pieces_of(hidden_t, grad_rows, out_rows, 1 - far_bit, out_layout, width)
+    got_a = swap(send_a, 1, 0)
+    grad_pre, grad_in_rows = expert_backward(pick, after(grad_rows, send_a), w_in, w_out, slope)
+    own, traded, sent_back = send_back(after(grad_in_rows, got_a))
+    got_b = swap(after(send_b, traded), 1, 0)
+    grad_pre = after(grad_pre, traded)
+    send_d, send_e, send_f, send_g = pieces_of(rows_t, grad_pre, in_rows, 1 - far_bit, in_layout, 512)
+    keep_d, keep_e, keep_f, keep_g = pieces_of(rows_t, grad_pre, in_rows, far_bit, in_layout, 512)
+    keep_a, keep_b, keep_c = pieces_of(hidden_t, after(grad_rows, keep_d), out_rows, far_bit, out_layout, width)
+    away_a, stay_a = near_add(got_a, keep_a)
+    far_a = far_trade(away_a)
+    away_b, stay_b = near_add(got_b, keep_b)
+    sent_back = collect(own, traded, [after(pair, away_b) for pair in sent_back])
+    sent_back, send_c, send_d = lax.optimization_barrier((sent_back, send_c, send_d))
+    far_b = far_trade(away_b)
+    got_c = swap(send_c, 1, 0)
+    got_d = swap(send_d, 1, 0)
 
     grad_gates = jnp.sum(grad_y[:, None, :] * picked, axis=-1)
     grad_normed2 = jnp.einsum("tks,sd->td", slot_hot, sent_back, preferred_element_type=f32)
@@ -551,6 +580,27 @@
     grad_attn_proj = grad_middle.astype(bf16)
     grad_attended = jnp.einsum("te,de->td", grad_attn_proj, out_full, preferred_element_type=f32).astype(bf16)
     grad_q, grad_k, grad_v, bands = attention_backward(qkv_rows, grad_attended, probs)
+    grad_q, grad_k, grad_v, got_c, got_d = lax.optimization_barrier((grad_q, grad_k, grad_v, got_c, got_d))
+    done_a = finish(after(far_a, grad_q), stay_a)
+
+    away_c, stay_c = near_add(got_c, keep_c)
+    far_c = far_trade(away_c)
+    away_d, stay_d = near_add(got_d, keep_d)
+    far_d = far_trade(away_d)
+    got_e, got_f, got_g = [swap(after(send, away_d), 1, 0) for send in (send_e, send_f, send_g)]
+    away_e, stay_e = near_add(got_e, keep_e)
+    far_e = far_trade(away_e)
+    away_f, stay_f = near_add(after(got_f, stay_e), keep_f)
+    far_f = far_trade(away_f)
+    away_g, stay_g = near_add(after(got_g, stay_f), keep_g)
+    far_g = far_trade(away_g)
+    done_b = finish(far_b, stay_b)
+    done_c = finish(far_c, stay_c)
+    done_d = finish(far_d, stay_d)
+    done_e = finish(far_e, stay_e)
+    done_f = finish(far_f, stay_f)
+    done_g = finish(far_g, stay_g)
+    due = [(stay_e,), (stay_g, done_b, done_c, done_d), (done_e, done_f), (done_g,)]
 
     def weight_gradient(left, right):
         return jnp.einsum("td,te->de", left, right, preferred_element_type=f32).astype(bf16)
@@ -570,13 +620,10 @@
         bit = (here_group // mask) % 2
         away_part = lax.dynamic_index_in_dim(total, 1 - bit, 0, keepdims=False)
         stay_part = lax.dynamic_index_in_dim(total, bit, 0, keepdims=False)
-        total = (swap(away_part, 0, mask).astype(f32) + stay_part.astype(f32)).astype(bf16)
+        total = add(after(swap(away_part, 0, mask), *(due.pop(0) if due else ())), stay_part)
     for mask in reversed(bits(copies)):
-        bit = (here_dp // mask) % 2
-        total = total.reshape((2, total.shape[0] // 2) + total.shape[1:])
-        away_part = lax.dynamic_index_in_dim(total, 1 - bit, 0, keepdims=False)
-        stay_part = lax.dynamic_index_in_dim(total, bit, 0, keepdims=False)
-        total = (swap(away_part, mask, 0).astype(f32) + stay_part.astype(f32)).astype(bf16)
+        away_part, stay_part = fold(total, (here_dp // mask) % 2)
+        total = add(after(swap(away_part, mask, 0), *(due.pop(0) if due else ())), stay_part)
     total = total[0]
     for mask in reversed(group_bits):
         bit = (here_group // mask) % 2
@@ -594,6 +641,18 @@
     grad_resid_norm, grad_gain_attn = first_back(grad_normed1)
     grad_input = grad_middle + grad_resid_norm
     grad_table = table_gradient(bands, position_bias_table.shape[1])
+
+    out_theirs = swap(jnp.concatenate([done_a, done_b[:1]]), PAIR, 0)
+    out_mine = jnp.concatenate([done_b[1:], done_c])
+    in_theirs = swap(jnp.concatenate([done_d, done_e]), PAIR, 0)
+    in_mine = jnp.concatenate([done_f, done_g])
+
+    def both_experts(mine, theirs):
+        mine, theirs = [part.reshape(-1, part.shape[-1]).astype(f32) for part in (mine, theirs)]
+        return jnp.stack([jnp.where(half == 0, mine, theirs), jnp.where(half == 0, theirs, mine)])
+
+    grad_w_out = both_experts(out_mine, out_theirs)
+    grad_w_in = both_experts(in_mine, in_theirs)
 
     def sum_many(values):
         flat = jnp.concatenate([value.reshape(-1) for value in values])
@@ -606,8 +665,9 @@
             place += value.size
         return done
 
-    grad_gain_moe, grad_router, square_total = sum_many((grad_gain_moe, grad_router, square_sum))
-    grad_gain_attn, grad_table = sum_many((grad_gain_attn, grad_table))
+    grad_gain_moe, grad_router, square_total, grad_gain_attn, grad_table = sum_many(
+        (grad_gain_moe, grad_router, square_sum, grad_gain_attn, grad_table)
+    )
     distill_loss = square_total / (width * valid_count)
     return (
         output.astype(bf16),

time: 594 us -> 544 us (0.916)
  blocking collectives: 33.5 us -> 0 us
  starting transfers between devices: 75 us -> 48.3 us
  matrix products: 69.8 us -> 49.5 us
  Pallas kernels: 99.2 us -> 112 us
  local copies, waits for them, and re-layouts: 46 us -> 54.4 us
  other arithmetic: 40.4 us -> 47.3 us
    all_gather x1 -> x2, waiting for transfers between devices: 0.14 us -> 52.9 us  [the longest x1 36 us: on_device(): mine = lax.all_gather(mine, 'dp', axis=1, tiled=True)]
    ppermute x72 -> x50, waiting for transfers between devices: 202 us -> 153 us  [swap(): return lax.ppermute(value, AXES, pairs)]
    all_gather x1 -> x0, blocking collectives: 33.5 us -> none  [gather_weight(): mine = lax.all_gather(mine, 'dp', axis=axis, tiled=True)]
    ppermute x72 -> x50, starting transfers between devices: 75 us -> 48.2 us  [swap(): return lax.ppermute(value, AXES, pairs)]
    dot_general x8 -> x0, matrix products: 20.3 us -> none  [in_units(): jnp.einsum('sir,rf->sif', part, cols, preferred_element_type=f32)]
    pallas_call x4, Pallas kernels: 21.5 us -> 33.4 us  [weight_part(): pl.pallas_call(lambda *refs: weight_part_kernel(*refs, count=count, layou...]
    unnamed x213 -> x183, local copies, waits for them, and re-layouts: 22.5 us -> 19.6 us
  transfers between devices with their start and end apart: 73 -> 52, of which waited for: 31 -> 28; matrix products, arithmetic and copies ran while one was open for 19% -> 22% of each run, Pallas kernels for 5% -> 19%
where the time goes in v2:
time: 544 us; the launch traced here: 538 us
  waiting for transfers between devices  206 us (38%)
  Pallas kernels  112 us (21%)
  local copies, waits for them, and re-layouts  54.4 us (10%)
  matrix products  49.5 us (9%)
  starting transfers between devices  48.3 us (9%)
  other arithmetic  47.3 us (9%)
  between operations  19.9 us (4%)
    ppermute x50, waiting for transfers between devices, swap(): return lax.ppermute(value, AXES, pairs)  153 us
    ppermute x50, starting transfers between devices, swap(): return lax.ppermute(value, AXES, pairs)  48.2 us
    all_gather x1, waiting for transfers between devices, on_device(): mine = lax.all_gather(mine, 'dp', axis=1, tiled=True)  36 us
    pallas_call x4, Pallas kernels, weight_part(): pl.pallas_call(lambda *refs: weight_part_kernel(*refs, count=count, layou...  33.4 us
    pallas_call x1, Pallas kernels, expert_forward(): pl.pallas_call(lambda *refs: expert_forward_kernel(*refs, chunk=chunk), g...  24.3 us
    pallas_call x1, Pallas kernels, expert_backward(): pl.pallas_call(lambda *refs: expert_backward_kernel(*refs, chunk=chunk),...  20.8 us
    unnamed x183, local copies, waits for them, and re-layouts  19.6 us
    pallas_call x1, Pallas kernels, attention_backward(): pl.pallas_call(lambda *refs: attention_backward_kernel(*refs, heads=64, b...  17.3 us
  transfers between devices with their start and end apart: 52, of which 28 were waited for; matrix products, arithmetic and copies ran while one was open for 22% of the time, Pallas kernels for 19%

profile of v2, /device:TPU:0, one launch (start us, length us, event | category | flops | bytes accessed | tf_op | source)
XLA Modules:
  0.0 537.7 jit_solution(11118795694732412265)
XLA Ops:
  23.5 36.0 %all-gather.3.cloned.1.call-done = bf16[3,768,384]{2,1,0:T(8,128)(2,1)} async-done(((bf16[3,96,384]{2,1,0:T(8,128)(2,1)}), bf16[3,768,384]{2,1,0:T(8,128)(2,1)}) %all-gather.3.cloned.1.call-update) | async-done | bytes 1769488 | tf_op jit(solution)/shard_map/all_gather | solution.py:469
  75.2 3.5 convert_bitcast_fusion.refs_1_.refs_2_.refs_3_.refs_0_
  78.7 16.5 %attention_forward.1 = (bf16[512,768]{1,0:T(8,128)(2,1)}, bf16[12,512,512]{2,1,0:T(8,128)(2,1)}) custom-call(f32[12]{0:T(128)} %slice_reduce_fusion.refs_0_, bf16[3,512,768]{2,1,0:T(8,128)(2,1)} %convert_bitcast_fusion.refs_1_.refs_2_.refs_3_.refs_0_, bf16[3,512,768]{2,1,0:T(8,128)(2,1)} %convert_bitcast_fusion.refs_1_.refs_2_.refs_3_.refs_0_, ...), custom_call_target="tpu_custom_call" | custom-call | flops 18699999232 | tf_op jit(solution)/shard_map/attention_forward/pallas_call | solution.py:198
  95.3 16.9 %all-gather.5.cloned.1.call-done = bf16[768,768]{1,0:T(8,128)(2,1)} async-done(((bf16[96,768]{1,0:T(8,128)(2,1)}), bf16[768,768]{1,0:T(8,128)(2,1)}) %all-gather.5.cloned.1.call-update) | async-done | bytes 1179664 | tf_op jit(solution)/shard_map/all_gather | solution.py:470
  121.0 9.3 %collective-permute-done.1 = bf16[2,160,768]{2,1,0:T(8,128)(2,1)S(1)} collective-permute-done((bf16[2,160,768]{2,1,0:T(8,128)(2,1)S(1)}, bf16[2,160,768]{2,1,0:T(8,128)(2,1)S(1)}, u32[]{:S(2)}, u32[]{:S(2)}) %collective-permute-start.1) | collective-permute-done | bytes 491552 | tf_op jit(solution)/shard_map/ppermute | solution.py:431
  133.1 7.8 %collective-permute-done.3 = bf16[2,160,768]{2,1,0:T(8,128)(2,1)S(1)} collective-permute-done((bf16[2,160,768]{2,1,0:T(8,128)(2,1)S(1)}, bf16[2,160,768]{2,1,0:T(8,128)(2,1)S(1)}, u32[]{:S(2)}, u32[]{:S(2)}) %collective-permute-start.3) | collective-permute-done | bytes 491552 | tf_op jit(solution)/shard_map/ppermute | solution.py:431
  148.0 3.1 collective-permute-done.11
  158.8 24.3 %expert_forward.1 = (bf16[3072,1280]{1,0:T(8,128)(2,1)}, bf16[1280,3072]{1,0:T(8,128)(2,1)}, bf16[1280,768]{1,0:T(8,128)(2,1)}, bf16[768,1280]{1,0:T(8,128)(2,1)}) custom-call(s32[1]{0:T(128)} %bitcast.17.refs_0_, bf16[1280,768]{1,0:T(8,128)(2,1)} %bitcast.263, bf16[2,768,3072]{2,1,0:T(8,128)(2,1)} %refs_2_.3, bf16[2,3072,768]{2,1,0:T(8,128)(2,1)} %refs_3_.3), custom_call_target="tpu_custom_call" | custom-call | flops 24199999488 | tf_op jit(solution)/shard_map/expert_forward/pallas_call | solution.py:54
  191.2 9.9 %collective-permute-done.6 = bf16[2,160,768]{2,1,0:T(8,128)(2,1)S(1)} collective-permute-done((bf16[2,160,768]{2,1,0:T(8,128)(2,1)S(1)}, bf16[2,160,768]{2,1,0:T(8,128)(2,1)S(1)}, u32[]{:S(2)}, u32[]{:S(2)}) %collective-permute-start.6) | collective-permute-done | bytes 491552 | tf_op jit(solution)/shard_map/ppermute | solution.py:431
  203.1 9.8 %collective-permute-done.8 = bf16[2,160,768]{2,1,0:T(8,128)(2,1)S(1)} collective-permute-done((bf16[2,160,768]{2,1,0:T(8,128)(2,1)S(1)}, bf16[2,160,768]{2,1,0:T(8,128)(2,1)S(1)}, u32[]{:S(2)}, u32[]{:S(2)}) %collective-permute-start.8) | collective-permute-done | bytes 491552 | tf_op jit(solution)/shard_map/ppermute | solution.py:431
  213.0 4.4 multiply_reduce_fusion.1
  219.0 3.8 bitcast_convert_fusion
  232.1 6.1 %collective-permute-done.14 = bf16[2,160,768]{2,1,0:T(8,128)(2,1)} collective-permute-done((bf16[2,160,768]{2,1,0:T(8,128)(2,1)}, bf16[2,160,768]{2,1,0:T(8,128)(2,1)}, u32[]{:S(2)}, u32[]{:S(2)}) %collective-permute-start.14) | collective-permute-done | bytes 491552 | tf_op jit(solution)/shard_map/ppermute | solution.py:431
  239.2 3.2 collective-permute-done.15
  242.5 8.5 %collective-permute-done.16 = bf16[2,160,768]{2,1,0:T(8,128)(2,1)S(1)} collective-permute-done((bf16[2,160,768]{2,1,0:T(8,128)(2,1)}, bf16[2,160,768]{2,1,0:T(8,128)(2,1)S(1)}, u32[]{:S(2)}, u32[]{:S(2)}) %collective-permute-start.16) | collective-permute-done | bytes 491552 | tf_op jit(solution)/shard_map/ppermute | solution.py:431
  255.2 7.8 %weight_part.4 = (bf16[2,2,128,768]{3,2,1,0:T(8,128)(2,1)}, bf16[2,3,128,768]{3,2,1,0:T(8,128)(2,1)}, bf16[2,1,128,768]{3,2,1,0:T(8,128)(2,1)}) custom-call(s32[4]{0:T(128)} %pad_add_fusion.1.refs_0_, bf16[3072,1280]{1,0:T(8,128)(2,1)} %get-tuple-element.67.refs_1_.refs_2_.refs_3_.refs_4_, ...), custom_call_target="tpu_custom_call" | custom-call | flops 5500000256 | tf_op jit(solution)/shard_map/weight_part/pallas_call | solution.py:316
  263.5 20.8 %expert_backward.1 = (bf16[1280,3072]{1,0:T(8,128)(2,1)}, bf16[1280,768]{1,0:T(8,128)(2,1)}) custom-call(s32[1]{0:T(128)} %bitcast.17.refs_0_, bf16[1280,768]{1,0:T(8,128)(2,1)} %bitcast.239, bf16[2,768,3072]{2,1,0:T(8,128)(2,1)} %refs_2_.3, bf16[2,3072,768]{2,1,0:T(8,128)(2,1)} %refs_3_.3, bf16[1280,3072]{1,0:T(8,128)(2,1)} %get-tuple-element.70.refs_4_), custom_call_target="tpu_custom_call" | custom-call | flops 22000001024 | tf_op jit(solution)/shard_map/expert_backward/pallas_call | solution.py:106
  300.1 8.7 %weight_part.5 = (bf16[2,2,32,3072]{3,2,1,0:T(8,128)(2,1)}, bf16[2,1,32,3072]{3,2,1,0:T(8,128)(2,1)}, bf16[2,1,32,3072]{3,2,1,0:T(8,128)(2,1)}, bf16[2,2,32,3072]{3,2,1,0:T(8,128)(2,1)}) custom-call(s32[4]{0:T(128)} %pad_add_fusion.2.refs_0_, bf16[768,1280]{1,0:T(8,128)(2,1)} %get-tuple-element.75.refs_1_.refs_2_.refs_3_.refs_4_, ...), custom_call_target="tpu_custom_call" | custom-call | flops 5500000256 | tf_op jit(solution)/shard_map/weight_part/pallas_call | solution.py:316
  308.9 7.9 %weight_part.6 = (bf16[2,2,128,768]{3,2,1,0:T(8,128)(2,1)}, bf16[2,3,128,768]{3,2,1,0:T(8,128)(2,1)}, bf16[2,1,128,768]{3,2,1,0:T(8,128)(2,1)}) custom-call(s32[4]{0:T(128)} %pad_add_fusion.2.refs_0_, bf16[3072,1280]{1,0:T(8,128)(2,1)} %get-tuple-element.67.refs_1_.refs_2_.refs_3_.refs_4_, ...), custom_call_target="tpu_custom_call" | custom-call | flops 5500000256 | tf_op jit(solution)/shard_map/weight_part/pallas_call | solution.py:316
  318.1 8.9 %weight_part.7 = (bf16[2,2,32,3072]{3,2,1,0:T(8,128)(2,1)}, bf16[2,1,32,3072]{3,2,1,0:T(8,128)(2,1)}, bf16[2,1,32,3072]{3,2,1,0:T(8,128)(2,1)}, bf16[2,2,32,3072]{3,2,1,0:T(8,128)(2,1)}) custom-call(s32[4]{0:T(128)} %pad_add_fusion.1.refs_0_, bf16[768,1280]{1,0:T(8,128)(2,1)} %get-tuple-element.75.refs_1_.refs_2_.refs_3_.refs_4_, ...), custom_call_target="tpu_custom_call" | custom-call | flops 5500000256 | tf_op jit(solution)/shard_map/weight_part/pallas_call | solution.py:316
  344.6 17.3 %attention_backward.1 = (bf16[512,768]{1,0:T(8,128)(2,1)}, bf16[512,768]{1,0:T(8,128)(2,1)}, bf16[512,768]{1,0:T(8,128)(2,1)}, f32[12,4,128,128]{3,2,1,0:T(8,128)}) custom-call(bf16[3,512,768]{2,1,0:T(8,128)(2,1)} %convert_bitcast_fusion.refs_1_.refs_2_.refs_3_.refs_0_, bf16[3,512,768]{2,1,0:T(8,128)(2,1)} %convert_bitcast_fusion.refs_1_.refs_2_.refs_3_.refs_0_, ...), custom_call_target="tpu_custom_call" | custom-call | flops 18699999232 | tf_op jit(solution)/shard_map/attention_backward/pallas_call | solution.py:276
  362.0 7.2 %fusion.51 = f32[12,32]{1,0:T(8,128)S(1)} fusion(s32[4,128,128]{2,1,0:T(8,128)S(1)} %copy-done.35, f32[12,4,128,128]{3,2,1,0:T(8,128)} %get-tuple-element.96), kind=kOutput, calls=%fused_computation.108 | convolution fusion | flops 304087040 | bytes 3409408 | tf_op jit(solution)/shard_map/hdxy,dxyb->hb/dot_general | solution.py:387
  376.0 5.3 collective-permute-done.24
  403.3 3.0 pad_maximum_fusion.1
  421.8 3.6 collective-permute-done.39
  430.1 10.8 %collective-permute-done.40 = bf16[1,1,32,3072]{3,2,1,0:T(8,128)(2,1)S(1)} collective-permute-done((bf16[1,1,32,3072]{3,2,1,0:T(8,128)(2,1)S(1)}, bf16[1,1,32,3072]{3,2,1,0:T(8,128)(2,1)S(1)}, u32[]{:S(2)}, u32[]{:S(2)}) %collective-permute-start.40) | collective-permute-done | bytes 196640 | tf_op jit(solution)/shard_map/ppermute | solution.py:431
  441.6 3.1 collective-permute-done.34
  448.5 15.1 %collective-permute-done.42 = bf16[1,2,32,3072]{3,2,1,0:T(8,128)(2,1)S(1)} collective-permute-done((bf16[1,2,32,3072]{3,2,1,0:T(8,128)(2,1)S(1)}, bf16[1,2,32,3072]{3,2,1,0:T(8,128)(2,1)S(1)}, u32[]{:S(2)}, u32[]{:S(2)}) %collective-permute-start.42) | collective-permute-done | bytes 393248 | tf_op jit(solution)/shard_map/ppermute | solution.py:431
  464.5 8.4 %collective-permute-done.33 = bf16[8,96,768]{2,1,0:T(8,128)(2,1)S(1)} collective-permute-done((bf16[8,96,768]{2,1,0:T(8,128)(2,1)S(1)}, bf16[8,96,768]{2,1,0:T(8,128)(2,1)S(1)}, u32[]{:S(2)}, u32[]{:S(2)}) %collective-permute-start.33) | collective-permute-done | bytes 1179680 | tf_op jit(solution)/shard_map/ppermute | solution.py:431
  484.6 17.9 %collective-permute-done.38 = bf16[4,96,768]{2,1,0:T(8,128)(2,1)} collective-permute-done((bf16[4,96,768]{2,1,0:T(8,128)(2,1)}, bf16[4,96,768]{2,1,0:T(8,128)(2,1)}, u32[]{:S(2)}, u32[]{:S(2)}) %collective-permute-start.38) | collective-permute-done | bytes 589856 | tf_op jit(solution)/shard_map/ppermute | solution.py:431
  505.1 10.0 %collective-permute-done.41 = bf16[2,96,768]{2,1,0:T(8,128)(2,1)S(1)} collective-permute-done((bf16[2,96,768]{2,1,0:T(8,128)(2,1)S(1)}, bf16[2,96,768]{2,1,0:T(8,128)(2,1)S(1)}, u32[]{:S(2)}, u32[]{:S(2)}) %collective-permute-start.41) | collective-permute-done | bytes 294944 | tf_op jit(solution)/shard_map/ppermute | solution.py:431
  522.3 3.4 collective-permute-done.44
  (446 shorter events, 195.5 us)
Async XLA Ops:
  7.2 52.3 %all-gather.3.cloned.1.call-start = ((), (), s32[]{:S(2)}) async-start(), calls=%async_computation | async-start | bytes 1990656 | tf_op jit(solution)/shard_map/all_gather | solution.py:469
  9.3 133.2 %collective-permute-start.9 = (f32[8,128]{1,0:T(8,128)S(1)}, f32[8,128]{1,0:T(8,128)S(1)}, u32[]{:S(2)}, u32[]{:S(2)}) collective-permute-start(f32[8,128]{1,0:T(8,128)S(1)} %broadcast_in_dim.118), channel_id=1, source_target_pairs={{0,1},{1,0},{2,3},{3,2},{4,5},{5,4},{6,7},{7,6},{8,9},{9,8},{10,11... | collective-permute-start | bytes 12296 | tf_op jit(solution)/shard_map/ppermute | solution.py:431
  10.5 101.6 %all-gather.5.cloned.1.call-start = ((), (), s32[]{:S(2)}) async-start(), calls=%async_computation.1 | async-start | bytes 1327104 | tf_op jit(solution)/shard_map/all_gather | solution.py:470
  118.8 14.2 %collective-permute-start.2 = (bf16[2,160,768]{2,1,0:T(8,128)(2,1)S(1)}, bf16[2,160,768]{2,1,0:T(8,128)(2,1)S(1)}, u32[]{:S(2)}, u32[]{:S(2)}) collective-permute-start(bf16[2,160,768]{2,1,0:T(8,128)(2,1)S(1)} %get-tuple-element.176), channel_id=1, source_target_pairs={{0,8},{1,9},{2,10},{3,11},{4,12},{5,13},{6,14},{7,15},{8,0},{9,1},... | collective-permute-start | bytes 1474568 | tf_op jit(solution)/shard_map/ppermute | solution.py:431
  119.9 21.0 %collective-permute-start.3 = (bf16[2,160,768]{2,1,0:T(8,128)(2,1)S(1)}, bf16[2,160,768]{2,1,0:T(8,128)(2,1)S(1)}, u32[]{:S(2)}, u32[]{:S(2)}) collective-permute-start(bf16[2,160,768]{2,1,0:T(8,128)(2,1)S(1)} %get-tuple-element.175), channel_id=1, source_target_pairs={{0,10},{1,11},{2,8},{3,9},{4,14},{5,15},{6,12},{7,13},{8,2},{9,3},... | collective-permute-start | bytes 1474568 | tf_op jit(solution)/shard_map/ppermute | solution.py:431
  142.3 14.3 %collective-permute-start.4 = (bf16[4,160,768]{2,1,0:T(8,128)(2,1)S(1)}, bf16[4,160,768]{2,1,0:T(8,128)(2,1)}, u32[]{:S(2)}, u32[]{:S(2)}) collective-permute-start(bf16[4,160,768]{2,1,0:T(8,128)(2,1)S(1)} %pad_maximum_fusion.7), channel_id=1, source_target_pairs={{0,1},{1,0},{2,3},{3,2},{4,5},{5,4},{6,7},{7,6},{8,9},{9,8},{10,11... | collective-permute-start | bytes 2949128 | tf_op jit(solution)/shard_map/ppermute | solution.py:431
  154.7 30.5 %collective-permute-start.13 = (f32[8,128]{1,0:T(8,128)S(1)}, f32[8,128]{1,0:T(8,128)S(1)}, u32[]{:S(2)}, u32[]{:S(2)}) collective-permute-start(f32[8,128]{1,0:T(8,128)S(1)} %add.881), channel_id=1, source_target_pairs={{0,16},{1,17},{2,18},{3,19},{4,20},{5,21},{6,22},{7,23},{8,24},{9,... | collective-permute-start | bytes 12296 | tf_op jit(solution)/shard_map/ppermute | solution.py:431
  187.4 13.6 %collective-permute-start.6 = (bf16[2,160,768]{2,1,0:T(8,128)(2,1)S(1)}, bf16[2,160,768]{2,1,0:T(8,128)(2,1)S(1)}, u32[]{:S(2)}, u32[]{:S(2)}) collective-permute-start(bf16[2,160,768]{2,1,0:T(8,128)(2,1)S(1)} %pad_maximum_fusion.13), channel_id=1, source_target_pairs={{0,2},{1,3},{2,0},{3,1},{4,6},{5,7},{6,4},{7,5},{8,10},{9,11},{10,... | collective-permute-start | bytes 1474568 | tf_op jit(solution)/shard_map/ppermute | solution.py:431
  189.0 14.1 %collective-permute-start.7 = (bf16[2,160,768]{2,1,0:T(8,128)(2,1)S(1)}, bf16[2,160,768]{2,1,0:T(8,128)(2,1)S(1)}, u32[]{:S(2)}, u32[]{:S(2)}) collective-permute-start(bf16[2,160,768]{2,1,0:T(8,128)(2,1)S(1)} %pad_maximum_fusion.14), channel_id=1, source_target_pairs={{0,8},{1,9},{2,10},{3,11},{4,12},{5,13},{6,14},{7,15},{8,0},{9,1},... | collective-permute-start | bytes 1474568 | tf_op jit(solution)/shard_map/ppermute | solution.py:431
  189.9 23.0 %collective-permute-start.8 = (bf16[2,160,768]{2,1,0:T(8,128)(2,1)S(1)}, bf16[2,160,768]{2,1,0:T(8,128)(2,1)S(1)}, u32[]{:S(2)}, u32[]{:S(2)}) collective-permute-start(bf16[2,160,768]{2,1,0:T(8,128)(2,1)S(1)} %pad_maximum_fusion.15), channel_id=1, source_target_pairs={{0,10},{1,11},{2,8},{3,9},{4,14},{5,15},{6,12},{7,13},{8,2},{9,3},... | collective-permute-start | bytes 1474568 | tf_op jit(solution)/shard_map/ppermute | solution.py:431
  228.0 14.4 %collective-permute-start.15 = (bf16[2,160,768]{2,1,0:T(8,128)(2,1)}, bf16[2,160,768]{2,1,0:T(8,128)(2,1)S(1)}, u32[]{:S(2)}, u32[]{:S(2)}) collective-permute-start(bf16[2,160,768]{2,1,0:T(8,128)(2,1)} %get-tuple-element.170), channel_id=1, source_target_pairs={{0,8},{1,9},{2,10},{3,11},{4,12},{5,13},{6,14},{7,15},{8,0},{9,1},... | collective-permute-start | bytes 1474568 | tf_op jit(solution)/shard_map/ppermute | solution.py:431
  229.8 21.2 %collective-permute-start.16 = (bf16[2,160,768]{2,1,0:T(8,128)(2,1)}, bf16[2,160,768]{2,1,0:T(8,128)(2,1)S(1)}, u32[]{:S(2)}, u32[]{:S(2)}) collective-permute-start(bf16[2,160,768]{2,1,0:T(8,128)(2,1)} %get-tuple-element.169), channel_id=1, source_target_pairs={{0,10},{1,11},{2,8},{3,9},{4,14},{5,15},{6,12},{7,13},{8,2},{9,3},... | collective-permute-start | bytes 1474568 | tf_op jit(solution)/shard_map/ppermute | solution.py:431
  263.0 21.4 %collective-permute-start.18 = (bf16[2,2,128,768]{3,2,1,0:T(8,128)(2,1)}, bf16[2,2,128,768]{3,2,1,0:T(8,128)(2,1)S(1)}, u32[]{:S(2)}, u32[]{:S(2)}) collective-permute-start(bf16[2,2,128,768]{3,2,1,0:T(8,128)(2,1)} %get-tuple-element.68), channel_id=1, source_target_pairs={{0,4},{1,5},{2,6},{3,7},{4,0},{5,1},{6,2},{7,3},{8,12},{9,13},{10,... | collective-permute-start | bytes 2359304 | tf_op jit(solution)/shard_map/ppermute | solution.py:431
  293.5 38.5 %collective-permute-start.20 = (bf16[2,160,768]{2,1,0:T(8,128)(2,1)}, bf16[2,160,768]{2,1,0:T(8,128)(2,1)S(1)}, u32[]{:S(2)}, u32[]{:S(2)}) collective-permute-start(bf16[2,160,768]{2,1,0:T(8,128)(2,1)} %pad_maximum_fusion.16), channel_id=1, source_target_pairs={{0,2},{1,3},{2,0},{3,1},{4,6},{5,7},{6,4},{7,5},{8,10},{9,11},{10,... | collective-permute-start | bytes 1474568 | tf_op jit(solution)/shard_map/ppermute | solution.py:431
  295.7 36.2 %collective-permute-start.22 = (bf16[2,160,768]{2,1,0:T(8,128)(2,1)}, bf16[2,160,768]{2,1,0:T(8,128)(2,1)}, u32[]{:S(2)}, u32[]{:S(2)}) collective-permute-start(bf16[2,160,768]{2,1,0:T(8,128)(2,1)} %pad_maximum_fusion.17), channel_id=1, source_target_pairs={{0,8},{1,9},{2,10},{3,11},{4,12},{5,13},{6,14},{7,15},{8,0},{9,1},... | collective-permute-start | bytes 1474568 | tf_op jit(solution)/shard_map/ppermute | solution.py:431
  297.5 34.5 %collective-permute-start.23 = (bf16[2,160,768]{2,1,0:T(8,128)(2,1)}, bf16[2,160,768]{2,1,0:T(8,128)(2,1)}, u32[]{:S(2)}, u32[]{:S(2)}) collective-permute-start(bf16[2,160,768]{2,1,0:T(8,128)(2,1)} %pad_maximum_fusion.18), channel_id=1, source_target_pairs={{0,10},{1,11},{2,8},{3,9},{4,14},{5,15},{6,12},{7,13},{8,2},{9,3},... | collective-permute-start | bytes 1474568 | tf_op jit(solution)/shard_map/ppermute | solution.py:431
  298.6 30.3 %collective-permute-start.21 = (bf16[2,3,128,768]{3,2,1,0:T(8,128)(2,1)}, bf16[2,3,128,768]{3,2,1,0:T(8,128)(2,1)S(1)}, u32[]{:S(2)}, u32[]{:S(2)}) collective-permute-start(bf16[2,3,128,768]{3,2,1,0:T(8,128)(2,1)} %get-tuple-element.74), channel_id=1, source_target_pairs={{0,4},{1,5},{2,6},{3,7},{4,0},{5,1},{6,2},{7,3},{8,12},{9,13},{10,... | collective-permute-start | bytes 3538952 | tf_op jit(solution)/shard_map/ppermute | solution.py:431
  327.8 61.1 %collective-permute-start.48 = (bf16[1,2,128,768]{3,2,1,0:T(8,128)(2,1)}, bf16[1,2,128,768]{3,2,1,0:T(8,128)(2,1)}, u32[]{:S(2)}, u32[]{:S(2)}) collective-permute-start(bf16[1,2,128,768]{3,2,1,0:T(8,128)(2,1)} %constant_dynamic-slice_fusion), channel_id=1, source_target_pairs={{0,16},{1,17},{2,18},{3,19},{4,20},{5,21},{6,22},{7,23},{8,24},{9,... | collective-permute-start | bytes 1179656 | tf_op jit(solution)/shard_map/ppermute | solution.py:431
  330.1 43.0 %collective-permute-start.47 = (bf16[1,3,128,768]{3,2,1,0:T(8,128)(2,1)}, bf16[1,3,128,768]{3,2,1,0:T(8,128)(2,1)}, u32[]{:S(2)}, u32[]{:S(2)}) collective-permute-start(bf16[1,3,128,768]{3,2,1,0:T(8,128)(2,1)} %constant_dynamic-slice_fusion.10), channel_id=1, source_target_pairs={{0,16},{1,17},{2,18},{3,19},{4,20},{5,21},{6,22},{7,23},{8,24},{9,... | collective-permute-start | bytes 1769480 | tf_op jit(solution)/shard_map/ppermute | solution.py:431
  341.0 40.3 %collective-permute-start.25 = (bf16[2,2,32,3072]{3,2,1,0:T(8,128)(2,1)}, bf16[2,2,32,3072]{3,2,1,0:T(8,128)(2,1)}, u32[]{:S(2)}, u32[]{:S(2)}) collective-permute-start(bf16[2,2,32,3072]{3,2,1,0:T(8,128)(2,1)} %get-tuple-element.92), channel_id=1, source_target_pairs={{0,4},{1,5},{2,6},{3,7},{4,0},{5,1},{6,2},{7,3},{8,12},{9,13},{10,... | collective-permute-start | bytes 2359304 | tf_op jit(solution)/shard_map/ppermute | solution.py:431
  389.9 38.4 %collective-permute-start.36 = (bf16[1,1,128,768]{3,2,1,0:T(8,128)(2,1)}, bf16[1,1,128,768]{3,2,1,0:T(8,128)(2,1)}, u32[]{:S(2)}, u32[]{:S(2)}) collective-permute-start(bf16[1,1,128,768]{3,2,1,0:T(8,128)(2,1)} %constant_dynamic-slice_fusion.5), channel_id=1, source_target_pairs={{0,16},{1,17},{2,18},{3,19},{4,20},{5,21},{6,22},{7,23},{8,24},{9,... | collective-permute-start | bytes 589832 | tf_op jit(solution)/shard_map/ppermute | solution.py:431
  391.7 55.8 %collective-permute-start.37 = (bf16[1,2,32,3072]{3,2,1,0:T(8,128)(2,1)}, bf16[1,2,32,3072]{3,2,1,0:T(8,128)(2,1)}, u32[]{:S(2)}, u32[]{:S(2)}) collective-permute-start(bf16[1,2,32,3072]{3,2,1,0:T(8,128)(2,1)} %constant_dynamic-slice_fusion.9), channel_id=1, source_target_pairs={{0,16},{1,17},{2,18},{3,19},{4,20},{5,21},{6,22},{7,23},{8,24},{9,... | collective-permute-start | bytes 1179656 | tf_op jit(solution)/shard_map/ppermute | solution.py:431
  393.6 19.3 %collective-permute-start.32 = (bf16[2,1,32,3072]{3,2,1,0:T(8,128)(2,1)}, bf16[2,1,32,3072]{3,2,1,0:T(8,128)(2,1)}, u32[]{:S(2)}, u32[]{:S(2)}) collective-permute-start(bf16[2,1,32,3072]{3,2,1,0:T(8,128)(2,1)} %get-tuple-element.99), channel_id=1, source_target_pairs={{0,4},{1,5},{2,6},{3,7},{4,0},{5,1},{6,2},{7,3},{8,12},{9,13},{10,... | collective-permute-start | bytes 1179656 | tf_op jit(solution)/shard_map/ppermute | solution.py:431
  395.0 32.2 %collective-permute-start.35 = (bf16[2,1,32,3072]{3,2,1,0:T(8,128)(2,1)}, bf16[2,1,32,3072]{3,2,1,0:T(8,128)(2,1)}, u32[]{:S(2)}, u32[]{:S(2)}) collective-permute-start(bf16[2,1,32,3072]{3,2,1,0:T(8,128)(2,1)} %get-tuple-element.105), channel_id=1, source_target_pairs={{0,4},{1,5},{2,6},{3,7},{4,0},{5,1},{6,2},{7,3},{8,12},{9,13},{10,... | collective-permute-start | bytes 1179656 | tf_op jit(solution)/shard_map/ppermute | solution.py:431
  419.6 84.2 %collective-permute-start.49 = (bf16[3,128,768]{2,1,0:T(8,128)(2,1)}, bf16[3,128,768]{2,1,0:T(8,128)(2,1)}, u32[]{:S(2)}, u32[]{:S(2)}) collective-permute-start(bf16[3,128,768]{2,1,0:T(8,128)(2,1)} %pad_maximum_fusion.12), channel_id=1, source_target_pairs={{0,8},{1,9},{2,10},{3,11},{4,12},{5,13},{6,14},{7,15},{8,0},{9,1},... | collective-permute-start | bytes 1769480 | tf_op jit(solution)/shard_map/ppermute | solution.py:431
  425.4 19.4 %collective-permute-start.34 = (bf16[2,2,32,3072]{3,2,1,0:T(8,128)(2,1)S(1)}, bf16[2,2,32,3072]{3,2,1,0:T(8,128)(2,1)S(1)}, u32[]{:S(2)}, u32[]{:S(2)}) collective-permute-start(bf16[2,2,32,3072]{3,2,1,0:T(8,128)(2,1)S(1)} %copy-done.80), channel_id=1, source_target_pairs={{0,4},{1,5},{2,6},{3,7},{4,0},{5,1},{6,2},{7,3},{8,12},{9,13},{10,... | collective-permute-start | bytes 2359304 | tf_op jit(solution)/shard_map/ppermute | solution.py:431
  427.2 17.9 %collective-permute-start.31 = (bf16[2,8,96,768]{3,2,1,0:T(8,128)(2,1)S(1)}, bf16[2,8,96,768]{3,2,1,0:T(8,128)(2,1)S(1)}, u32[]{:S(2)}, u32[]{:S(2)}) collective-permute-start(bf16[2,8,96,768]{3,2,1,0:T(8,128)(2,1)S(1)} %dynamic-slice_bitcast_fusion), channel_id=1, source_target_pairs={{0,1},{1,0},{2,3},{3,2},{4,5},{5,4},{6,7},{7,6},{8,9},{9,8},{10,11... | collective-permute-start | bytes 7077896 | tf_op jit(solution)/shard_map/ppermute | solution.py:431
  440.9 38.4 %collective-permute-start.30 = (f32[64,128]{1,0:T(8,128)S(1)}, f32[64,128]{1,0:T(8,128)S(1)}, u32[]{:S(2)}, u32[]{:S(2)}) collective-permute-start(f32[64,128]{1,0:T(8,128)S(1)} %add.933), channel_id=1, source_target_pairs={{0,16},{1,17},{2,18},{3,19},{4,20},{5,21},{6,22},{7,23},{8,24},{9,... | collective-permute-start | bytes 98312 | tf_op jit(solution)/shard_map/ppermute | solution.py:431
  445.0 18.6 %collective-permute-start.42 = (bf16[1,2,32,3072]{3,2,1,0:T(8,128)(2,1)S(1)}, bf16[1,2,32,3072]{3,2,1,0:T(8,128)(2,1)S(1)}, u32[]{:S(2)}, u32[]{:S(2)}) collective-permute-start(bf16[1,2,32,3072]{3,2,1,0:T(8,128)(2,1)S(1)} %constant_dynamic-slice_fusion.2), channel_id=1, source_target_pairs={{0,16},{1,17},{2,18},{3,19},{4,20},{5,21},{6,22},{7,23},{8,24},{9,... | collective-permute-start | bytes 1179656 | tf_op jit(solution)/shard_map/ppermute | solution.py:431
  445.9 27.0 %collective-permute-start.33 = (bf16[8,96,768]{2,1,0:T(8,128)(2,1)S(1)}, bf16[8,96,768]{2,1,0:T(8,128)(2,1)S(1)}, u32[]{:S(2)}, u32[]{:S(2)}) collective-permute-start(bf16[8,96,768]{2,1,0:T(8,128)(2,1)S(1)} %dynamic-slice_bitcast_fusion.1), channel_id=1, source_target_pairs={{0,2},{1,3},{2,0},{3,1},{4,6},{5,7},{6,4},{7,5},{8,10},{9,11},{10,... | collective-permute-start | bytes 3538952 | tf_op jit(solution)/shard_map/ppermute | solution.py:431
  475.1 27.4 %collective-permute-start.38 = (bf16[4,96,768]{2,1,0:T(8,128)(2,1)}, bf16[4,96,768]{2,1,0:T(8,128)(2,1)}, u32[]{:S(2)}, u32[]{:S(2)}) collective-permute-start(bf16[4,96,768]{2,1,0:T(8,128)(2,1)} %dynamic-slice_bitcast_fusion.2), channel_id=1, source_target_pairs={{0,16},{1,17},{2,18},{3,19},{4,20},{5,21},{6,22},{7,23},{8,24},{9,... | collective-permute-start | bytes 1769480 | tf_op jit(solution)/shard_map/ppermute | solution.py:431
  484.6 37.5 %collective-permute-start.46 = (bf16[3,32,3072]{2,1,0:T(8,128)(2,1)S(1)}, bf16[3,32,3072]{2,1,0:T(8,128)(2,1)S(1)}, u32[]{:S(2)}, u32[]{:S(2)}) collective-permute-start(bf16[3,32,3072]{2,1,0:T(8,128)(2,1)S(1)} %pad_maximum_fusion.10), channel_id=1, source_target_pairs={{0,8},{1,9},{2,10},{3,11},{4,12},{5,13},{6,14},{7,15},{8,0},{9,1},... | collective-permute-start | bytes 1769480 | tf_op jit(solution)/shard_map/ppermute | solution.py:431
  (102 other events, 819.3 us)
Sparse Core Ops, SparseCore 0:
  10.8 48.6 all-gather.2
  71.8 40.2 all-gather.4

commit v3 on v2

v3 whole, which is shorter than its diff:
```python
import math
import jax
import jax.numpy as jnp
from jax import lax
from jax.experimental import pallas as pl
from jax.experimental.pallas import tpu as pltpu
from jax.sharding import PartitionSpec as P

BLOCK = 128
THIRDS = 3
EPS = 1e-06
GELU_A = math.sqrt(2.0 / math.pi)
GELU_B = 0.044715
NT = (((1,), (1,)), ((), ()))
TN = (((0,), (0,)), ((), ()))
VMEM_BYTES = 56 * 1024 * 1024


def cost(micros):
    return pl.CostEstimate(flops=int(micros * 0.37e9), bytes_accessed=0, transcendentals=0)


def dot_f32(left, right, dims=(((1,), (0,)), ((), ()))):
    return lax.dot_general(left, right, dims, preferred_element_type=jnp.float32)


def assemble(rows, pieces, relayed):
    capacity = pieces[0].shape[0] // 2
    for place, piece in enumerate(pieces):
        rows[pl.ds(place * capacity, capacity), :] = piece[pl.ds(0, capacity), :]
    rows[pl.ds(len(pieces) * capacity, relayed.shape[0]), :] = relayed[...]


def whole(shape):
    return pl.BlockSpec(shape, lambda *step: (0,) * len(shape))


def expert_forward_kernel(pick, *refs, chunk, count):
    pieces, relayed, w_in, w_out = refs[:count], refs[count], refs[count + 1], refs[count + 2]
    hidden_t, slope, mine, theirs, rows_t, rows, total = refs[count + 3 :]
    step = pl.program_id(0)

    @pl.when(step == 0)
    def _():
        assemble(rows, pieces, relayed)
        total[...] = jnp.zeros_like(total)
        rows_t[...] = rows[...].T

    for start in range(0, rows.shape[0], chunk):
        part = pl.ds(start, chunk)
        pre = dot_f32(rows[part, :], w_in[0])
        square = pre * pre
        bend = jnp.tanh(pre * (GELU_A + (GELU_A * GELU_B) * square))
        half = 0.5 + 0.5 * bend
        act = (pre * half).astype(jnp.bfloat16)
        lift = pre * (0.5 * GELU_A + (1.5 * GELU_A * GELU_B) * square)
        slope[part, :] = (half + lift * (1.0 - bend * bend)).astype(jnp.bfloat16)
        hidden_t[:, part] = act.T
        total[part, :] += dot_f32(act, w_out[0])

    @pl.when(step == pl.num_programs(0) - 1)
    def _():
        half = mine.shape[0]
        mine[...] = total[pl.ds(0, half), :].astype(jnp.bfloat16)
        theirs[...] = total[pl.ds(half, half), :].astype(jnp.bfloat16)


def expert_forward(pick, pieces, relayed, w_in, w_out, tile=512, chunk=256):
    many, width = pieces[0].shape[0] * len(pieces), relayed.shape[1]
    inner = w_in.shape[2]
    bf16 = jnp.bfloat16
    return pl.pallas_call(
        lambda *refs: expert_forward_kernel(*refs, chunk=chunk, count=len(pieces)),
        grid_spec=pltpu.PrefetchScalarGridSpec(
            num_scalar_prefetch=1,
            grid=(inner // tile,),
            in_specs=[whole(piece.shape) for piece in pieces]
            + [
                whole(relayed.shape),
                pl.BlockSpec((1, width, tile), lambda f, pick: (pick[0], 0, f)),
                pl.BlockSpec((1, tile, width), lambda f, pick: (pick[0], f, 0)),
            ],
            out_specs=[
                pl.BlockSpec((tile, many), lambda f, pick: (f, 0)),
                pl.BlockSpec((many, tile), lambda f, pick: (0, f)),
                whole((many // 2, width)),
                whole((many // 2, width)),
                whole((width, many)),
            ],
            scratch_shapes=[pltpu.VMEM((many, width), bf16), pltpu.VMEM((many, width), jnp.float32)],
        ),
        out_shape=[
            jax.ShapeDtypeStruct((inner, many), bf16),
            jax.ShapeDtypeStruct((many, inner), bf16),
            jax.ShapeDtypeStruct((many // 2, width), bf16),
            jax.ShapeDtypeStruct((many // 2, width), bf16),
            jax.ShapeDtypeStruct((width, many), bf16),
        ],
        compiler_params=pltpu.CompilerParams(vmem_limit_bytes=VMEM_BYTES),
        cost_estimate=cost(22),
        name="expert_forward",
    )(pick, *pieces, relayed, w_in, w_out)


def expert_backward_kernel(pick, grads, w_in, w_out, slope, grad_pre, mine, theirs, total, *, chunk):
    step = pl.program_id(0)

    @pl.when(step == 0)
    def _():
        total[...] = jnp.zeros_like(total)

    for start in range(0, grads.shape[0], chunk):
        part = pl.ds(start, chunk)
        back = dot_f32(grads[part, :], w_out[0], NT) * slope[part, :].astype(jnp.float32)
        back = back.astype(jnp.bfloat16)
        grad_pre[part, :] = back
        total[part, :] += dot_f32(back, w_in[0], NT)

    @pl.when(step == pl.num_programs(0) - 1)
    def _():
        half = mine.shape[0]
        mine[...] = total[pl.ds(0, half), :].astype(jnp.bfloat16)
        theirs[...] = total[pl.ds(half, half), :].astype(jnp.bfloat16)


def expert_backward(pick, grads, w_in, w_out, slope, tile=512, chunk=640):
    many, width = grads.shape
    inner = w_in.shape[2]
    bf16 = jnp.bfloat16
    return pl.pallas_call(
        lambda *refs: expert_backward_kernel(*refs, chunk=chunk),
        grid_spec=pltpu.PrefetchScalarGridSpec(
            num_scalar_prefetch=1,
            grid=(inner // tile,),
            in_specs=[
                whole((many, width)),
                pl.BlockSpec((1, width, tile), lambda f, pick: (pick[0], 0, f)),
                pl.BlockSpec((1, tile, width), lambda f, pick: (pick[0], f, 0)),
                pl.BlockSpec((many, tile), lambda f, pick: (0, f)),
            ],
            out_specs=[
                pl.BlockSpec((many, tile), lambda f, pick: (0, f)),
                whole((many // 2, width)),
                whole((many // 2, width)),
            ],
            scratch_shapes=[pltpu.VMEM((many, width), jnp.float32)],
        ),
        out_shape=[
            jax.ShapeDtypeStruct((many, inner), bf16),
            jax.ShapeDtypeStruct((many // 2, width), bf16),
            jax.ShapeDtypeStruct((many // 2, width), bf16),
        ],
        compiler_params=pltpu.CompilerParams(vmem_limit_bytes=VMEM_BYTES),
        cost_estimate=cost(20),
        name="expert_backward",
    )(pick, grads, w_in, w_out, slope)


def seen_blocks(row_block, blocks):
    return max(row_block + 1, blocks // 2)


def attention_forward_kernel(far, queries, keys, values, near, attended, probs, *, heads, blocks):
    pair = pl.program_id(0)
    lane = lax.broadcasted_iota(jnp.int32, (BLOCK, 2 * heads), 1)
    for row_block in range(blocks):
        rows = pl.ds(row_block * BLOCK, BLOCK)
        span = seen_blocks(row_block, blocks)
        seen = pl.ds(0, span * BLOCK)
        outs = []
        for head in range(2):
            mine = (lane < heads) if head == 0 else (lane >= heads)
            query = jnp.where(mine, queries[rows, :] * 0.125, 0.0).astype(jnp.bfloat16)
            score = dot_f32(query, keys[seen, :], NT)
            far_bias = far[pair * 2 + head]
            pieces = []
            for key_block in range(span):
                piece = score[:, key_block * BLOCK : (key_block + 1) * BLOCK]
                slot = near_slot(row_block, key_block, blocks)
                pieces.append(piece + (far_bias if slot is None else near[head, slot]))
            peak = pieces[0]
            for piece in pieces[1:]:
                peak = jnp.maximum(peak, piece)
            peak = jnp.max(peak, axis=1, keepdims=True)
            pieces = [jnp.exp(piece - peak) for piece in pieces]
            mass = pieces[0]
            for piece in pieces[1:]:
                mass = mass + piece
            scale = 1.0 / jnp.sum(mass, axis=1, keepdims=True)
            weights = jnp.concatenate([(piece * scale).astype(jnp.bfloat16) for piece in pieces], axis=1)
            probs[head, rows, seen] = weights
            outs.append(dot_f32(weights, values[seen, :]))
        attended[rows, :] = jnp.where(lane < heads, outs[0], outs[1]).astype(jnp.bfloat16)


def near_slot(row_block, key_block, blocks):
    half = blocks // 2
    if key_block < row_block - 1:
        return None
    if key_block == row_block - 1:
        return 0
    if key_block == row_block:
        return 1 + min(row_block, half)
    count = 2 + half
    for row in range(half):
        for key in range(row + 1, half):
            if (row, key) == (row_block, key_block):
                return count
            count += 1
    raise ValueError


def near_pairs(blocks):
    half = blocks // 2
    pairs = [(1, 0)] + [(row, row) for row in range(half + 1)]
    return pairs + [(row, key) for row in range(half) for key in range(row + 1, half)]


def attention_forward(far, qk_rows, v_rows, near):
    length, width = v_rows.shape
    pairs = width // 128
    blocks = length // BLOCK
    slots = near.shape[1]
    return pl.pallas_call(
        lambda *refs: attention_forward_kernel(*refs, heads=64, blocks=blocks),
        grid_spec=pltpu.PrefetchScalarGridSpec(
            num_scalar_prefetch=1,
            grid=(pairs,),
            in_specs=[
                pl.BlockSpec((None, length, 128), lambda h, far: (0, 0, h)),
                pl.BlockSpec((None, length, 128), lambda h, far: (1, 0, h)),
                pl.BlockSpec((length, 128), lambda h, far: (0, h)),
                pl.BlockSpec((2, slots, BLOCK, BLOCK), lambda h, far: (h, 0, 0, 0)),
            ],
            out_specs=[
                pl.BlockSpec((length, 128), lambda h, far: (0, h)),
                pl.BlockSpec((2, length, length), lambda h, far: (h, 0, 0)),
            ],
        ),
        out_shape=[
            jax.ShapeDtypeStruct((length, width), jnp.bfloat16),
            jax.ShapeDtypeStruct((2 * pairs, length, length), jnp.bfloat16),
        ],
        compiler_params=pltpu.CompilerParams(vmem_limit_bytes=VMEM_BYTES),
        cost_estimate=cost(17),
        name="attention_forward",
    )(far, qk_rows, qk_rows, v_rows, near)


def attention_backward_kernel(queries, keys, values, grads, probs, grad_rows, bands, flow, *, heads, blocks):
    lane = lax.broadcasted_iota(jnp.int32, (BLOCK, 2 * heads), 1)
    query_t = (queries[...] * 0.125).astype(jnp.bfloat16).T
    grad_t = grads[...].T
    half = blocks // 2
    dk, dv = [], []
    dq = [[], []]
    for head in range(2):
        mine = (lane < heads) if head == 0 else (lane >= heads)
        sums = [None] * 4
        for row_block in range(blocks):
            rows = pl.ds(row_block * BLOCK, BLOCK)
            span = seen_blocks(row_block, blocks)
            seen = pl.ds(0, span * BLOCK)
            grad = jnp.where(mine, grads[rows, :], 0.0).astype(jnp.bfloat16)
            soft = probs[head, rows, seen].astype(jnp.float32)
            back = dot_f32(grad, values[seen, :], NT)
            inner = jnp.sum(soft * back, axis=1, keepdims=True)
            score_grad = (soft * (back - inner)).astype(jnp.bfloat16)
            flow[rows, seen] = score_grad
            dq[head].append(dot_f32(score_grad, keys[seen, :]) * 0.125)
            for key_block in range(span):
                band = max(key_block - row_block, -2)
                if band > 1:
                    continue
                tile = score_grad[:, key_block * BLOCK : (key_block + 1) * BLOCK].astype(jnp.float32)
                sums[band + 2] = tile if sums[band + 2] is None else sums[band + 2] + tile
        for band in range(4):
            bands[head, band] = sums[band]
        part = slice(head * heads, (head + 1) * heads)
        key_pieces, value_pieces = [], []
        for key_block in range(blocks):
            first = 0 if key_block < half else key_block
            rows = pl.ds(first * BLOCK, (blocks - first) * BLOCK)
            cols = pl.ds(key_block * BLOCK, BLOCK)
            key_pieces.append(dot_f32(query_t[part, first * BLOCK :], flow[rows, cols]))
            value_pieces.append(dot_f32(grad_t[part, first * BLOCK :], probs[head, rows, cols]))
        dk.append(jnp.concatenate(key_pieces, axis=1))
        dv.append(jnp.concatenate(value_pieces, axis=1))
    for row_block in range(blocks):
        rows = pl.ds(row_block * BLOCK, BLOCK)
        grad_rows[0, rows, :] = jnp.where(lane < heads, dq[0][row_block], dq[1][row_block]).astype(jnp.bfloat16)
    grad_rows[1] = jnp.concatenate(dk, axis=0).T.astype(jnp.bfloat16)
    grad_rows[2] = jnp.concatenate(dv, axis=0).T.astype(jnp.bfloat16)


def attention_backward(qk_rows, v_rows, grads, probs):
    length, width = grads.shape
    pairs = width // 128
    blocks = length // BLOCK
    block = pl.BlockSpec((length, 128), lambda h: (0, h))
    of_two = [pl.BlockSpec((None, length, 128), lambda h, c=c: (c, 0, h)) for c in range(2)]
    return pl.pallas_call(
        lambda *refs: attention_backward_kernel(*refs, heads=64, blocks=blocks),
        grid=(pairs,),
        in_specs=[*of_two, block, block, pl.BlockSpec((2, length, length), lambda h: (h, 0, 0))],
        out_specs=[pl.BlockSpec((3, length, 128), lambda h: (0, 0, h)), pl.BlockSpec((2, 4, BLOCK, BLOCK), lambda h: (h, 0, 0, 0))],
        out_shape=[jax.ShapeDtypeStruct((3, length, width), jnp.bfloat16)]
        + [jax.ShapeDtypeStruct((2 * pairs, 4, BLOCK, BLOCK), jnp.float32)],
        scratch_shapes=[pltpu.VMEM((length, length), jnp.bfloat16)],
        compiler_params=pltpu.CompilerParams(vmem_limit_bytes=VMEM_BYTES),
        cost_estimate=cost(17),
        name="attention_backward",
    )(qk_rows, qk_rows, v_rows, grads, probs)


def cut_slices(result, outs, count, layout):
    rows = result.shape[0] // count
    part, many = rows // THIRDS, count // 2
    place = 0
    for out, pieces in zip(outs, layout):
        for piece in range(pieces):
            half, third = divmod(place, THIRDS)
            for k in range(many):
                start = (half * many + k) * rows + third * part
                out[k, piece] = result[start : start + part]
            place += 1


def weight_part_kernel(picks, *refs, count, layout):
    lefts, right, outs = refs[:count], refs[count], refs[count + 1 :]
    left = jnp.concatenate([ref[...] for ref in lefts], axis=0)
    cut_slices(dot_f32(left, right[...]).astype(jnp.bfloat16), outs, count, layout)


def weight_first_kernel(picks, *refs, count, layout, pieces):
    lefts, parts, relayed, outs = refs[:count], refs[count : count + pieces], refs[count + pieces], refs[count + pieces + 1 :]
    assemble(outs[0], parts, relayed)
    left = jnp.concatenate([ref[...] for ref in lefts], axis=0)
    cut_slices(dot_f32(left, outs[0][...]).astype(jnp.bfloat16), outs[1:], count, layout)


def weight_part_plain(picks, left, right, rows, layout):
    depth, width = right.shape
    many, part = picks.shape[0] // 2, rows // THIRDS
    result = jnp.take(left.reshape(-1, rows, depth), picks, axis=0)
    result = jnp.einsum("srd,dw->srw", result, right, preferred_element_type=jnp.float32).astype(jnp.bfloat16)
    result = result.reshape(2, many, THIRDS, part, width).transpose(1, 0, 2, 3, 4).reshape(many, 2 * THIRDS, part, width)
    starts = [sum(layout[:place]) for place in range(len(layout))]
    return [result[:, start : start + pieces] for start, pieces in zip(starts, layout)]


def weight_part(picks, left, right, rows, layout, tile):
    depth, width = right.shape
    count = picks.shape[0]
    many, part = count // 2, rows // THIRDS
    if part % 16:
        return weight_part_plain(picks, left, right, rows, layout)
    return pl.pallas_call(
        lambda *refs: weight_part_kernel(*refs, count=count, layout=layout),
        grid_spec=pltpu.PrefetchScalarGridSpec(
            num_scalar_prefetch=1,
            grid=(width // tile,),
            in_specs=[pl.BlockSpec((rows, depth), lambda i, picks, k=k: (picks[k], 0)) for k in range(count)]
            + [pl.BlockSpec((depth, tile), lambda i, picks: (0, i))],
            out_specs=[pl.BlockSpec((many, pieces, part, tile), lambda i, picks: (0, 0, 0, i)) for pieces in layout],
        ),
        out_shape=[jax.ShapeDtypeStruct((many, pieces, part, width), jnp.bfloat16) for pieces in layout],
        compiler_params=pltpu.CompilerParams(vmem_limit_bytes=VMEM_BYTES),
        cost_estimate=cost(7),
        name="weight_part",
    )(picks, *([left] * count), right)


def weight_first(picks, left, pieces, relayed, rows, layout):
    depth, width = left.shape[1], relayed.shape[1]
    count = picks.shape[0]
    many, part = count // 2, rows // THIRDS
    if part % 16:
        capacity = pieces[0].shape[0] // 2
        right = jnp.concatenate([piece[:capacity] for piece in pieces] + [relayed])
        return [right, *weight_part_plain(picks, left, right, rows, layout)]
    return pl.pallas_call(
        lambda *refs: weight_first_kernel(*refs, count=count, layout=layout, pieces=len(pieces)),
        grid_spec=pltpu.PrefetchScalarGridSpec(
            num_scalar_prefetch=1,
            grid=(1,),
            in_specs=[pl.BlockSpec((rows, depth), lambda i, picks, k=k: (picks[k], 0)) for k in range(count)]
            + [whole(piece.shape) for piece in pieces]
            + [whole(relayed.shape)],
            out_specs=[whole((depth, width))] + [whole((many, pieces, part, width)) for pieces in layout],
        ),
        out_shape=[jax.ShapeDtypeStruct((depth, width), jnp.bfloat16)]
        + [jax.ShapeDtypeStruct((many, pieces, part, width), jnp.bfloat16) for pieces in layout],
        compiler_params=pltpu.CompilerParams(vmem_limit_bytes=VMEM_BYTES),
        cost_estimate=cost(7),
        name="weight_first",
    )(picks, *([left] * count), *pieces, relayed)


def hot_columns(slots, first, count):
    rows = first + lax.broadcasted_iota(jnp.int32, (count, slots.shape[1]), 0)
    return (rows == slots).astype(jnp.bfloat16)


def hot_rows(slots, first, count):
    cols = first + lax.broadcasted_iota(jnp.int32, (slots.shape[0], count), 1)
    return (cols == slots).astype(jnp.bfloat16)


def pack_kernel(slots, values, *outs):
    table = values[...]
    for place, out in enumerate(outs):
        count = out.shape[0]
        hot = hot_columns(slots[0:1, :], place * count, count) + hot_columns(slots[1:2, :], place * count, count)
        out[...] = dot_f32(hot, table).astype(jnp.bfloat16)


def pack(slots, values, pieces, count):
    return pl.pallas_call(
        pack_kernel,
        out_shape=[jax.ShapeDtypeStruct((count, values.shape[1]), jnp.bfloat16)] * pieces,
        compiler_params=pltpu.CompilerParams(vmem_limit_bytes=VMEM_BYTES),
        cost_estimate=cost(4),
        name="pack",
    )(slots, values)


def slot_pieces(near, passed, far):
    capacity = far[0].shape[0] // 2
    return [(near, capacity), (passed, capacity)] + [(ref, 2 * capacity) for ref in far]


def unpack(slots, refs):
    total, first = None, 0
    for ref, count in refs:
        part = dot_f32(hot_rows(slots, first, count), ref[pl.ds(0, count), :])
        total = part if total is None else total + part
        first += count
    return total


def combine_kernel(*refs, chips):
    slots, slots_t, scale, near, passed = refs[:5]
    far = refs[5 : 5 + chips - 1]
    middle, teacher, cotangent, valid, gates = refs[4 + chips : 9 + chips]
    output, grad_y, grad_gates, square = refs[9 + chips : 13 + chips]
    sends = refs[13 + chips :]
    f32 = jnp.float32
    order = slot_pieces(near, passed, far)
    picked = [unpack(slots[:, k : k + 1], order) for k in range(2)]
    result = middle[...] + (gates[:, 0:1] * picked[0] + gates[:, 1:2] * picked[1])
    output[...] = result.astype(jnp.bfloat16)
    misfit = valid[...] * (result - teacher[...].astype(f32))
    square[...] = jnp.sum((misfit * misfit).reshape(-1, 8, misfit.shape[1]), axis=0)
    grad = cotangent[...].astype(f32) + misfit * scale[0, 0]
    grad_y[...] = grad
    for k in range(2):
        grad_gates[:, k : k + 1] = jnp.sum(grad * picked[k], axis=1, keepdims=True)
    scaled = [(gates[:, k : k + 1] * grad).astype(jnp.bfloat16) for k in range(2)]
    for place, out in enumerate(sends):
        count = out.shape[0]
        rows = [dot_f32(hot_columns(slots_t[k : k + 1, :], place * count, count), scaled[k]) for k in range(2)]
        out[...] = (rows[0] + rows[1]).astype(jnp.bfloat16)


def combine(slots, scale, near, passed, far, middle, teacher, cotangent, valid, gates):
    length, width = middle.shape
    chips = len(far) + 1
    f32, bf16 = jnp.float32, jnp.bfloat16
    return pl.pallas_call(
        lambda *refs: combine_kernel(*refs, chips=chips),
        in_specs=[pl.BlockSpec(memory_space=pltpu.VMEM)] * 2
        + [pl.BlockSpec(memory_space=pltpu.SMEM)]
        + [pl.BlockSpec(memory_space=pltpu.VMEM)] * (6 + chips),
        out_shape=[
            jax.ShapeDtypeStruct((length, width), bf16),
            jax.ShapeDtypeStruct((length, width), f32),
            jax.ShapeDtypeStruct((length, 2), f32),
            jax.ShapeDtypeStruct((8, width), f32),
        ]
        + [jax.ShapeDtypeStruct(far[0].shape, bf16)] * chips,
        compiler_params=pltpu.CompilerParams(vmem_limit_bytes=VMEM_BYTES),
        cost_estimate=cost(8),
        name="combine",
    )(slots, slots.T, scale, near, passed, *far, middle, teacher, cotangent, valid, gates)


def collect_kernel(*refs, chips):
    slots, near, passed = refs[:3]
    far = refs[3 : 2 + chips]
    middle, gain, grad_logits, router, grad_y, weight = refs[2 + chips : 8 + chips]
    grad_middle, rounded, grad_attended, grad_gain = refs[8 + chips :]
    f32 = jnp.float32
    order = slot_pieces(near, passed, far)
    grad = dot_f32(grad_logits[...], router[...], NT)
    grad = grad + (unpack(slots[:, 0:1], order) + unpack(slots[:, 1:2], order))
    value = middle[...]
    root = lax.rsqrt(jnp.mean(value * value, axis=1, keepdims=True) + EPS)
    normed = value * root
    grad_gain[...] = jnp.sum((grad * normed).reshape(-1, 8, value.shape[1]), axis=0)
    scaled = grad * gain[...]
    inner = jnp.mean(scaled * normed, axis=1, keepdims=True)
    result = grad_y[...] + root * (scaled - normed * inner)
    grad_middle[...] = result
    low = result.astype(jnp.bfloat16)
    rounded[...] = low
    grad_attended[...] = dot_f32(low, weight[...], NT).astype(jnp.bfloat16)


def collect(slots, near, passed, far, middle, gain, grad_logits, router, grad_y, weight):
    length, width = middle.shape
    chips = len(far) + 1
    f32, bf16 = jnp.float32, jnp.bfloat16
    return pl.pallas_call(
        lambda *refs: collect_kernel(*refs, chips=chips),
        out_shape=[
            jax.ShapeDtypeStruct((length, width), f32),
            jax.ShapeDtypeStruct((length, width), bf16),
            jax.ShapeDtypeStruct((length, width), bf16),
            jax.ShapeDtypeStruct((8, width), f32),
        ],
        compiler_params=pltpu.CompilerParams(vmem_limit_bytes=VMEM_BYTES),
        cost_estimate=cost(7),
        name="collect",
    )(slots, near, passed, *far, middle, gain.reshape(1, -1), grad_logits, router, grad_y, weight)


def outer_halves_kernel(core, left, right, away, stay, left_t, *, count):
    step = pl.program_id(0)

    @pl.when(step == 0)
    def _():
        left_t[...] = left[...].T

    result = dot_f32(left_t[...], right[...]).astype(jnp.bfloat16)

    @pl.when(step < count)
    def _():
        away[...] = result

    @pl.when(step >= count)
    def _():
        stay[...] = result


def outer_halves(core, left, right):
    length, width = left.shape
    count, half = right.shape[0], right.shape[2] // 2
    shape = jax.ShapeDtypeStruct((count, width, half), jnp.bfloat16)
    return pl.pallas_call(
        lambda *refs: outer_halves_kernel(*refs, count=count),
        grid_spec=pltpu.PrefetchScalarGridSpec(
            num_scalar_prefetch=1,
            grid=(2 * count,),
            in_specs=[
                pl.BlockSpec((length, width), lambda i, core: (0, 0)),
                pl.BlockSpec((None, length, half), lambda i, core: (i % count, 0, jnp.where(i < count, 1 - core[0], core[0]))),
            ],
            out_specs=[
                pl.BlockSpec((None, width, half), lambda i, core: (jnp.minimum(i, count - 1), 0, 0)),
                pl.BlockSpec((None, width, half), lambda i, core: (jnp.maximum(i - count, 0), 0, 0)),
            ],
            scratch_shapes=[pltpu.VMEM((width, length), jnp.bfloat16)],
        ),
        out_shape=[shape, shape],
        compiler_params=pltpu.CompilerParams(vmem_limit_bytes=VMEM_BYTES),
        cost_estimate=cost(2 * count),
        name="outer_halves",
    )(core, left, right)


def project_kernel(core, rows, mine, other, result, joined, *, used):
    half = mine.shape[1]
    first = jnp.where(core[0] == 0, mine[...], other[...])
    second = jnp.where(core[0] == 0, other[...], mine[...])
    joined[:, :half] = first
    joined[:, half:] = second

    @pl.when(pl.program_id(0) < used)
    def _():
        result[:, :half] = dot_f32(rows[...], first).astype(jnp.bfloat16)
        result[:, half:] = dot_f32(rows[...], second).astype(jnp.bfloat16)


def project(core, rows, mine, other, used):
    count, width, half = mine.shape
    length = rows.shape[0]
    return pl.pallas_call(
        lambda *refs: project_kernel(*refs, used=used),
        grid_spec=pltpu.PrefetchScalarGridSpec(
            num_scalar_prefetch=1,
            grid=(count,),
            in_specs=[
                pl.BlockSpec((length, width), lambda i, core: (0, 0)),
                pl.BlockSpec((None, width, half), lambda i, core: (i, 0, 0)),
                pl.BlockSpec((None, width, half), lambda i, core: (i, 0, 0)),
            ],
            out_specs=[
                pl.BlockSpec((None, length, 2 * half), lambda i, core: (jnp.minimum(i, used - 1), 0, 0)),
                pl.BlockSpec((None, width, 2 * half), lambda i, core: (i, 0, 0)),
            ],
        ),
        out_shape=[
            jax.ShapeDtypeStruct((used, length, 2 * half), jnp.bfloat16),
            jax.ShapeDtypeStruct((count, width, 2 * half), jnp.bfloat16),
        ],
        compiler_params=pltpu.CompilerParams(vmem_limit_bytes=VMEM_BYTES),
        cost_estimate=cost(3),
        name="project",
    )(core, rows, mine, other)


BOUNDS = (12, 16, 23, 32, 46, 64, 91)
TOP_PRECISION = lax.Precision.HIGHEST
AXES = ("dp", "expert")
PAIR = 2


def after(value, *others):
    return lax.optimization_barrier((value, *others))[0] if others else value


def bucket_index(offset):
    distance = jnp.abs(offset)
    far_bucket = 8 + sum([(distance >= level).astype(jnp.int32) for level in BOUNDS])
    near_bucket = jnp.where(distance < 8, distance, far_bucket)
    return jnp.where(offset > 0, 16, 0) + near_bucket


def norm_apply(inputs, gain_vec):
    return inputs * lax.rsqrt(jnp.mean(inputs * inputs, axis=-1, keepdims=True) + EPS) * gain_vec


def gate_values(logits, routes):
    soft_probs = jax.nn.softmax(logits, axis=-1)
    picked_hot = (
        routes[:, :, None] == jnp.arange(logits.shape[1], dtype=jnp.int32)[None, None, :]
    ).astype(jnp.float32)
    chosen = jnp.sum(soft_probs[:, None, :] * picked_hot, axis=-1)
    return chosen / jnp.sum(chosen, axis=1, keepdims=True)


def tile_offsets(query_block, key_block):
    rows = query_block * BLOCK + lax.broadcasted_iota(jnp.int32, (BLOCK, BLOCK), 0)
    cols = key_block * BLOCK + lax.broadcasted_iota(jnp.int32, (BLOCK, BLOCK), 1)
    return rows, cols


def near_bias(table, prefix_len, blocks):
    buckets = table.shape[1]
    tiles = []
    for query_block, key_block in near_pairs(blocks):
        rows, cols = tile_offsets(query_block, key_block)
        hot = (bucket_index(cols - rows)[None] == jnp.arange(buckets, dtype=jnp.int32)[:, None, None]).astype(jnp.float32)
        tile = jnp.einsum("hb,bxy->hxy", table, hot, precision=TOP_PRECISION)
        if key_block >= query_block:
            tile = jnp.where(((cols <= rows) | (cols < prefix_len))[None], tile, -1e30)
        tiles.append(tile)
    return jnp.stack(tiles, axis=1)


def table_gradient(bands, buckets):
    rows, cols = tile_offsets(0, 0)
    ids = [jnp.full((BLOCK, BLOCK), bucket_far(), jnp.int32)]
    ids += [bucket_index(shift * BLOCK + cols - rows) for shift in (-1, 0, 1)]
    hot = (jnp.stack(ids)[..., None] == jnp.arange(buckets, dtype=jnp.int32)).astype(jnp.float32)
    return jnp.einsum("hdxy,dxyb->hb", bands, hot, precision=TOP_PRECISION)


def bucket_far():
    return 8 + len(BOUNDS)


def on_device(
    tokens,
    qkv_weight,
    out_weight,
    position_bias_table,
    gain_attn,
    gain_moe,
    router,
    w_in,
    w_out,
    routes,
    prefix,
    valid_mask,
    teacher,
    cotangent,
):
    length, width = tokens.shape
    bf16, f32 = jnp.bfloat16, jnp.float32
    expert_count = router.shape[1]
    top_count = routes.shape[1]
    groups = lax.axis_size("expert")
    copies = lax.axis_size("dp")
    inner = w_in.shape[2]
    capacity = 5 * length * top_count // (4 * expert_count)
    total_tokens = length * copies * groups
    sources = 2 * groups
    blocks = length // BLOCK
    here_dp, here_group = lax.axis_index("dp"), lax.axis_index("expert")
    half = (here_dp // PAIR) % 2
    core = here_group % 2
    rest = copies // 4

    def swap(value, dp_mask, group_mask):
        pairs = [
            (i, ((i // groups) ^ dp_mask) * groups + ((i % groups) ^ group_mask))
            for i in range(copies * groups)
        ]
        return lax.ppermute(value, AXES, pairs)

    def bits(count):
        return [1 << place for place in range(count.bit_length() - 1)]

    def partial_sums(value):
        sums = []
        for masks in [(0, mask) for mask in bits(groups)] + [(mask, 0) for mask in bits(copies)]:
            value = value + swap(value, *masks)
            sums.append(value)
        return sums

    chips = groups

    def across(value, place):
        return swap(value, PAIR * (place // (groups // 2)), 2 * (place % (groups // 2)))

    def send_out(pieces):
        got = [pieces[0]] + [across(pieces[place], place) for place in range(1, chips)]
        return got, swap(jnp.concatenate([piece[capacity:] for piece in got]), 0, 1)

    def send_back(mine, theirs):
        passed = swap(theirs, 0, 1)
        sends = []
        for place in range(1, chips):
            part = slice(place * capacity, (place + 1) * capacity)
            sends.append(jnp.concatenate([mine[part], passed[part]]))
        return passed, sends, [across(send, place) for place, send in enumerate(sends, 1)]

    def ring_place(device):
        return jnp.where(device % 2 == 0, device // 2, copies - 1 - device // 2)

    ring = list(range(0, copies, 2)) + list(range(copies - 1, 0, -2))

    def gather_ring(shard, due):
        if copies > 8:
            return lax.all_gather(shard, "dp", axis=1, tiled=True)
        count, rows, columns = shard.shape
        place = ring_place(here_dp)
        table = jnp.array(ring, jnp.int32)
        full = jnp.zeros((count, copies, rows, columns), bf16)
        full = lax.dynamic_update_index_in_dim(full, shard, here_dp, 1)
        for turn, steps in ((1, copies // 2), (-1, copies // 2 - 1)):
            held = shard
            pairs = [(ring[i], ring[(i + turn) % copies]) for i in range(copies)]
            for step in range(1, steps + 1):
                held = lax.ppermute(after(held, *due[step - 2 : step - 1]) if step > 1 else held, "dp", pairs)
                full = lax.dynamic_update_index_in_dim(full, held, table[(place - turn * step) % copies], 1)
        return full.reshape(count, copies * rows, columns)

    columns = width // 2
    core_index = core.reshape(1).astype(jnp.int32)
    shards = jnp.concatenate([qkv_weight, out_weight[None]])
    shards = lax.dynamic_slice_in_dim(shards, core * columns, columns, 2)
    valid_rows = valid_mask.astype(f32)[:, None]
    counts = partial_sums(jnp.broadcast_to(jnp.sum(valid_rows), (8, 128)))
    valid_count = counts[-1][0, 0]
    mine_qk, mine_vo = gather_ring(shards[:2], counts), gather_ring(shards[2:], ())
    other_qk, other_vo = swap(mine_qk, 0, 1), swap(mine_vo, 0, 1)
    prefix_len = prefix[0]
    near = near_bias(position_bias_table, prefix_len, blocks)

    flat_routes = routes.reshape(-1)
    pair_count = length * top_count
    slot_count = sources * capacity
    route_hits = (flat_routes[:, None] == jnp.arange(expert_count, dtype=jnp.int32)[None, :]).astype(bf16)
    lower_ones = (
        lax.broadcasted_iota(jnp.int32, (pair_count, pair_count), 0)
        >= lax.broadcasted_iota(jnp.int32, (pair_count, pair_count), 1)
    ).astype(bf16)
    running = jnp.dot(lower_ones, route_hits, preferred_element_type=f32)
    pair_rank = jnp.sum((running - 1.0) * route_hits.astype(f32), axis=1).astype(jnp.int32)
    away = (flat_routes // 2) ^ here_group
    chip = ((flat_routes % 2) ^ half) * (groups // 2) + away // 2
    slots = ((chip * 2 + away % 2) * capacity + pair_rank).reshape(length, top_count)
    slots_t = slots.T

    resid = tokens.astype(f32)
    normed1 = norm_apply(resid, gain_attn).astype(bf16)
    qk_rows, weight_qk = project(core_index, normed1, mine_qk, other_qk, 2)
    v_rows, weight_vo = project(core_index, normed1, mine_vo, other_vo, 1)
    v_rows = v_rows[0]
    near = after(near, valid_count)
    attended, probs = attention_forward(position_bias_table[:, bucket_far()], qk_rows, v_rows, near)
    middle = resid + jnp.dot(attended, weight_vo[1], preferred_element_type=f32)
    normed2 = norm_apply(middle, gain_moe).astype(bf16)
    sends = pack(slots_t, normed2, chips, 2 * capacity)
    logits = jnp.dot(normed2, router, preferred_element_type=f32)
    gate_vals = gate_values(logits, routes)

    rows_got, rows_passed = send_out(sends)
    pick = half.reshape(1).astype(jnp.int32)
    hidden_t, slope, mine, theirs, rows_t = expert_forward(pick, rows_got, rows_passed, w_in, w_out)
    passed, _, far = send_back(mine, theirs)
    scale = (total_tokens / valid_count).reshape(1, 1)
    output, grad_y, grad_gates, squares, *sends = combine(
        slots, scale, mine, passed, far, middle, teacher, cotangent, valid_rows, gate_vals
    )
    grads_got, grads_passed = send_out(sends)
    gate_back = jax.vjp(lambda logit_vals: gate_values(logit_vals, routes), logits)[1]
    grad_logits = gate_back(grad_gates)[0].astype(bf16)
    grad_router = jnp.einsum("td,te->de", normed2, grad_logits, preferred_element_type=f32)

    out_rows = inner // copies
    in_rows = width // copies
    far_bit = here_dp % 2
    slices = jnp.arange(rest, dtype=jnp.int32) * 4

    def picks(bit0):
        return jnp.concatenate([slices + ((half ^ other_half) * 2 + bit0) for other_half in (1, 0)]).astype(jnp.int32)

    sent, kept = picks(1 - far_bit), picks(far_bit)

    def add(left, right):
        return (left.astype(f32) + right.astype(f32)).astype(bf16)

    def fold(unit, bit, axis=0):
        unit = unit.reshape(unit.shape[:axis] + (2, unit.shape[axis] // 2) + unit.shape[axis + 1 :])
        away_part = lax.dynamic_index_in_dim(unit, 1 - bit, axis, keepdims=False)
        return away_part, lax.dynamic_index_in_dim(unit, bit, axis, keepdims=False)

    far_masks = list(reversed(bits(copies)[2:]))

    def near_add(got, keep):
        away_part, stay_part = fold(add(got, keep), (here_dp // far_masks[0]) % 2)
        return away_part, stay_part

    def far_trade(away_part):
        return swap(away_part, far_masks[0], 0)

    def finish(got, stay):
        unit = add(got, stay)
        for mask in far_masks[1:]:
            away_part, stay_part = fold(unit, (here_dp // mask) % 2)
            unit = add(swap(away_part, mask, 0), stay_part)
        return unit[0]

    out_layout, in_layout = (2, 3, 1), (2, 1, 1, 2)
    grad_rows, send_a, send_b, send_c = weight_first(sent, hidden_t, grads_got, grads_passed, out_rows, out_layout)
    got_a = swap(send_a, 1, 0)
    grad_pre, mine, theirs = expert_backward(pick, after(grad_rows, send_a), w_in, w_out, slope)
    passed, sends, far = send_back(mine, after(theirs, got_a))
    got_b = swap(after(send_b, passed), 1, 0)
    grad_pre = after(grad_pre, *sends)
    send_d, send_e, send_f, send_g = weight_part(sent, rows_t, grad_pre, in_rows, in_layout, inner // 2)
    keep_d, keep_e, keep_f, keep_g = weight_part(kept, rows_t, grad_pre, in_rows, in_layout, inner // 2)
    keep_a, keep_b, keep_c = weight_part(kept, hidden_t, after(grad_rows, keep_d), out_rows, out_layout, width)
    away_a, stay_a = near_add(got_a, keep_a)
    far_a = far_trade(away_a)
    away_b, stay_b = near_add(got_b, keep_b)
    far = [after(pair, away_b) for pair in far]
    far_b = far_trade(away_b)
    grad_middle, grad_attn_proj, grad_attended, gain_moe_parts = collect(
        slots, mine, passed, far, middle, gain_moe, grad_logits, router, grad_y, weight_vo[1]
    )
    grad_gain_moe = jnp.sum(gain_moe_parts, axis=0)
    send_c, send_d = after((send_c, send_d), *far)
    got_c = swap(send_c, 1, 0)
    got_d = swap(send_d, 1, 0)
    out_away, out_stay = outer_halves(core_index, attended, grad_attn_proj[None])
    out_got = swap(out_away, 0, 1)
    grad_attended = after(grad_attended, out_away)
    grad_qkv_rows, bands = attention_backward(qk_rows, v_rows, grad_attended, probs)
    grad_qkv_rows, got_c, got_d = lax.optimization_barrier((grad_qkv_rows, got_c, got_d))
    done_a = finish(after(far_a, grad_qkv_rows), stay_a)
    done_b = finish(after(far_b, grad_qkv_rows), stay_b)

    away_c, stay_c = near_add(got_c, keep_c)
    far_c = far_trade(away_c)
    away_d, stay_d = near_add(got_d, keep_d)
    far_d = far_trade(away_d)
    got_e, got_f, got_g = [swap(after(send, away_d), 1, 0) for send in (send_e, send_f, send_g)]

    qkv_away, qkv_stay = outer_halves(core_index, normed1, grad_qkv_rows)
    qkv_got = swap(qkv_away, 0, 1)
    away_e, stay_e = near_add(got_e, keep_e)
    far_e = far_trade(away_e)
    qkv_total = add(after(qkv_got, stay_e), qkv_stay)
    away_f, stay_f = near_add(after(got_f, qkv_total), keep_f)
    far_f = far_trade(away_f)
    group_masks = bits(groups)[1:]
    dp_masks = sorted(bits(copies), key=lambda mask: (mask != PAIR, mask))

    def owners(part):
        return part.reshape(part.shape[0], copies, in_rows, columns)

    def over_groups(total, due):
        for mask in group_masks:
            away_part, stay_part = fold(total, (here_group // mask) % 2, 2)
            total = add(after(swap(away_part, 0, mask), *due), stay_part)
        return total

    out_total = over_groups(owners(add(out_got, out_stay)), ())
    done_c = finish(after(far_c, qkv_total), stay_c)
    total = over_groups(owners(qkv_total), (stay_f, done_c))
    away_g, stay_g = near_add(after(got_g, total), keep_g)
    far_g = far_trade(away_g)
    far_d, far_e, far_f = [after(far, total) for far in (far_d, far_e, far_f)]
    done_d = finish(far_d, stay_d)
    done_e = finish(far_e, stay_e)
    done_f = finish(far_f, stay_f)
    done_g = finish(far_g, stay_g)
    due = [(done_d,), (done_e, done_f), (done_g,)]
    reduced = total
    total = jnp.concatenate([total, out_total])
    total = total.reshape((4,) + (2,) * len(dp_masks) + total.shape[2:])
    left_bits = sorted(dp_masks, reverse=True)
    for mask in dp_masks:
        axis = 1 + left_bits.index(mask)
        left_bits.remove(mask)
        bit = (here_dp // mask) % 2
        away_part = lax.dynamic_index_in_dim(total, 1 - bit, axis, keepdims=False)
        stay_part = lax.dynamic_index_in_dim(total, bit, axis, keepdims=False)
        total = add(after(swap(away_part, mask, 0), *(due.pop(0) if due else ())), stay_part)
    for mask in reversed(group_masks):
        bit = (here_group // mask) % 2
        other = swap(total, 0, mask)
        total = jnp.concatenate([jnp.where(bit == 0, total, other), jnp.where(bit == 0, other, total)], axis=1)
    other = swap(total, 0, 1)
    total = jnp.concatenate([jnp.where(core == 0, total, other), jnp.where(core == 0, other, total)], axis=2)
    total = total.astype(f32)
    grad_qkv, grad_out_weight = total[:3], total[3]

    later = after(grad_qkv_rows, qkv_total)
    grad_normed1 = jnp.einsum("cte,cde->td", later[:2], weight_qk, preferred_element_type=f32)
    grad_normed1 = grad_normed1 + jnp.einsum("te,de->td", later[2], weight_vo[0], preferred_element_type=f32)
    first_back = jax.vjp(norm_apply, resid, gain_attn)[1]
    grad_resid_norm, grad_gain_attn = first_back(grad_normed1)
    grad_input = grad_middle + grad_resid_norm
    grad_table = table_gradient(after(bands, qkv_total), position_bias_table.shape[1])
    square_sum = jnp.sum(squares)

    def sum_many(values):
        flat = jnp.concatenate([value.reshape(-1) for value in values])
        flat = after(flat, reduced)
        size = flat.shape[0]
        flat = jnp.pad(flat, (0, -size % 1024)).reshape(-1, 128)
        flat = partial_sums(flat)[-1].reshape(-1)
        done, place = [], 0
        for value in values:
            done.append(flat[place : place + value.size].reshape(value.shape))
            place += value.size
        return done

    out_theirs = swap(jnp.concatenate([done_a, done_b[:1]]), PAIR, 0)
    out_mine = jnp.concatenate([done_b[1:], done_c])
    in_theirs = swap(jnp.concatenate([done_d, done_e]), PAIR, 0)
    in_mine = jnp.concatenate([done_f, done_g])

    def both_experts(mine, theirs):
        mine, theirs = [part.reshape(-1, part.shape[-1]).astype(f32) for part in (mine, theirs)]
        return jnp.stack([jnp.where(half == 0, mine, theirs), jnp.where(half == 0, theirs, mine)])

    grad_w_out = both_experts(out_mine, out_theirs)
    grad_w_in = both_experts(in_mine, in_theirs)

    grad_gain_moe, grad_router, square_total, grad_gain_attn, grad_table = sum_many(
        (grad_gain_moe, grad_router, square_sum, grad_gain_attn, grad_table)
    )
    distill_loss = square_total / (width * valid_count)
    return (
        output.astype(bf16),
        distill_loss,
        grad_input,
        grad_qkv,
        grad_out_weight,
        grad_w_in,
        grad_w_out,
        grad_router,
        grad_table,
        grad_gain_attn,
        grad_gain_moe,
    )


def solution(mesh):
    rows = P(AXES, None)
    return jax.shard_map(
        on_device,
        mesh=mesh,
        in_specs=(
            rows,
            P(None, "dp", None),
            P("dp", None),
            P(),
            P(),
            P(),
            P(),
            P("expert", None, None),
            P("expert", None, None),
            rows,
            P(AXES),
            P(AXES),
            rows,
            rows,
        ),
        out_specs=(
            rows,
            P(),
            rows,
            P(None, "dp", None),
            P("dp", None),
            P("expert", "dp", None),
            P("expert", "dp", None),
            P(),
            P(),
            P(),
            P(),
        ),
        check_vma=False,
    )
```

time: 544 us -> 498 us (0.915)
  waiting for transfers between devices: 206 us -> 131 us
  Pallas kernels: 112 us -> 156 us
  matrix products: 49.5 us -> 18.3 us
  starting transfers between devices: 48.3 us -> 68.5 us
    pallas_call x1 -> x9, Pallas kernels: 24.3 us -> 79.5 us  [the longest x1 24.7 us: expert_forward(): pl.pallas_call(lambda *refs: expert_forward_kernel(*refs, chunk=chunk, co...]
    all_gather x2 -> x0, waiting for transfers between devices: 52.9 us -> none  [the longest x1 36 us: on_device(): mine = lax.all_gather(mine, 'dp', axis=1, tiled=True)]
    ppermute x50 -> x53, waiting for transfers between devices: 153 us -> 127 us  [swap(): return lax.ppermute(value, AXES, pairs)]
    dot_general x15 -> x3, matrix products: 32.6 us -> 6.15 us  [the longest x1 2.73 us: on_device(): jnp.einsum('te,de->td', later[2], weight_vo[0], preferred_element_type=f32)]
    ppermute x0 -> x14, starting transfers between devices: none -> 16.6 us  [gather_ring(): lax.ppermute(after(held, *due[step - 2:step - 1]) if step > 1 else held,...]
    dynamic_update_slice x0 -> x16, local copies, waits for them, and re-layouts: none -> 13.8 us  [the longest x14 13.1 us: gather_ring(): lax.dynamic_update_index_in_dim(full, held, table[(place - turn * step) %...]
    unnamed x183 -> x108, local copies, waits for them, and re-layouts: 19.6 us -> 6.75 us
    pallas_call x4 -> x3, Pallas kernels: 33.4 us -> 22.8 us  [weight_part(): pl.pallas_call(lambda *refs: weight_part_kernel(*refs, count=count, layou...]
  transfers between devices with their start and end apart: 52 -> 67, of which waited for: 28 -> 26; matrix products, arithmetic and copies ran while one was open for 22% -> 21% of each run, Pallas kernels for 19% -> 18%
where the time goes in v3:
time: 498 us; the launch traced here: 490 us
  Pallas kernels  156 us (31%)
  waiting for transfers between devices  131 us (26%)
  starting transfers between devices  68.5 us (14%)
  local copies, waits for them, and re-layouts  50.7 us (10%)
  other arithmetic  45.8 us (9%)
  between operations  19.7 us (4%)
  matrix products  18.3 us (4%)
    ppermute x53, waiting for transfers between devices, swap(): return lax.ppermute(value, AXES, pairs)  127 us
    ppermute x53, starting transfers between devices, swap(): return lax.ppermute(value, AXES, pairs)  52 us
    pallas_call x1, Pallas kernels, expert_forward(): pl.pallas_call(lambda *refs: expert_forward_kernel(*refs, chunk=chunk, co...  24.7 us
    pallas_call x3, Pallas kernels, weight_part(): pl.pallas_call(lambda *refs: weight_part_kernel(*refs, count=count, layou...  22.8 us
    pallas_call x1, Pallas kernels, expert_backward(): pl.pallas_call(lambda *refs: expert_backward_kernel(*refs, chunk=chunk),...  19.5 us
    pallas_call x1, Pallas kernels, attention_backward(): pl.pallas_call(lambda *refs: attention_backward_kernel(*refs, heads=64, b...  17.2 us
    pallas_call x1, Pallas kernels, attention_forward(): pl.pallas_call(lambda *refs: attention_forward_kernel(*refs, heads=64, bl...  16.7 us
    ppermute x14, starting transfers between devices, gather_ring(): lax.ppermute(after(held, *due[step - 2:step - 1]) if step > 1 else held,...  16.6 us
  transfers between devices with their start and end apart: 67, of which 26 were waited for; matrix products, arithmetic and copies ran while one was open for 21% of the time, Pallas kernels for 18%

profile of v3, /device:TPU:0, one launch (start us, length us, event | category | flops | bytes accessed | tf_op | source)
XLA Modules:
  0.0 489.6 jit_solution(7828502797829472256)
XLA Ops:
  2.5 3.0 collective-permute-start.13
  87.8 4.4 project.3
  92.1 5.2 %project.2 = (bf16[2,512,768]{2,1,0:T(8,128)(2,1)}, bf16[2,768,768]{2,1,0:T(8,128)(2,1)}) custom-call(s32[1]{0:T(128)} %bitcast.4.refs_0_, bf16[512,768]{1,0:T(8,128)(2,1)} %fusion.12.refs_1_, bf16[2,768,384]{2,1,0:T(8,128)(2,1)} %bitcast.229, bf16[2,768,384]{2,1,0:T(8,128)(2,1)} %collective-permute-done.12.refs_3_), custom_call_target="tpu_custom_call" | custom-call | flops 1110000000 | tf_op jit(solution)/shard_map/project/pallas_call | solution.py:588
  97.3 16.7 %attention_forward.1 = (bf16[512,768]{1,0:T(8,128)(2,1)}, bf16[12,512,512]{2,1,0:T(8,128)(2,1)}) custom-call(f32[12]{0:T(128)} %slice_reduce_fusion.refs_0_, bf16[2,512,768]{2,1,0:T(8,128)(2,1)} %get-tuple-element.106.refs_1_.refs_2_.refs_0_, bf16[2,512,768]{2,1,0:T(8,128)(2,1)} %get-tuple-element.106.refs_1_.refs_2_.refs_0_, bf16[512,768]{1,0:T(8,128)(2,1)} %bitcast.236, ...), custom_call_target="tpu_custom_call" | custom-call | flops 6289999872 | tf_op jit(solution)/shard_map/attention_forward/pallas_call | solution.py:224
  117.4 3.1 pack.1
  125.0 9.0 %collective-permute-done.21.refs_2_ = bf16[320,768]{1,0:T(8,128)(2,1)S(1)} collective-permute-done((bf16[320,768]{1,0:T(8,128)(2,1)}, bf16[320,768]{1,0:T(8,128)(2,1)S(1)}, u32[]{:S(2)}, u32[]{:S(2)}) %collective-permute-start.21) | collective-permute-done | bytes 491552 | tf_op jit(solution)/shard_map/ppermute | solution.py:711
  136.4 7.3 %collective-permute-done.23.refs_4_ = bf16[320,768]{1,0:T(8,128)(2,1)S(1)} collective-permute-done((bf16[320,768]{1,0:T(8,128)(2,1)}, bf16[320,768]{1,0:T(8,128)(2,1)S(1)}, u32[]{:S(2)}, u32[]{:S(2)}) %collective-permute-start.23) | collective-permute-done | bytes 491552 | tf_op jit(solution)/shard_map/ppermute | solution.py:711
  146.6 24.7 %expert_forward.1 = (bf16[3072,1280]{1,0:T(8,128)(2,1)}, bf16[1280,3072]{1,0:T(8,128)(2,1)}, bf16[640,768]{1,0:T(8,128)(2,1)}, bf16[640,768]{1,0:T(8,128)(2,1)}, bf16[768,1280]{1,0:T(8,128)(2,1)}) custom-call(s32[1]{0:T(128)} %bitcast.3.refs_0_, bf16[320,768]{1,0:T(8,128)(2,1)} %get-tuple-element.111.refs_1_, bf16[320,768]{1,0:T(8,128)(2,1)} %copy-done.32, ...), custom_call_target="tpu_custom_call" | custom-call | flops 8140000256 | tf_op jit(solution)/shard_map/expert_forward/pallas_call | solution.py:72
  176.7 2.8 collective-permute-start.28
  182.5 9.3 %collective-permute-done.28.refs_7_ = bf16[320,768]{1,0:T(8,128)(2,1)} collective-permute-done((bf16[320,768]{1,0:T(8,128)(2,1)S(1)}, bf16[320,768]{1,0:T(8,128)(2,1)}, u32[]{:S(2)}, u32[]{:S(2)}) %collective-permute-start.28) | collective-permute-done | bytes 491552 | tf_op jit(solution)/shard_map/ppermute | solution.py:711
  191.8 10.0 %collective-permute-done.27.refs_6_ = bf16[320,768]{1,0:T(8,128)(2,1)} collective-permute-done((bf16[320,768]{1,0:T(8,128)(2,1)S(1)}, bf16[320,768]{1,0:T(8,128)(2,1)}, u32[]{:S(2)}, u32[]{:S(2)}) %collective-permute-start.27) | collective-permute-done | bytes 491552 | tf_op jit(solution)/shard_map/ppermute | solution.py:711
  201.9 11.6 %combine.1 = (bf16[512,768]{1,0:T(8,128)(2,1)}, f32[512,768]{1,0:T(8,128)}, f32[512,2]{1,0:T(8,128)}, f32[8,768]{1,0:T(8,128)}, bf16[320,768]{1,0:T(8,128)(2,1)}...) custom-call(s32[512,2]{1,0:T(8,128)} %copy-done.18, s32[2,512]{1,0:T(2,128)} %copy.197.slots.refs_1_, ...), custom_call_target="tpu_custom_call" | custom-call | flops 2960000000 | tf_op jit(solution)/shard_map/combine/pallas_call | solution.py:470
  220.6 6.3 %collective-permute-done.29.refs_6_ = bf16[320,768]{1,0:T(8,128)(2,1)S(1)} collective-permute-done((bf16[320,768]{1,0:T(8,128)(2,1)}, bf16[320,768]{1,0:T(8,128)(2,1)S(1)}, u32[]{:S(2)}, u32[]{:S(2)}) %collective-permute-start.29) | collective-permute-done | bytes 491552 | tf_op jit(solution)/shard_map/ppermute | solution.py:711
  229.3 9.2 %collective-permute-done.31.refs_8_ = bf16[320,768]{1,0:T(8,128)(2,1)S(1)} collective-permute-done((bf16[320,768]{1,0:T(8,128)(2,1)}, bf16[320,768]{1,0:T(8,128)(2,1)S(1)}, u32[]{:S(2)}, u32[]{:S(2)}) %collective-permute-start.31) | collective-permute-done | bytes 491552 | tf_op jit(solution)/shard_map/ppermute | solution.py:711
  242.5 8.3 %weight_first.1 = (bf16[1280,768]{1,0:T(8,128)(2,1)}, bf16[2,2,128,768]{3,2,1,0:T(8,128)(2,1)}, bf16[2,3,128,768]{3,2,1,0:T(8,128)(2,1)}, bf16[2,1,128,768]{3,2,1,0:T(8,128)(2,1)}) custom-call(s32[4]{0:T(128)} %pad_add_fusion.1.refs_0_, bf16[3072,1280]{1,0:T(8,128)(2,1)} %get-tuple-element.118.refs_1_.refs_2_.refs_3_.refs_4_, ...), custom_call_target="tpu_custom_call" | custom-call | flops 2590000128 | tf_op jit(solution)/shard_map/weight_first/pallas_call | solution.py:382
  251.6 19.5 %expert_backward.1 = (bf16[1280,3072]{1,0:T(8,128)(2,1)}, bf16[640,768]{1,0:T(8,128)(2,1)}, bf16[640,768]{1,0:T(8,128)(2,1)}) custom-call(s32[1]{0:T(128)} %bitcast.3.refs_0_, bf16[1280,768]{1,0:T(8,128)(2,1)} %get-tuple-element.136.refs_1_.refs_5_, bf16[2,768,3072]{2,1,0:T(8,128)(2,1)} %refs_2_.1, bf16[2,3072,768]{2,1,0:T(8,128)(2,1)} %refs_3_.1, ...), custom_call_target="tpu_custom_call" | custom-call | flops 7400000000 | tf_op jit(solution)/shard_map/expert_backward/pallas_call | solution.py:130
  282.0 7.5 %weight_part.3 = (bf16[2,2,32,3072]{3,2,1,0:T(8,128)(2,1)}, bf16[2,1,32,3072]{3,2,1,0:T(8,128)(2,1)}, bf16[2,1,32,3072]{3,2,1,0:T(8,128)(2,1)}, bf16[2,2,32,3072]{3,2,1,0:T(8,128)(2,1)}) custom-call(s32[4]{0:T(128)} %pad_add_fusion.2.refs_0_, bf16[768,1280]{1,0:T(8,128)(2,1)} %get-tuple-element.132.refs_1_.refs_2_.refs_3_.refs_4_, ...), custom_call_target="tpu_custom_call" | custom-call | flops 2590000128 | tf_op jit(solution)/shard_map/weight_part/pallas_call | solution.py:358
  289.5 7.5 %weight_part.5 = (bf16[2,2,32,3072]{3,2,1,0:T(8,128)(2,1)}, bf16[2,1,32,3072]{3,2,1,0:T(8,128)(2,1)}, bf16[2,1,32,3072]{3,2,1,0:T(8,128)(2,1)}, bf16[2,2,32,3072]{3,2,1,0:T(8,128)(2,1)}) custom-call(s32[4]{0:T(128)} %pad_add_fusion.1.refs_0_, bf16[768,1280]{1,0:T(8,128)(2,1)} %get-tuple-element.132.refs_1_.refs_2_.refs_3_.refs_4_, ...), custom_call_target="tpu_custom_call" | custom-call | flops 2590000128 | tf_op jit(solution)/shard_map/weight_part/pallas_call | solution.py:358
  297.0 7.8 %weight_part.4 = (bf16[2,2,128,768]{3,2,1,0:T(8,128)(2,1)}, bf16[2,3,128,768]{3,2,1,0:T(8,128)(2,1)}, bf16[2,1,128,768]{3,2,1,0:T(8,128)(2,1)}) custom-call(s32[4]{0:T(128)} %pad_add_fusion.2.refs_0_, bf16[3072,1280]{1,0:T(8,128)(2,1)} %get-tuple-element.118.refs_1_.refs_2_.refs_3_.refs_4_, ...), custom_call_target="tpu_custom_call" | custom-call | flops 2590000128 | tf_op jit(solution)/shard_map/weight_part/pallas_call | solution.py:358
  313.9 10.3 %collect.1 = (f32[512,768]{1,0:T(8,128)}, bf16[512,768]{1,0:T(8,128)(2,1)}, bf16[512,768]{1,0:T(8,128)(2,1)}, f32[8,768]{1,0:T(8,128)}) custom-call(s32[512,2]{1,0:T(8,128)} %copy-done.18, bf16[640,768]{1,0:T(8,128)(2,1)} %get-tuple-element.127.refs_1_, bf16[640,768]{1,0:T(8,128)(2,1)} %collective-permute-done.34.refs_2_, ...), custom_call_target="tpu_custom_call" | custom-call | flops 2590000128 | tf_op jit(solution)/shard_map/collect/pallas_call | solution.py:514
  324.2 3.9 outer_halves.2
  328.1 17.2 %attention_backward.1 = (bf16[3,512,768]{2,1,0:T(8,128)(2,1)}, f32[12,4,128,128]{3,2,1,0:T(8,128)}) custom-call(bf16[2,512,768]{2,1,0:T(8,128)(2,1)} %get-tuple-element.106.refs_1_.refs_2_.refs_0_, bf16[2,512,768]{2,1,0:T(8,128)(2,1)} %get-tuple-element.106.refs_1_.refs_2_.refs_0_, bf16[512,768]{1,0:T(8,128)(2,1)} %bitcast.237, ...), custom_call_target="tpu_custom_call" | custom-call | flops 6289999872 | tf_op jit(solution)/shard_map/attention_backward/pallas_call | solution.py:302
  353.5 7.9 %outer_halves.3 = (bf16[3,768,384]{2,1,0:T(8,128)(2,1)}, bf16[3,768,384]{2,1,0:T(8,128)(2,1)}) custom-call(s32[1]{0:T(128)} %bitcast.4.refs_0_, bf16[512,768]{1,0:T(8,128)(2,1)} %fusion.12.refs_1_, bf16[3,512,768]{2,1,0:T(8,128)(2,1)} %get-tuple-element.163.refs_2_), custom_call_target="tpu_custom_call" | custom-call | flops 2220000000 | tf_op jit(solution)/shard_map/outer_halves/pallas_call | solution.py:550
  370.5 8.4 %collective-permute-done.42 = bf16[2,1,32,3072]{3,2,1,0:T(8,128)(2,1)S(1)} collective-permute-done((bf16[2,1,32,3072]{3,2,1,0:T(8,128)(2,1)S(1)}, bf16[2,1,32,3072]{3,2,1,0:T(8,128)(2,1)S(1)}, u32[]{:S(2)}, u32[]{:S(2)}) %collective-permute-start.42) | collective-permute-done | bytes 393248 | tf_op jit(solution)/shard_map/ppermute | solution.py:711
  382.3 12.3 %collective-permute-done.45 = bf16[1,1,128,768]{3,2,1,0:T(8,128)(2,1)S(1)} collective-permute-done((bf16[1,1,128,768]{3,2,1,0:T(8,128)(2,1)S(1)}, bf16[1,1,128,768]{3,2,1,0:T(8,128)(2,1)S(1)}, u32[]{:S(2)}, u32[]{:S(2)}) %collective-permute-start.45) | collective-permute-done | bytes 196640 | tf_op jit(solution)/shard_map/ppermute | solution.py:711
  399.7 5.3 %fusion.26 = f32[12,32]{1,0:T(8,128)S(1)} fusion(s32[4,128,128]{2,1,0:T(8,128)S(1)} %copy-done.15, f32[12,4,128,128]{3,2,1,0:T(8,128)S(1)} %copy-done.2), kind=kOutput, calls=%fused_computation.57 | convolution fusion | flops 304087040 | bytes 3409408 | tf_op jit(solution)/shard_map/hdxy,dxyb->hb/dot_general | solution.py:667
  405.1 2.7 fusion.16
  407.8 2.9 collective-permute-start.57
  415.1 3.3 pad_maximum_fusion.1
  437.5 22.2 %collective-permute-done.49 = f32[64,128]{1,0:T(8,128)S(1)} collective-permute-done((f32[64,128]{1,0:T(8,128)S(1)}, f32[64,128]{1,0:T(8,128)S(1)}, u32[]{:S(2)}, u32[]{:S(2)}) %collective-permute-start.49) | collective-permute-done | bytes 32800 | tf_op jit(solution)/shard_map/ppermute | solution.py:711
  472.5 6.7 %collective-permute-done.58 = bf16[4,48,384]{2,1,0:T(8,128)(2,1)S(1)} collective-permute-done((bf16[4,48,384]{2,1,0:T(8,128)(2,1)S(1)}, bf16[4,48,384]{2,1,0:T(8,128)(2,1)S(1)}, u32[]{:S(2)}, u32[]{:S(2)}) %collective-permute-start.58) | collective-permute-done | bytes 147488 | tf_op jit(solution)/shard_map/ppermute | solution.py:711
  480.1 4.3 collective-permute-done.61
  (417 shorter events, 189.1 us)
Async XLA Ops:
  2.5 46.6 %collective-permute-start.13 = (bf16[2,96,384]{2,1,0:T(8,128)(2,1)}, bf16[2,96,384]{2,1,0:T(8,128)(2,1)}, u32[]{:S(2)}, u32[]{:S(2)}) collective-permute-start(bf16[2,96,384]{2,1,0:T(8,128)(2,1)} %get-tuple-element.252), channel_id=1, source_target_pairs={{0,8},{8,16},{16,24},{24,28},{28,20},{20,12},{12,4},{4,0},{1,9},{9... | collective-permute-start | bytes 442376 | tf_op jit(solution)/shard_map/ppermute | solution.py:757
  5.5 45.2 %collective-permute-start.17 = (bf16[2,96,384]{2,1,0:T(8,128)(2,1)}, bf16[2,96,384]{2,1,0:T(8,128)(2,1)}, u32[]{:S(2)}, u32[]{:S(2)}) collective-permute-start(bf16[2,96,384]{2,1,0:T(8,128)(2,1)} %get-tuple-element.252), channel_id=1, source_target_pairs={{0,4},{8,0},{16,8},{24,16},{28,24},{20,28},{12,20},{4,12},{1,5},{9... | collective-permute-start | bytes 442376 | tf_op jit(solution)/shard_map/ppermute | solution.py:757
  5.5 41.5 %collective-permute-start.5 = (bf16[2,96,384]{2,1,0:T(8,128)(2,1)}, bf16[2,96,384]{2,1,0:T(8,128)(2,1)}, u32[]{:S(2)}, u32[]{:S(2)}) collective-permute-start(bf16[2,96,384]{2,1,0:T(8,128)(2,1)} %get-tuple-element.253), channel_id=1, source_target_pairs={{0,8},{8,16},{16,24},{24,28},{28,20},{20,12},{12,4},{4,0},{1,9},{9... | collective-permute-start | bytes 442376 | tf_op jit(solution)/shard_map/ppermute | solution.py:757
  7.6 41.1 %collective-permute-start.9 = (bf16[2,96,384]{2,1,0:T(8,128)(2,1)}, bf16[2,96,384]{2,1,0:T(8,128)(2,1)}, u32[]{:S(2)}, u32[]{:S(2)}) collective-permute-start(bf16[2,96,384]{2,1,0:T(8,128)(2,1)} %get-tuple-element.253), channel_id=1, source_target_pairs={{0,4},{8,0},{16,8},{24,16},{28,24},{20,28},{12,20},{4,12},{1,5},{9... | collective-permute-start | bytes 442376 | tf_op jit(solution)/shard_map/ppermute | solution.py:757
  30.4 16.7 %collective-permute-start.2 = (f32[8,128]{1,0:T(8,128)S(1)}, f32[8,128]{1,0:T(8,128)S(1)}, u32[]{:S(2)}, u32[]{:S(2)}) collective-permute-start(f32[8,128]{1,0:T(8,128)S(1)} %fusion.170), channel_id=1, source_target_pairs={{0,4},{1,5},{2,6},{3,7},{4,0},{5,1},{6,2},{7,3},{8,12},{9,13},{10,... | collective-permute-start | bytes 12296 | tf_op jit(solution)/shard_map/ppermute | solution.py:711
  55.9 19.6 %collective-permute-start.11 = (bf16[2,96,384]{2,1,0:T(8,128)(2,1)S(1)}, bf16[2,96,384]{2,1,0:T(8,128)(2,1)S(1)}, u32[]{:S(2)}, u32[]{:S(2)}) collective-permute-start(bf16[2,96,384]{2,1,0:T(8,128)(2,1)S(1)} %collective-permute-done.10), channel_id=1, source_target_pairs={{0,4},{8,0},{16,8},{24,16},{28,24},{20,28},{12,20},{4,12},{1,5},{9... | collective-permute-start | bytes 442376 | tf_op jit(solution)/shard_map/ppermute | solution.py:757
  123.6 20.1 %collective-permute-start.23 = (bf16[320,768]{1,0:T(8,128)(2,1)}, bf16[320,768]{1,0:T(8,128)(2,1)S(1)}, u32[]{:S(2)}, u32[]{:S(2)}) collective-permute-start(bf16[320,768]{1,0:T(8,128)(2,1)} %get-tuple-element.114), channel_id=1, source_target_pairs={{0,10},{1,11},{2,8},{3,9},{4,14},{5,15},{6,12},{7,13},{8,2},{9,3},... | collective-permute-start | bytes 1474568 | tf_op jit(solution)/shard_map/ppermute | solution.py:711
  179.5 22.4 %collective-permute-start.27 = (bf16[320,768]{1,0:T(8,128)(2,1)S(1)}, bf16[320,768]{1,0:T(8,128)(2,1)}, u32[]{:S(2)}, u32[]{:S(2)}) collective-permute-start(bf16[320,768]{1,0:T(8,128)(2,1)S(1)} %pad_maximum_fusion.10), channel_id=1, source_target_pairs={{0,8},{1,9},{2,10},{3,11},{4,12},{5,13},{6,14},{7,15},{8,0},{9,1},... | collective-permute-start | bytes 1474568 | tf_op jit(solution)/shard_map/ppermute | solution.py:711
  180.6 21.2 %collective-permute-start.26 = (bf16[320,768]{1,0:T(8,128)(2,1)}, bf16[320,768]{1,0:T(8,128)(2,1)}, u32[]{:S(2)}, u32[]{:S(2)}) collective-permute-start(bf16[320,768]{1,0:T(8,128)(2,1)} %pad_maximum_fusion.9), channel_id=1, source_target_pairs={{0,2},{1,3},{2,0},{3,1},{4,6},{5,7},{6,4},{7,5},{8,10},{9,11},{10,... | collective-permute-start | bytes 1474568 | tf_op jit(solution)/shard_map/ppermute | solution.py:711
  216.6 21.9 %collective-permute-start.31 = (bf16[320,768]{1,0:T(8,128)(2,1)}, bf16[320,768]{1,0:T(8,128)(2,1)S(1)}, u32[]{:S(2)}, u32[]{:S(2)}) collective-permute-start(bf16[320,768]{1,0:T(8,128)(2,1)} %get-tuple-element.122), channel_id=1, source_target_pairs={{0,10},{1,11},{2,8},{3,9},{4,14},{5,15},{6,12},{7,13},{8,2},{9,3},... | collective-permute-start | bytes 1474568 | tf_op jit(solution)/shard_map/ppermute | solution.py:711
  250.8 20.3 %collective-permute-start.33 = (bf16[2,2,128,768]{3,2,1,0:T(8,128)(2,1)}, bf16[2,2,128,768]{3,2,1,0:T(8,128)(2,1)S(1)}, u32[]{:S(2)}, u32[]{:S(2)}) collective-permute-start(bf16[2,2,128,768]{3,2,1,0:T(8,128)(2,1)} %get-tuple-element.124), channel_id=1, source_target_pairs={{0,4},{1,5},{2,6},{3,7},{4,0},{5,1},{6,2},{7,3},{8,12},{9,13},{10,... | collective-permute-start | bytes 2359304 | tf_op jit(solution)/shard_map/ppermute | solution.py:711
  275.5 33.7 %collective-permute-start.36 = (bf16[2,3,128,768]{3,2,1,0:T(8,128)(2,1)}, bf16[2,3,128,768]{3,2,1,0:T(8,128)(2,1)S(1)}, u32[]{:S(2)}, u32[]{:S(2)}) collective-permute-start(bf16[2,3,128,768]{3,2,1,0:T(8,128)(2,1)} %get-tuple-element.131), channel_id=1, source_target_pairs={{0,4},{1,5},{2,6},{3,7},{4,0},{5,1},{6,2},{7,3},{8,12},{9,13},{10,... | collective-permute-start | bytes 3538952 | tf_op jit(solution)/shard_map/ppermute | solution.py:711
  278.2 32.8 %collective-permute-start.38 = (bf16[320,768]{1,0:T(8,128)(2,1)S(1)}, bf16[320,768]{1,0:T(8,128)(2,1)S(1)}, u32[]{:S(2)}, u32[]{:S(2)}) collective-permute-start(bf16[320,768]{1,0:T(8,128)(2,1)S(1)} %pad_maximum_fusion.14), channel_id=1, source_target_pairs={{0,10},{1,11},{2,8},{3,9},{4,14},{5,15},{6,12},{7,13},{8,2},{9,3},... | collective-permute-start | bytes 1474568 | tf_op jit(solution)/shard_map/ppermute | solution.py:711
  281.0 30.1 %collective-permute-start.37 = (bf16[320,768]{1,0:T(8,128)(2,1)S(1)}, bf16[320,768]{1,0:T(8,128)(2,1)S(1)}, u32[]{:S(2)}, u32[]{:S(2)}) collective-permute-start(bf16[320,768]{1,0:T(8,128)(2,1)S(1)} %pad_maximum_fusion.13), channel_id=1, source_target_pairs={{0,8},{1,9},{2,10},{3,11},{4,12},{5,13},{6,14},{7,15},{8,0},{9,1},... | collective-permute-start | bytes 1474568 | tf_op jit(solution)/shard_map/ppermute | solution.py:711
  281.4 29.7 %collective-permute-start.35 = (bf16[320,768]{1,0:T(8,128)(2,1)S(1)}, bf16[320,768]{1,0:T(8,128)(2,1)}, u32[]{:S(2)}, u32[]{:S(2)}) collective-permute-start(bf16[320,768]{1,0:T(8,128)(2,1)S(1)} %pad_maximum_fusion.12), channel_id=1, source_target_pairs={{0,2},{1,3},{2,0},{3,1},{4,6},{5,7},{6,4},{7,5},{8,10},{9,11},{10,... | collective-permute-start | bytes 1474568 | tf_op jit(solution)/shard_map/ppermute | solution.py:711
  307.0 54.5 %collective-permute-start.65 = (bf16[1,2,128,768]{3,2,1,0:T(8,128)(2,1)}, bf16[1,2,128,768]{3,2,1,0:T(8,128)(2,1)}, u32[]{:S(2)}, u32[]{:S(2)}) collective-permute-start(bf16[1,2,128,768]{3,2,1,0:T(8,128)(2,1)} %constant_dynamic-slice_fusion.8), channel_id=1, source_target_pairs={{0,16},{1,17},{2,18},{3,19},{4,20},{5,21},{6,22},{7,23},{8,24},{9,... | collective-permute-start | bytes 1179656 | tf_op jit(solution)/shard_map/ppermute | solution.py:711
  310.4 41.9 %collective-permute-start.64 = (bf16[1,3,128,768]{3,2,1,0:T(8,128)(2,1)}, bf16[1,3,128,768]{3,2,1,0:T(8,128)(2,1)}, u32[]{:S(2)}, u32[]{:S(2)}) collective-permute-start(bf16[1,3,128,768]{3,2,1,0:T(8,128)(2,1)} %constant_dynamic-slice_fusion.6), channel_id=1, source_target_pairs={{0,16},{1,17},{2,18},{3,19},{4,20},{5,21},{6,22},{7,23},{8,24},{9,... | collective-permute-start | bytes 1769480 | tf_op jit(solution)/shard_map/ppermute | solution.py:711
  311.9 37.7 %collective-permute-start.40 = (bf16[2,2,32,3072]{3,2,1,0:T(8,128)(2,1)}, bf16[2,2,32,3072]{3,2,1,0:T(8,128)(2,1)S(1)}, u32[]{:S(2)}, u32[]{:S(2)}) collective-permute-start(bf16[2,2,32,3072]{3,2,1,0:T(8,128)(2,1)} %get-tuple-element.154), channel_id=1, source_target_pairs={{0,4},{1,5},{2,6},{3,7},{4,0},{5,1},{6,2},{7,3},{8,12},{9,13},{10,... | collective-permute-start | bytes 2359304 | tf_op jit(solution)/shard_map/ppermute | solution.py:711
  312.5 37.1 %collective-permute-start.39 = (bf16[2,1,128,768]{3,2,1,0:T(8,128)(2,1)}, bf16[2,1,128,768]{3,2,1,0:T(8,128)(2,1)}, u32[]{:S(2)}, u32[]{:S(2)}) collective-permute-start(bf16[2,1,128,768]{3,2,1,0:T(8,128)(2,1)} %get-tuple-element.153), channel_id=1, source_target_pairs={{0,4},{1,5},{2,6},{3,7},{4,0},{5,1},{6,2},{7,3},{8,12},{9,13},{10,... | collective-permute-start | bytes 1179656 | tf_op jit(solution)/shard_map/ppermute | solution.py:711
  328.1 18.5 %collective-permute-start.51 = (bf16[1,768,384]{2,1,0:T(8,128)(2,1)}, bf16[1,768,384]{2,1,0:T(8,128)(2,1)}, u32[]{:S(2)}, u32[]{:S(2)}) collective-permute-start(bf16[1,768,384]{2,1,0:T(8,128)(2,1)} %get-tuple-element.147), channel_id=1, source_target_pairs={{0,1},{1,0},{2,3},{3,2},{4,5},{5,4},{6,7},{7,6},{8,9},{9,8},{10,11... | collective-permute-start | bytes 1769480 | tf_op jit(solution)/shard_map/ppermute | solution.py:711
  348.1 21.3 %collective-permute-start.52 = (bf16[1,8,48,384]{3,2,1,0:T(8,128)(2,1)S(1)}, bf16[1,8,48,384]{3,2,1,0:T(8,128)(2,1)S(1)}, u32[]{:S(2)}, u32[]{:S(2)}) collective-permute-start(bf16[1,8,48,384]{3,2,1,0:T(8,128)(2,1)S(1)} %dynamic-slice_bitcast_fusion.3), channel_id=1, source_target_pairs={{0,2},{1,3},{2,0},{3,1},{4,6},{5,7},{6,4},{7,5},{8,10},{9,11},{10,... | collective-permute-start | bytes 884744 | tf_op jit(solution)/shard_map/ppermute | solution.py:711
  362.8 45.1 %collective-permute-start.66 = (bf16[3,128,768]{2,1,0:T(8,128)(2,1)S(1)}, bf16[3,128,768]{2,1,0:T(8,128)(2,1)S(1)}, u32[]{:S(2)}, u32[]{:S(2)}) collective-permute-start(bf16[3,128,768]{2,1,0:T(8,128)(2,1)S(1)} %pad_maximum_fusion.8), channel_id=1, source_target_pairs={{0,8},{1,9},{2,10},{3,11},{4,12},{5,13},{6,14},{7,15},{8,0},{9,1},... | collective-permute-start | bytes 1769480 | tf_op jit(solution)/shard_map/ppermute | solution.py:711
  365.0 57.6 %collective-permute-start.54 = (bf16[1,2,32,3072]{3,2,1,0:T(8,128)(2,1)}, bf16[1,2,32,3072]{3,2,1,0:T(8,128)(2,1)}, u32[]{:S(2)}, u32[]{:S(2)}) collective-permute-start(bf16[1,2,32,3072]{3,2,1,0:T(8,128)(2,1)} %constant_dynamic-slice_fusion.5), channel_id=1, source_target_pairs={{0,16},{1,17},{2,18},{3,19},{4,20},{5,21},{6,22},{7,23},{8,24},{9,... | collective-permute-start | bytes 1179656 | tf_op jit(solution)/shard_map/ppermute | solution.py:711
  369.4 25.1 %collective-permute-start.45 = (bf16[1,1,128,768]{3,2,1,0:T(8,128)(2,1)S(1)}, bf16[1,1,128,768]{3,2,1,0:T(8,128)(2,1)S(1)}, u32[]{:S(2)}, u32[]{:S(2)}) collective-permute-start(bf16[1,1,128,768]{3,2,1,0:T(8,128)(2,1)S(1)} %constant_dynamic-slice_fusion.2), channel_id=1, source_target_pairs={{0,16},{1,17},{2,18},{3,19},{4,20},{5,21},{6,22},{7,23},{8,24},{9,... | collective-permute-start | bytes 589832 | tf_op jit(solution)/shard_map/ppermute | solution.py:711
  380.4 47.5 %collective-permute-start.59 = (bf16[2,2,32,3072]{3,2,1,0:T(8,128)(2,1)}, bf16[2,2,32,3072]{3,2,1,0:T(8,128)(2,1)}, u32[]{:S(2)}, u32[]{:S(2)}) collective-permute-start(bf16[2,2,32,3072]{3,2,1,0:T(8,128)(2,1)} %get-tuple-element.184), channel_id=1, source_target_pairs={{0,4},{1,5},{2,6},{3,7},{4,0},{5,1},{6,2},{7,3},{8,12},{9,13},{10,... | collective-permute-start | bytes 2359304 | tf_op jit(solution)/shard_map/ppermute | solution.py:711
  394.5 27.0 %collective-permute-start.56 = (bf16[1,1,32,3072]{3,2,1,0:T(8,128)(2,1)}, bf16[1,1,32,3072]{3,2,1,0:T(8,128)(2,1)}, u32[]{:S(2)}, u32[]{:S(2)}) collective-permute-start(bf16[1,1,32,3072]{3,2,1,0:T(8,128)(2,1)} %get-tuple-element.248), channel_id=1, source_target_pairs={{0,16},{1,17},{2,18},{3,19},{4,20},{5,21},{6,22},{7,23},{8,24},{9,... | collective-permute-start | bytes 589832 | tf_op jit(solution)/shard_map/ppermute | solution.py:711
  396.4 23.7 %collective-permute-start.43 = (bf16[3,8,48,384]{3,2,1,0:T(8,128)(2,1)}, bf16[3,8,48,384]{3,2,1,0:T(8,128)(2,1)}, u32[]{:S(2)}, u32[]{:S(2)}) collective-permute-start(bf16[3,8,48,384]{3,2,1,0:T(8,128)(2,1)} %dynamic-slice_bitcast_fusion), channel_id=1, source_target_pairs={{0,2},{1,3},{2,0},{3,1},{4,6},{5,7},{6,4},{7,5},{8,10},{9,11},{10,... | collective-permute-start | bytes 2654216 | tf_op jit(solution)/shard_map/ppermute | solution.py:711
  407.8 29.7 %collective-permute-start.57 = (bf16[1,1,32,3072]{3,2,1,0:T(8,128)(2,1)}, bf16[1,1,32,3072]{3,2,1,0:T(8,128)(2,1)}, u32[]{:S(2)}, u32[]{:S(2)}) collective-permute-start(bf16[1,1,32,3072]{3,2,1,0:T(8,128)(2,1)} %get-tuple-element.246), channel_id=1, source_target_pairs={{0,16},{1,17},{2,18},{3,19},{4,20},{5,21},{6,22},{7,23},{8,24},{9,... | collective-permute-start | bytes 589832 | tf_op jit(solution)/shard_map/ppermute | solution.py:711
  423.8 56.1 %collective-permute-start.63 = (bf16[3,32,3072]{2,1,0:T(8,128)(2,1)S(1)}, bf16[3,32,3072]{2,1,0:T(8,128)(2,1)S(1)}, u32[]{:S(2)}, u32[]{:S(2)}) collective-permute-start(bf16[3,32,3072]{2,1,0:T(8,128)(2,1)S(1)} %pad_maximum_fusion.6), channel_id=1, source_target_pairs={{0,8},{1,9},{2,10},{3,11},{4,12},{5,13},{6,14},{7,15},{8,0},{9,1},... | collective-permute-start | bytes 1769480 | tf_op jit(solution)/shard_map/ppermute | solution.py:711
  427.9 33.0 %collective-permute-start.53 = (bf16[4,2,2,48,384]{4,3,2,1,0:T(8,128)(2,1)S(1)}, bf16[4,2,2,48,384]{4,3,2,1,0:T(8,128)(2,1)S(1)}, u32[]{:S(2)}, u32[]{:S(2)}) collective-permute-start(bf16[4,2,2,48,384]{4,3,2,1,0:T(8,128)(2,1)S(1)} %dynamic-slice_bitcast_fusion.1), channel_id=1, source_target_pairs={{0,8},{1,9},{2,10},{3,11},{4,12},{5,13},{6,14},{7,15},{8,0},{9,1},... | collective-permute-start | bytes 1769480 | tf_op jit(solution)/shard_map/ppermute | solution.py:711
  434.2 25.5 %collective-permute-start.49 = (f32[64,128]{1,0:T(8,128)S(1)}, f32[64,128]{1,0:T(8,128)S(1)}, u32[]{:S(2)}, u32[]{:S(2)}) collective-permute-start(f32[64,128]{1,0:T(8,128)S(1)} %add.1041), channel_id=1, source_target_pairs={{0,8},{1,9},{2,10},{3,11},{4,12},{5,13},{6,14},{7,15},{8,0},{9,1},... | collective-permute-start | bytes 98312 | tf_op jit(solution)/shard_map/ppermute | solution.py:711
  435.8 36.6 %collective-permute-start.60 = (bf16[1,2,32,3072]{3,2,1,0:T(8,128)(2,1)}, bf16[1,2,32,3072]{3,2,1,0:T(8,128)(2,1)S(1)}, u32[]{:S(2)}, u32[]{:S(2)}) collective-permute-start(bf16[1,2,32,3072]{3,2,1,0:T(8,128)(2,1)} %constant_dynamic-slice_fusion.7), channel_id=1, source_target_pairs={{0,16},{1,17},{2,18},{3,19},{4,20},{5,21},{6,22},{7,23},{8,24},{9,... | collective-permute-start | bytes 1179656 | tf_op jit(solution)/shard_map/ppermute | solution.py:711
  (87 other events, 658.0 us)
